TPU v7x, 256 devices: a whole 4x4x8 slice. The times are simulated.
256 devices in a mesh: ctx: 8 (over x, core), head: 4 (over y), dp: 8 (over z).
Axes of the slice: x: 4, y: 4, z: 8, core: 2. Of those that a mesh axis runs over, the one named last changes fastest.
Arguments:
- student_q: bfloat16 [8, 2048, 3584], P('dp', 'ctx', 'head'), may hold values from -6 to 6
- student_k: bfloat16 [8, 2048, 3584], P('dp', 'ctx', 'head'), may hold values from -6 to 6
- student_v: bfloat16 [8, 2048, 3584], P('dp', 'ctx', 'head'), may hold values from -6 to 6
- beta: float32 [8, 28, 2048], P('dp', 'head', 'ctx'), may hold values from 0 to 0.95
- log_decay: float32 [8, 28, 2048], P('dp', 'head', 'ctx'), may hold values from -1 to 0
- kernel: float32 [8, 28, 4, 2048], P('dp', 'head', None, 'ctx'), may hold values from -3 to 3
- out_gain: float32 [3584], P('head'), may hold values from 0.1 to 1.9
- teacher_q: bfloat16 [8, 2048, 3584], P('dp', 'ctx', 'head'), may hold values from -8 to 8
- teacher_k: bfloat16 [8, 2048, 512], P('dp', 'ctx', 'head'), may hold values from -8 to 8
- teacher_v: bfloat16 [8, 2048, 512], P('dp', 'ctx', 'head'), may hold values from -6 to 6
- segment_ids: int32 [8, 2048], P('dp', 'ctx'), may hold values from 0 to 7, never falling along the last dimension, each value on 1 to 1024 neighbouring positions
- loss_weight: float32 [8, 28, 2048], P('dp', 'head', 'ctx'), may hold values from 0.05 to 40.5
Outputs:
- student_out: bfloat16 [8, 2048, 3584], P('dp', 'ctx', 'head')
- teacher_out: bfloat16 [8, 2048, 3584], P('dp', 'ctx', 'head')
- loss: float32 [], replicated
All inputs are finite; a program needn't handle non-finite values.
Results may differ from a plain program's by a relative error of at most 0.0085.
Values may be sent and summed in bfloat16 or wider, within the bound.
No kernel may reach another device: no remote copies, remote signals or barrier semaphores. Data moves between devices by JAX's collectives and lax.ppermute only.
A program may use at most 128 MiB of HBM per device.

v0:
```python
import math

import jax
import jax.numpy as jnp
from jax import lax
from jax.sharding import PartitionSpec as P

SPAN = 64


PRECISE = lax.Precision.HIGHEST
EPSILON = 1e-06
MASKED = -1e30


def from_behind(block, axis, distance):
    devices = range(lax.axis_size(axis))
    route = [(i - distance, i) for i in devices if i - distance in devices]
    return lax.ppermute(block, axis, route)


def matmul(left, right):
    return jnp.dot(left, right, precision=PRECISE)


def batched(left, right):
    return jnp.einsum("shij,shjv->shiv", left, right, precision=PRECISE)


def unit_rows(matrix):
    return matrix * lax.rsqrt(jnp.sum(matrix * matrix, axis=-1, keepdims=True) + EPSILON)


def span_terms(query_rows, key_rows, value_rows, beta_rows, decay_rows, segment_rows, previous):
    length = query_rows.shape[0]
    head_dim = key_rows.shape[1]
    row_index = lax.broadcasted_iota(jnp.int32, (length, length), 0)
    col_index = lax.broadcasted_iota(jnp.int32, (length, length), 1)
    running = jnp.cumsum(decay_rows)
    same_doc = segment_rows[:, None] == segment_rows[None, :]
    reachable = (col_index <= row_index) & same_doc
    between = jnp.exp(jnp.minimum(running[:, None] - running[None, :], 0.0))
    between = jnp.where(reachable, between, 0.0)
    from_start = jnp.where(segment_rows == previous, jnp.exp(running), 0.0)
    weighted = between * beta_rows[None, :]
    coupling = jnp.where(col_index < row_index, weighted * matmul(key_rows, key_rows.T), 0.0)
    reading = weighted * matmul(query_rows, key_rows.T)
    identity_small = jnp.eye(length, dtype=jnp.float32)
    power_term = -coupling
    inverse = identity_small + power_term
    for doubling in range(1, (length - 1).bit_length()):
        power_term = matmul(power_term, power_term)
        inverse = matmul(inverse, identity_small + power_term)
    fresh_values = matmul(inverse, value_rows)
    carried = matmul(inverse, from_start[:, None] * key_rows)
    end_keys = weighted[length - 1][:, None] * key_rows
    transition = from_start[length - 1] * jnp.eye(head_dim, dtype=jnp.float32) - matmul(
        end_keys.T, carried
    )
    injection = matmul(end_keys.T, fresh_values)
    local_part = matmul(reading, fresh_values)
    state_reader = from_start[:, None] * query_rows - matmul(reading, carried)
    return (transition, injection, local_part, state_reader)


def on_device(
    student_q,
    student_k,
    student_v,
    beta,
    log_decay,
    kernel,
    out_gain,
    teacher_q,
    teacher_k,
    teacher_v,
    segment_ids,
    loss_weight,
):
    sequences, tokens, features = student_q.shape
    local_heads = beta.shape[1]
    head_dim = features // local_heads
    taps_count = kernel.shape[2]
    span_count = tokens // SPAN
    margin = taps_count - 1
    id_values = segment_ids.astype(jnp.bfloat16)
    rim_values, rim_ids = from_behind(
        (student_v[:, tokens - margin :], id_values[:, tokens - margin :]), "ctx", 1
    )
    padded = jnp.concatenate([rim_values, student_v], axis=1).astype(jnp.float32)
    padded = padded.reshape(sequences, tokens + margin, local_heads, head_dim)
    padded_ids = jnp.concatenate([rim_ids, id_values], axis=1).astype(jnp.float32)
    own_ids = segment_ids.astype(jnp.float32)
    convolved = jnp.zeros((sequences, tokens, local_heads, head_dim), jnp.float32)
    for offset in range(taps_count):
        start_row = margin - offset
        shifted = padded[:, start_row : start_row + tokens]
        keep_mask = (padded_ids[:, start_row : start_row + tokens] == own_ids).astype(jnp.float32)
        taps_now = jnp.transpose(kernel[:, :, offset, :], (0, 2, 1))
        convolved = convolved + taps_now[:, :, :, None] * keep_mask[:, :, None, None] * shifted
    values = jax.nn.silu(convolved)
    queries = unit_rows(
        student_q.astype(jnp.float32).reshape(sequences, tokens, local_heads, head_dim)
    )
    keys_unit = unit_rows(
        student_k.astype(jnp.float32).reshape(sequences, tokens, local_heads, head_dim)
    )

    def by_span(matrix):
        return jnp.transpose(
            matrix.reshape(sequences, span_count, SPAN, local_heads, head_dim), (0, 3, 1, 2, 4)
        )

    beta_rows = beta.reshape(sequences, local_heads, span_count, SPAN)
    decay_rows = log_decay.reshape(sequences, local_heads, span_count, SPAN)
    segment_rows = own_ids.reshape(sequences, span_count, SPAN)
    previous = padded_ids[:, margin - 1 : margin - 1 + tokens : SPAN]
    over_spans = jax.vmap(span_terms)
    over_heads = jax.vmap(over_spans, in_axes=(0, 0, 0, 0, 0, None, None))
    over_all = jax.vmap(over_heads)
    transition, injection, local_part, state_reader = over_all(
        by_span(queries),
        by_span(keys_unit),
        by_span(values),
        beta_rows,
        decay_rows,
        segment_rows,
        previous,
    )
    identity = jnp.broadcast_to(
        jnp.eye(head_dim, dtype=jnp.float32), (sequences, local_heads, head_dim, head_dim)
    )
    empty_state = jnp.zeros((sequences, local_heads, head_dim, head_dim), jnp.float32)
    moved_transition = jnp.moveaxis(transition, 2, 0)
    moved_injection = jnp.moveaxis(injection, 2, 0)

    def compose(carry, bundle):
        whole_map, whole_input = carry
        step_map, step_input = bundle
        return ((batched(step_map, whole_map), batched(step_map, whole_input) + step_input), None)

    (device_map, device_input), _ = lax.scan(
        compose, (identity, empty_state), (moved_transition, moved_injection)
    )

    def advance(counter, arriving):
        leaving = batched(device_map, arriving) + device_input
        return from_behind(leaving.astype(jnp.bfloat16), "ctx", 1).astype(leaving.dtype)

    incoming = lax.fori_loop(0, lax.axis_size("ctx") - 1, advance, empty_state)

    def emit(state_now, bundle):
        step_map, step_input, part_local, part_reader = bundle
        produced = part_local + jnp.einsum(
            "shck,shkv->shcv", part_reader, state_now, precision=PRECISE
        )
        return (batched(step_map, state_now) + step_input, produced)

    _, produced = lax.scan(
        emit,
        incoming,
        (
            moved_transition,
            moved_injection,
            jnp.moveaxis(local_part, 2, 0),
            jnp.moveaxis(state_reader, 2, 0),
        ),
    )
    student = jnp.moveaxis(produced, 0, 2).reshape(sequences, local_heads, tokens, head_dim)
    gains = out_gain.reshape(local_heads, head_dim)[None, :, None, :]
    student = (
        student * lax.rsqrt(jnp.mean(student * student, axis=-1, keepdims=True) + EPSILON) * gains
    )
    kv_heads = teacher_k.shape[2] // head_dim
    per_group = local_heads // kv_heads
    grouped_q = teacher_q.reshape(sequences, tokens, kv_heads, per_group, head_dim)
    query_pos = lax.axis_index("ctx") * tokens + lax.broadcasted_iota(jnp.int32, (tokens, 1), 0)
    score_scale = head_dim ** (-0.5)
    initial = (
        jnp.full((sequences, kv_heads, per_group, tokens), MASKED, jnp.float32),
        jnp.zeros((sequences, kv_heads, per_group, tokens), jnp.float32),
        jnp.zeros((sequences, kv_heads, per_group, tokens, head_dim), jnp.float32),
    )
    key_rows = lax.all_gather(teacher_k, "ctx", axis=1, tiled=True)
    value_rows = lax.all_gather(teacher_v, "ctx", axis=1, tiled=True)
    key_ids = lax.all_gather(id_values, "ctx", axis=1, tiled=True)
    piece_rows = key_rows.shape[1]
    block_rows = math.gcd(piece_rows, 512)

    def one_block(block_index, state_now):
        running_max, denominator, weighted_sum = state_now
        block_start = block_index * block_rows
        key_block = lax.dynamic_slice_in_dim(key_rows, block_start, block_rows, 1).reshape(
            sequences, block_rows, kv_heads, head_dim
        )
        value_block = lax.dynamic_slice_in_dim(value_rows, block_start, block_rows, 1).reshape(
            sequences, block_rows, kv_heads, head_dim
        )
        id_block = lax.dynamic_slice_in_dim(key_ids, block_start, block_rows, 1).astype(jnp.float32)
        key_pos = block_start + lax.broadcasted_iota(jnp.int32, (1, block_rows), 1)
        visible = (key_pos <= query_pos)[None] & (own_ids[:, :, None] == id_block[:, None, :])
        visible = visible[:, None, None]
        scores = (
            jnp.einsum(
                "sqkgd,spkd->skgqp", grouped_q, key_block, preferred_element_type=jnp.float32
            )
            * score_scale
        )
        new_max = jnp.maximum(running_max, jnp.max(jnp.where(visible, scores, MASKED), axis=-1))
        weights = jnp.where(visible, jnp.exp(scores - new_max[..., None]), 0.0)
        factor = jnp.exp(running_max - new_max)
        denominator = denominator * factor + jnp.sum(weights, axis=-1)
        weighted_sum = weighted_sum * factor[..., None] + jnp.einsum(
            "skgqp,spkd->skgqd",
            weights.astype(jnp.bfloat16),
            value_block,
            preferred_element_type=jnp.float32,
        )
        return (new_max, denominator, weighted_sum)

    final_max, denominator, weighted_sum = lax.fori_loop(
        0, piece_rows // block_rows, one_block, initial
    )
    teacher = (weighted_sum / denominator[..., None]).reshape(
        sequences, local_heads, tokens, head_dim
    )
    difference = student - teacher
    errors = jnp.mean(difference * difference, axis=-1)
    partial_loss = jnp.sum(loss_weight * errors)
    summed = lax.psum(partial_loss, ("ctx", "head", "dp"))
    loss = summed / (
        sequences
        * local_heads
        * tokens
        * lax.axis_size("ctx")
        * lax.axis_size("head")
        * lax.axis_size("dp")
    )
    student_out = (
        jnp.transpose(student, (0, 2, 1, 3))
        .reshape(sequences, tokens, features)
        .astype(jnp.bfloat16)
    )
    teacher_out = (
        jnp.transpose(teacher, (0, 2, 1, 3))
        .reshape(sequences, tokens, features)
        .astype(jnp.bfloat16)
    )
    return (student_out, teacher_out, loss)


def solution(mesh):
    placed = (
        P("dp", "ctx", "head"),
        P("dp", "ctx", "head"),
        P("dp", "ctx", "head"),
        P("dp", "head", "ctx"),
        P("dp", "head", "ctx"),
        P("dp", "head", None, "ctx"),
        P("head"),
        P("dp", "ctx", "head"),
        P("dp", "ctx", "head"),
        P("dp", "ctx", "head"),
        P("dp", "ctx"),
        P("dp", "head", "ctx"),
    )
    return jax.shard_map(
        on_device,
        mesh=mesh,
        in_specs=placed,
        out_specs=(P("dp", "ctx", "head"), P("dp", "ctx", "head"), P()),
        check_vma=False,
    )
```

profile of v0, /device:TPU:1, one launch (start us, length us, event | category | flops | bytes accessed | tf_op | source)
XLA Modules:
  0.0 321.8 jit_solution(3871048183611870563)
XLA Ops:
  2.5 4.5 %collective-permute-start.1 = (bf16[1,3]{1,0:T(2,128)(2,1)}, bf16[1,3]{1,0:T(2,128)(2,1)}, u32[]{:S(2)}, u32[]{:S(2)}) collective-permute-start(bf16[1,3]{1,0:T(2,128)(2,1)} %slice.68), channel_id=1, source_target_pairs={{0,32},{32,64},{64,96},{96,128},{128,160},{160,192},{192,224},{1,3... | collective-permute-start | bytes 26 | tf_op jit(solution)/shard_map/ppermute | solution.py:19
  8.3 1.9 collective-permute-start.2
  13.6 2.0 reshape.851
  17.7 9.6 %all_gather.9 = bf16[1,2048]{1,0:T(2,128)(2,1)S(1)} all-gather(bf16[1,256]{1,0:T(2,128)(2,1)S(1)} %get-tuple-element.446), channel_id=1, replica_groups=mesh['ctx'=8,'head'=4,'dp'=8] {'ctx'}, dimensions={1}, use_global_device_ids=true | all-gather | bytes 4608 | tf_op jit(solution)/shard_map/all_gather | solution.py:186
  28.6 1.6 reduce_sum.58
  30.4 1.9 reduce_window_sum.11
  32.7 1.9 fusion.57
  42.1 2.0 convolution_add_fusion.4
  44.1 2.0 fusion.75
  46.1 2.7 copy.75
  52.4 13.3 %all_gather.10 = bf16[1,2048,128]{2,1,0:T(8,128)(2,1)S(1)} all-gather(bf16[1,256,128]{2,1,0:T(8,128)(2,1)} %param.28), channel_id=1, replica_groups=mesh['ctx'=8,'head'=4,'dp'=8] {'ctx'}, dimensions={1}, use_global_device_ids=true | all-gather | bytes 589824 | tf_op jit(solution)/shard_map/all_gather | solution.py:184
  65.7 14.4 %all_gather.11 = bf16[1,2048,128]{2,1,0:T(8,128)(2,1)} all-gather(bf16[1,256,128]{2,1,0:T(8,128)(2,1)} %param.29), channel_id=1, replica_groups=mesh['ctx'=8,'head'=4,'dp'=8] {'ctx'}, dimensions={1}, use_global_device_ids=true | all-gather | bytes 589824 | tf_op jit(solution)/shard_map/all_gather | solution.py:185
  80.1 35.0 %while.56 = (s32[]{:T(128)}, f32[1,1,7,256]{3,2,1,0:T(8,128)S(1)}, f32[1,1,7,256]{3,2,1,0:T(8,128)S(1)}, f32[1,1,7,256,128]{4,3,2,1,0:T(8,128)}, f32[1,256]{1,0:...) while((s32[]{:T(128)}, f32[1,1,7,256]{3,2,1,0:T(8,128)S(1)}, ...), condition=%wide.region_13.14_spmd.clone, body=%wide.region_10.13_spmd.clone.sunk | while | flops 480947968 | bytes 28897516 | solution.py:221
  81.0 2.5 fusion.175
  83.5 4.3 %fusion.178 = f32[1,1,7,256,128]{4,3,2,1,0:T(8,128)} fusion(f32[512,256,7]{1,0,2:T(8,128)} %get-tuple-element.617, f32[7,256]{1,0:T(8,128)S(1)} %bitcast.346, pred[256,512]{0,1:T(8,128)(4,1)S(1)} %compare_and_fusion.3, f32[1,1,7,256,128]{4,3,2,1,0:T(8,128)} %get-tuple-element.696, f32[7,256]{1,0:T(8,128)S(1)} %get-tuple-element.618, ...), kind=kOutput, calls=%fused_computation.45.clone.1 | convolution fusion | flops 239239168 | bytes 5781509 | tf_op jit(solution)/shard_map/while/body/eval_jaxpr/skgqp,spkd->skgqd/dot_general | solution.py:213
  89.5 2.5 fusion.175
  92.1 4.6 %fusion.178 = f32[1,1,7,256,128]{4,3,2,1,0:T(8,128)} fusion(f32[512,256,7]{1,0,2:T(8,128)} %get-tuple-element.617, f32[7,256]{1,0:T(8,128)S(1)} %bitcast.346, pred[256,512]{0,1:T(8,128)(4,1)S(1)} %compare_and_fusion.3, f32[1,1,7,256,128]{4,3,2,1,0:T(8,128)} %get-tuple-element.696, f32[7,256]{1,0:T(8,128)S(1)} %get-tuple-element.618, ...), kind=kOutput, calls=%fused_computation.45.clone.1 | convolution fusion | flops 239239168 | bytes 5781509 | tf_op jit(solution)/shard_map/while/body/eval_jaxpr/skgqp,spkd->skgqd/dot_general | solution.py:213
  98.4 2.5 fusion.175
  100.9 4.6 %fusion.178 = f32[1,1,7,256,128]{4,3,2,1,0:T(8,128)} fusion(f32[512,256,7]{1,0,2:T(8,128)} %get-tuple-element.617, f32[7,256]{1,0:T(8,128)S(1)} %bitcast.346, pred[256,512]{0,1:T(8,128)(4,1)S(1)} %compare_and_fusion.3, f32[1,1,7,256,128]{4,3,2,1,0:T(8,128)} %get-tuple-element.696, f32[7,256]{1,0:T(8,128)S(1)} %get-tuple-element.618, ...), kind=kOutput, calls=%fused_computation.45.clone.1 | convolution fusion | flops 239239168 | bytes 5781509 | tf_op jit(solution)/shard_map/while/body/eval_jaxpr/skgqp,spkd->skgqd/dot_general | solution.py:213
  107.2 2.5 fusion.175
  109.7 4.6 %fusion.178 = f32[1,1,7,256,128]{4,3,2,1,0:T(8,128)} fusion(f32[512,256,7]{1,0,2:T(8,128)} %get-tuple-element.617, f32[7,256]{1,0:T(8,128)S(1)} %bitcast.346, pred[256,512]{0,1:T(8,128)(4,1)S(1)} %compare_and_fusion.3, f32[1,1,7,256,128]{4,3,2,1,0:T(8,128)} %get-tuple-element.696, f32[7,256]{1,0:T(8,128)S(1)} %get-tuple-element.618, ...), kind=kOutput, calls=%fused_computation.45.clone.1 | convolution fusion | flops 239239168 | bytes 5781509 | tf_op jit(solution)/shard_map/while/body/eval_jaxpr/skgqp,spkd->skgqd/dot_general | solution.py:213
  115.1 1.5 fusion.91
  117.8 2.5 fusion.113
  120.3 3.0 convolution_multiply_fusion
  124.8 1.4 fusion.71
  126.3 2.2 fusion.59
  129.1 3.7 %subtract_bitcast_fusion = f32[4,1,7,128,128]{4,3,0,2,1:T(8,128)S(1)} fusion(f32[7,4,64,128]{3,2,1,0:T(8,128)S(1)} %fusion.71, f32[128,128]{1,0:T(8,128)S(1)} %fusion.105, f32[7,4]{1,0:T(8,128)S(1)} %copy.62, f32[1,4,64,7,128]{4,2,1,3,0:T(8,128)S(1)} %copy.67, f32[4,64,7]{1,0,2:T(4,128)S(1)} %rsqrt.34, f32[7,4,64]{2,1,0:T(4,128)S(1)} %multiply_bitcast_fusion), kind=kOutput, calls=%fused_computation.66 | convolution fusion | flops 353697792 | bytes 3750000 | tf_op jit(solution)/shard_map/vmap(vmap(vmap()))/dot_general | solution.py:23
  135.3 1.7 divide_multiply_fusion
  137.0 2.5 copy.70
  139.5 2.3 fusion.114
  141.8 2.0 convolution_bitcast_fusion.3
  143.8 3.8 %convolution_bitcast_fusion.1 = f32[4,1,7,128,128]{4,3,0,2,1:T(8,128)S(1)} fusion(f32[7,4,64,128]{3,2,1,0:T(8,128)S(1)} %fusion.114, f32[1,4,64,7,128]{4,2,1,3,0:T(8,128)S(1)} %copy-done.2, f32[4,64,7]{1,0,2:T(4,128)S(1)} %rsqrt.34, f32[7,4,64]{2,1,0:T(4,128)S(1)} %copy-done.12), kind=kOutput, calls=%fused_computation.67 | convolution fusion | flops 352780288 | bytes 3684352 | tf_op jit(solution)/shard_map/vmap(vmap(vmap()))/dot_general | solution.py:23
  149.1 9.2 %while.53 = (s32[]{:T(128)}, f32[1,7,128,128]{3,2,1,0:T(8,128)S(1)}, f32[1,7,128,128]{3,2,1,0:T(8,128)S(1)}, f32[4,1,7,128,128]{4,3,2,1,0:T(8,128)S(1)}, f32[4,1,7,128,128]{4,3,2,1,0:T(8,128)}, /*index=5*/s32[]{:T(128)}) while((s32[]{:T(128)}, f32[1,7,128,128]{3,2,1,0:T(8,128)S(1)}, f32[1,7,128,128]{3,2,1,0:T(8,128)S(1)}, ...), condition=%wide.region_3.4_spmd, body=%wide.region_2.3_spmd.sunk | while | flops 352436224 | bytes 5047369 | solution.py:142
  149.1 1.6 fusion.163
  151.4 1.6 fusion.163
  153.7 1.6 fusion.163
  156.0 1.6 fusion.163
  158.3 60.6 %while.55 = (s32[]{:T(128)}, f32[1,7,128,128]{3,2,1,0:T(8,128)S(1)}, f32[1,7,128,128]{3,2,1,0:T(8,128)S(1)}, f32[1,7,128,128]{3,2,1,0:T(8,128)S(1)}, s32[]{:T(128)}, /*index=5*/s32[]{:T(128)}) while((s32[]{:T(128)}, f32[1,7,128,128]{3,2,1,0:T(8,128)S(1)}, f32[1,7,128,128]{3,2,1,0:T(8,128)S(1)}, f32[1,7,128,128]{3,2,1,0:T(8,128)S(1)}, ...), condition=%wide.region_5.6_spmd.clone, body=%wide.region_4.5_spmd.clone.sunk | while | flops 176619520 | bytes 3211383 | solution.py:150
  158.9 1.9 collective-permute-start
  160.8 2.9 collective-permute-done
  165.3 4.5 %collective-permute-start = (bf16[1,7,128,128]{3,2,1,0:T(8,128)(2,1)S(1)}, bf16[1,7,128,128]{3,2,1,0:T(8,128)(2,1)}, u32[]{:S(2)}, u32[]{:S(2)}) collective-permute-start(bf16[1,7,128,128]{3,2,1,0:T(8,128)(2,1)S(1)} %fusion.172), channel_id=1, source_target_pairs={{0,32},{32,64},{64,96},{96,128},{128,160},{160,192},{192,224},{1,3... | collective-permute-start | bytes 688136 | tf_op jit(solution)/shard_map/while/body/eval_jaxpr/ppermute | solution.py:19
  169.9 2.9 collective-permute-done
  174.4 4.5 %collective-permute-start = (bf16[1,7,128,128]{3,2,1,0:T(8,128)(2,1)S(1)}, bf16[1,7,128,128]{3,2,1,0:T(8,128)(2,1)}, u32[]{:S(2)}, u32[]{:S(2)}) collective-permute-start(bf16[1,7,128,128]{3,2,1,0:T(8,128)(2,1)S(1)} %fusion.172), channel_id=1, source_target_pairs={{0,32},{32,64},{64,96},{96,128},{128,160},{160,192},{192,224},{1,3... | collective-permute-start | bytes 688136 | tf_op jit(solution)/shard_map/while/body/eval_jaxpr/ppermute | solution.py:19
  178.9 2.9 collective-permute-done
  183.4 4.5 %collective-permute-start = (bf16[1,7,128,128]{3,2,1,0:T(8,128)(2,1)S(1)}, bf16[1,7,128,128]{3,2,1,0:T(8,128)(2,1)}, u32[]{:S(2)}, u32[]{:S(2)}) collective-permute-start(bf16[1,7,128,128]{3,2,1,0:T(8,128)(2,1)S(1)} %fusion.172), channel_id=1, source_target_pairs={{0,32},{32,64},{64,96},{96,128},{128,160},{160,192},{192,224},{1,3... | collective-permute-start | bytes 688136 | tf_op jit(solution)/shard_map/while/body/eval_jaxpr/ppermute | solution.py:19
  187.9 2.9 collective-permute-done
  192.4 4.5 %collective-permute-start = (bf16[1,7,128,128]{3,2,1,0:T(8,128)(2,1)S(1)}, bf16[1,7,128,128]{3,2,1,0:T(8,128)(2,1)}, u32[]{:S(2)}, u32[]{:S(2)}) collective-permute-start(bf16[1,7,128,128]{3,2,1,0:T(8,128)(2,1)S(1)} %fusion.172), channel_id=1, source_target_pairs={{0,32},{32,64},{64,96},{96,128},{128,160},{160,192},{192,224},{1,3... | collective-permute-start | bytes 688136 | tf_op jit(solution)/shard_map/while/body/eval_jaxpr/ppermute | solution.py:19
  196.9 2.9 collective-permute-done
  201.4 4.5 %collective-permute-start = (bf16[1,7,128,128]{3,2,1,0:T(8,128)(2,1)S(1)}, bf16[1,7,128,128]{3,2,1,0:T(8,128)(2,1)}, u32[]{:S(2)}, u32[]{:S(2)}) collective-permute-start(bf16[1,7,128,128]{3,2,1,0:T(8,128)(2,1)S(1)} %fusion.172), channel_id=1, source_target_pairs={{0,32},{32,64},{64,96},{96,128},{128,160},{160,192},{192,224},{1,3... | collective-permute-start | bytes 688136 | tf_op jit(solution)/shard_map/while/body/eval_jaxpr/ppermute | solution.py:19
  205.9 2.9 collective-permute-done
  210.5 4.5 %collective-permute-start = (bf16[1,7,128,128]{3,2,1,0:T(8,128)(2,1)S(1)}, bf16[1,7,128,128]{3,2,1,0:T(8,128)(2,1)}, u32[]{:S(2)}, u32[]{:S(2)}) collective-permute-start(bf16[1,7,128,128]{3,2,1,0:T(8,128)(2,1)S(1)} %fusion.172), channel_id=1, source_target_pairs={{0,32},{32,64},{64,96},{96,128},{128,160},{160,192},{192,224},{1,3... | collective-permute-start | bytes 688136 | tf_op jit(solution)/shard_map/while/body/eval_jaxpr/ppermute | solution.py:19
  215.0 2.9 collective-permute-done
  218.9 15.9 %while.54 = (s32[]{:T(128)}, f32[1,7,128,128]{3,2,1,0:T(8,128)S(1)}, f32[4,1,7,64,128]{4,3,0,2,1:T(8,128)}, f32[4,1,7,128,128]{4,3,2,1,0:T(8,128)S(1)}, f32[4,1,...) while((s32[]{:T(128)}, ...), condition=%wide.region_8.9_spmd, body=%wide.region_7.8_spmd.sunk | while | flops 264413184 | bytes 3901525 | solution.py:159
  219.0 2.4 fusion.169
  221.3 1.6 fusion.168
  223.0 2.3 fusion.169
  225.3 1.6 fusion.168
  227.0 2.3 fusion.169
  229.2 1.6 fusion.168
  230.9 2.3 fusion.169
  233.2 1.6 fusion.168
  234.8 1.5 fusion.68
  236.4 2.0 fusion.67
  240.2 79.5 %psum.7 = f32[]{:T(128)} all-reduce(f32[]{:T(128)} %multiply_reduce_fusion), channel_id=1, replica_groups=mesh['ctx'=8,'head'=4,'dp'=8] {'ctx','head','dp'}, use_global_device_ids=true, to_apply=%region_16.17 | all-reduce | flops 1 | bytes 8 | tf_op jit(solution)/shard_map/psum | solution.py:230
  (207 shorter events, 50.6 us)
Async XLA Ops:
  1.9 15.7 %copy-start.24 = (bf16[1,256]{1,0:T(2,128)(2,1)}, bf16[1,256]{1,0:T(2,128)(2,1)S(1)}, u32[]{:S(2)}) copy-start(bf16[1,256]{1,0:T(2,128)(2,1)S(1)} %get-tuple-element.446) | copy-start | bytes 1540
  2.5 121.0 %collective-permute-start.1 = (bf16[1,3]{1,0:T(2,128)(2,1)}, bf16[1,3]{1,0:T(2,128)(2,1)}, u32[]{:S(2)}, u32[]{:S(2)}) collective-permute-start(bf16[1,3]{1,0:T(2,128)(2,1)} %slice.68), channel_id=1, source_target_pairs={{0,32},{32,64},{64,96},{96,128},{128,160},{160,192},{192,224},{1,3... | collective-permute-start | bytes 26 | tf_op jit(solution)/shard_map/ppermute | solution.py:19
  8.3 124.7 %collective-permute-start.2 = (bf16[1,3,896]{2,1,0:T(4,128)(2,1)}, bf16[1,3,896]{2,1,0:T(4,128)(2,1)}, u32[]{:S(2)}, u32[]{:S(2)}) collective-permute-start(bf16[1,3,896]{2,1,0:T(4,128)(2,1)} %slice.57), channel_id=1, source_target_pairs={{0,32},{32,64},{64,96},{96,128},{128,160},{160,192},{192,224},{1,3... | collective-permute-start | bytes 16136 | tf_op jit(solution)/shard_map/ppermute | solution.py:19
  11.5 1.8 copy-start.26
  11.5 1.9 copy-start.8
  13.6 3.1 copy-start.7
  27.3 3.0 copy-start.28
  27.3 5.1 %copy-start.29 = (f32[1,7,256]{2,0,1:T(1,128)S(1)}, f32[1,7,256]{2,0,1:T(1,128)}, u32[]{:S(2)}) copy-start(f32[1,7,256]{2,0,1:T(1,128)} %param.23) | copy-start | bytes 21508
  28.6 100.5 %copy-start.1 = (f32[1,4,64,7,128]{4,2,1,3,0:T(8,128)}, f32[1,4,64,7,128]{4,2,1,3,0:T(8,128)S(1)}, u32[]{:S(2)}) copy-start(f32[1,4,64,7,128]{4,2,1,3,0:T(8,128)S(1)} %copy.67) | copy-start | bytes 2752516
  32.4 3.3 %copy-start.16 = (f32[4,64]{1,0:T(4,128)}, f32[4,64]{1,0:T(4,128)S(1)}, u32[]{:S(2)}) copy-start(f32[4,64]{1,0:T(4,128)S(1)} %reshape.821) | copy-start | bytes 3076
  32.5 3.2 %copy-start.13 = (f32[7,4,64]{2,1,0:T(4,128)}, f32[7,4,64]{2,1,0:T(4,128)S(1)}, u32[]{:S(2)}) copy-start(f32[7,4,64]{2,1,0:T(4,128)S(1)} %mul.360) | copy-start | bytes 21508
  32.7 3.1 copy-start.9
  46.1 2.7 copy-start.6
  46.1 2.9 copy-start.18
  83.5 4.3 %copy-start = (f32[512,256,7]{1,0,2:T(8,128)S(1)}, f32[512,256,7]{1,0,2:T(8,128)}, u32[]{:S(2)}) copy-start(f32[512,256,7]{1,0,2:T(8,128)} %get-tuple-element.617) | copy-start | bytes 11010052 | tf_op jit(solution)/shard_map/while
  92.1 4.6 %copy-start = (f32[512,256,7]{1,0,2:T(8,128)S(1)}, f32[512,256,7]{1,0,2:T(8,128)}, u32[]{:S(2)}) copy-start(f32[512,256,7]{1,0,2:T(8,128)} %get-tuple-element.617) | copy-start | bytes 11010052 | tf_op jit(solution)/shard_map/while
  100.9 4.6 %copy-start = (f32[512,256,7]{1,0,2:T(8,128)S(1)}, f32[512,256,7]{1,0,2:T(8,128)}, u32[]{:S(2)}) copy-start(f32[512,256,7]{1,0,2:T(8,128)} %get-tuple-element.617) | copy-start | bytes 11010052 | tf_op jit(solution)/shard_map/while
  109.7 4.6 %copy-start = (f32[512,256,7]{1,0,2:T(8,128)S(1)}, f32[512,256,7]{1,0,2:T(8,128)}, u32[]{:S(2)}) copy-start(f32[512,256,7]{1,0,2:T(8,128)} %get-tuple-element.617) | copy-start | bytes 11010052 | tf_op jit(solution)/shard_map/while
  116.8 3.5 %copy-start.10 = (pred[4,64,64]{2,1,0:T(8,128)(4,1)S(1)}, pred[4,64,64]{2,1,0:T(8,128)(4,1)}, u32[]{:S(2)}) copy-start(pred[4,64,64]{2,1,0:T(8,128)(4,1)} %copy-done.9) | copy-start | bytes 49156
  116.8 3.5 %copy-start.14 = (f32[7,4,64]{2,1,0:T(4,128)S(1)}, f32[7,4,64]{2,1,0:T(4,128)}, u32[]{:S(2)}) copy-start(f32[7,4,64]{2,1,0:T(4,128)} %copy-done.13) | copy-start | bytes 21508
  120.3 3.1 copy-start.23
  120.3 3.1 copy-start.32
  120.3 3.2 copy-start.25
  120.3 4.0 %copy-start.27 = (s32[1,256]{1,0:T(1,128)S(1)}, s32[1,256]{1,0:T(1,128)}, u32[]{:S(2)}) copy-start(s32[1,256]{1,0:T(1,128)} %param.30) | copy-start | bytes 3076
  120.3 4.0 %copy-start.17 = (f32[4,64]{1,0:T(4,128)S(1)}, f32[4,64]{1,0:T(4,128)}, u32[]{:S(2)}) copy-start(f32[4,64]{1,0:T(4,128)} %copy-done.16) | copy-start | bytes 3076
  123.5 5.6 %copy-start.11 = (f32[7,4,64]{2,1,0:T(4,128)}, f32[7,4,64]{2,1,0:T(4,128)S(1)}, u32[]{:S(2)}) copy-start(f32[7,4,64]{2,1,0:T(4,128)S(1)} %multiply_bitcast_fusion) | copy-start | bytes 21508
  124.8 1.4 copy-start.3
  126.3 2.2 copy-start.21
  126.3 2.2 copy-start.22
  126.3 2.2 copy-start.19
  126.3 2.2 copy-start.20
  134.0 1.3 copy-start.15
  139.5 2.3 copy-start.4
  141.8 2.0 copy-start.2
  141.8 2.0 copy-start.12
  158.9 4.9 %collective-permute-start = (bf16[1,7,128,128]{3,2,1,0:T(8,128)(2,1)S(1)}, bf16[1,7,128,128]{3,2,1,0:T(8,128)(2,1)}, u32[]{:S(2)}, u32[]{:S(2)}) collective-permute-start(bf16[1,7,128,128]{3,2,1,0:T(8,128)(2,1)S(1)} %fusion.172), channel_id=1, source_target_pairs={{0,32},{32,64},{64,96},{96,128},{128,160},{160,192},{192,224},{1,3... | collective-permute-start | bytes 688136 | tf_op jit(solution)/shard_map/while/body/eval_jaxpr/ppermute | solution.py:19
  165.3 7.4 %collective-permute-start = (bf16[1,7,128,128]{3,2,1,0:T(8,128)(2,1)S(1)}, bf16[1,7,128,128]{3,2,1,0:T(8,128)(2,1)}, u32[]{:S(2)}, u32[]{:S(2)}) collective-permute-start(bf16[1,7,128,128]{3,2,1,0:T(8,128)(2,1)S(1)} %fusion.172), channel_id=1, source_target_pairs={{0,32},{32,64},{64,96},{96,128},{128,160},{160,192},{192,224},{1,3... | collective-permute-start | bytes 688136 | tf_op jit(solution)/shard_map/while/body/eval_jaxpr/ppermute | solution.py:19
  174.4 7.4 %collective-permute-start = (bf16[1,7,128,128]{3,2,1,0:T(8,128)(2,1)S(1)}, bf16[1,7,128,128]{3,2,1,0:T(8,128)(2,1)}, u32[]{:S(2)}, u32[]{:S(2)}) collective-permute-start(bf16[1,7,128,128]{3,2,1,0:T(8,128)(2,1)S(1)} %fusion.172), channel_id=1, source_target_pairs={{0,32},{32,64},{64,96},{96,128},{128,160},{160,192},{192,224},{1,3... | collective-permute-start | bytes 688136 | tf_op jit(solution)/shard_map/while/body/eval_jaxpr/ppermute | solution.py:19
  183.4 7.4 %collective-permute-start = (bf16[1,7,128,128]{3,2,1,0:T(8,128)(2,1)S(1)}, bf16[1,7,128,128]{3,2,1,0:T(8,128)(2,1)}, u32[]{:S(2)}, u32[]{:S(2)}) collective-permute-start(bf16[1,7,128,128]{3,2,1,0:T(8,128)(2,1)S(1)} %fusion.172), channel_id=1, source_target_pairs={{0,32},{32,64},{64,96},{96,128},{128,160},{160,192},{192,224},{1,3... | collective-permute-start | bytes 688136 | tf_op jit(solution)/shard_map/while/body/eval_jaxpr/ppermute | solution.py:19
  192.4 7.4 %collective-permute-start = (bf16[1,7,128,128]{3,2,1,0:T(8,128)(2,1)S(1)}, bf16[1,7,128,128]{3,2,1,0:T(8,128)(2,1)}, u32[]{:S(2)}, u32[]{:S(2)}) collective-permute-start(bf16[1,7,128,128]{3,2,1,0:T(8,128)(2,1)S(1)} %fusion.172), channel_id=1, source_target_pairs={{0,32},{32,64},{64,96},{96,128},{128,160},{160,192},{192,224},{1,3... | collective-permute-start | bytes 688136 | tf_op jit(solution)/shard_map/while/body/eval_jaxpr/ppermute | solution.py:19
  201.4 7.4 %collective-permute-start = (bf16[1,7,128,128]{3,2,1,0:T(8,128)(2,1)S(1)}, bf16[1,7,128,128]{3,2,1,0:T(8,128)(2,1)}, u32[]{:S(2)}, u32[]{:S(2)}) collective-permute-start(bf16[1,7,128,128]{3,2,1,0:T(8,128)(2,1)S(1)} %fusion.172), channel_id=1, source_target_pairs={{0,32},{32,64},{64,96},{96,128},{128,160},{160,192},{192,224},{1,3... | collective-permute-start | bytes 688136 | tf_op jit(solution)/shard_map/while/body/eval_jaxpr/ppermute | solution.py:19
  210.5 7.4 %collective-permute-start = (bf16[1,7,128,128]{3,2,1,0:T(8,128)(2,1)S(1)}, bf16[1,7,128,128]{3,2,1,0:T(8,128)(2,1)}, u32[]{:S(2)}, u32[]{:S(2)}) collective-permute-start(bf16[1,7,128,128]{3,2,1,0:T(8,128)(2,1)S(1)} %fusion.172), channel_id=1, source_target_pairs={{0,32},{32,64},{64,96},{96,128},{128,160},{160,192},{192,224},{1,3... | collective-permute-start | bytes 688136 | tf_op jit(solution)/shard_map/while/body/eval_jaxpr/ppermute | solution.py:19
  218.9 17.5 %copy-start.5 = (f32[1,1,7,256,128]{4,3,2,1,0:T(8,128)S(1)}, f32[1,1,7,256,128]{4,3,2,1,0:T(8,128)}, u32[]{:S(2)}) copy-start(f32[1,1,7,256,128]{4,3,2,1,0:T(8,128)} %get-tuple-element.264) | copy-start | bytes 2752516
  218.9 17.5 %copy-start.31 = (f32[896]{0:T(1024)S(1)}, f32[896]{0:T(1024)}, u32[]{:S(2)}) copy-start(f32[896]{0:T(1024)} %param.26) | copy-start | bytes 10756
  236.3 2.4 copy-start.30
where the time goes:
time: 326 us; the launch traced here: 322 us
  blocking collectives  117 us (36%)
  matrix products  90.6 us (28%)
  starting transfers between devices  35.3 us (11%)
  other arithmetic  30.9 us (9%)
  local copies, waits for them, and re-layouts  23.3 us (7%)
  waiting for transfers between devices  20.6 us (6%)
  between operations  3.36 us (1%)
    psum x1, blocking collectives, on_device(): summed = lax.psum(partial_loss, ('ctx', 'head', 'dp'))  79.5 us
    ppermute x9, starting transfers between devices, from_behind(): return lax.ppermute(block, axis, route)  35.3 us
    dot_general x18, matrix products, matmul(): return jnp.dot(left, right, precision=PRECISE)  34.2 us
    ppermute x9, waiting for transfers between devices, from_behind(): return lax.ppermute(block, axis, route)  20.6 us
    dot_general x19, matrix products, batched(): return jnp.einsum('shij,shjv->shiv', left, right, precision=PRECISE)  19.2 us
    dot_general x4, matrix products, one_block(): jnp.einsum('skgqp,spkd->skgqd', weights.astype(jnp.bfloat16), value_block...  17.9 us
    all_gather x1, blocking collectives, on_device(): value_rows = lax.all_gather(teacher_v, 'ctx', axis=1, tiled=True)  14.4 us
    all_gather x1, blocking collectives, on_device(): key_rows = lax.all_gather(teacher_k, 'ctx', axis=1, tiled=True)  13.3 us
  transfers between devices with their start and end apart: 9, of which 7 were waited for; matrix products, arithmetic and copies ran while one was open for 27% of the time, Pallas kernels for 0%

commit v1 on v0

v1 whole, which is shorter than its diff:
```python
import math

import jax
import jax.numpy as jnp
from jax import lax
from jax.experimental import pallas as pl
from jax.experimental.pallas import tpu as pltpu
from jax.sharding import PartitionSpec as P

EPSILON = 1e-06
MASKED = -1e30
HEAD = 128
F32 = jnp.float32
BF16 = jnp.bfloat16
VMEM_BYTES = 32 * 1024 * 1024


def nn(a, b, precision=None):
    return lax.dot_general(
        a, b, (((1,), (0,)), ((), ())), precision=precision, preferred_element_type=F32
    )


def nt(a, b):
    return lax.dot_general(a, b, (((1,), (1,)), ((), ())), preferred_element_type=F32)


def tn(a, b):
    return lax.dot_general(a, b, (((0,), (0,)), ((), ())), preferred_element_type=F32)


def head_lanes(h):
    return slice(h * HEAD, (h + 1) * HEAD)


def call(body, outs, *args, scratch=(), flops=0):
    return pl.pallas_call(
        body,
        out_shape=[jax.ShapeDtypeStruct(s, d) for s, d in outs],
        in_specs=[pl.BlockSpec(memory_space=pltpu.VMEM)] * len(args),
        out_specs=[pl.BlockSpec(memory_space=pltpu.VMEM)] * len(outs),
        scratch_shapes=[pltpu.VMEM(s, d) for s, d in scratch],
        compiler_params=pltpu.CompilerParams(vmem_limit_bytes=VMEM_BYTES),
        cost_estimate=pl.CostEstimate(flops=flops, bytes_accessed=0, transcendentals=0),
    )(*args)


def pack_body(tk, tv, sv, ids, kv, rim):
    tokens = tk.shape[1]
    kv[0:tokens] = tk[0]
    kv[tokens : 2 * tokens] = tv[0]
    idf = ids[...].astype(F32)
    rows = lax.broadcasted_iota(jnp.int32, (16, 128), 0)
    block = jnp.zeros((16, 128), F32)
    for i in range(tokens // 128):
        block = jnp.where(rows == i, idf[:, i * 128 : (i + 1) * 128], block)
    kv[2 * tokens : 2 * tokens + 16] = block.astype(BF16)
    features = sv.shape[2]
    rim[:, 0:features] = sv[0, tokens - 16 : tokens, :]
    rim[:, features : features + 128] = jnp.broadcast_to(
        idf[:, tokens - 128 : tokens], (16, 128)
    ).astype(BF16)


def keys_body(k, beta, decay, ids, t_out, uk_out, kend_out, m_out, rows_out, cols_out, eight, a_s, t_s):
    tokens = k.shape[1]
    heads = beta.shape[1]
    half = tokens // 2
    idf = ids[...].astype(F32)
    lane = lax.broadcasted_iota(jnp.int32, (tokens, 128), 1)
    packed = jnp.zeros((tokens, 128), F32)
    for h in range(heads):
        kf = k[0, :, head_lanes(h)].astype(F32)
        norm = lax.rsqrt(jnp.sum(kf * kf, axis=1, keepdims=True) + EPSILON)
        packed = jnp.where(lane == h, norm, packed)
    r8 = packed.T[0:8]
    eight[...] = jnp.zeros_like(eight)
    eight[0, 0:heads] = decay[0]
    eight[1, 0:heads] = beta[0]
    row_index = lax.broadcasted_iota(jnp.int32, (tokens, tokens), 0)
    col_index = lax.broadcasted_iota(jnp.int32, (tokens, tokens), 1)
    upto = jnp.where(row_index <= col_index, 1.0, 0.0)
    run8 = nn(eight[0], upto, lax.Precision.HIGHEST)
    br8 = eight[1] * r8
    fs8 = jnp.where(idf == idf[:, 0:1], jnp.exp(run8), 0.0)
    wend8 = (
        jnp.where(
            idf == idf[:, tokens - 1 : tokens],
            jnp.exp(run8[:, tokens - 1 : tokens] - run8),
            0.0,
        )
        * br8
    )
    ids8 = jnp.broadcast_to(idf, (8, tokens))
    rows_out[...] = jnp.concatenate([run8, br8], axis=0)
    stacked = jnp.concatenate(
        [run8, wend8, fs8 * r8, fs8, ids8, r8, jnp.zeros((80, tokens), F32)], axis=0
    )
    cols = stacked.T
    cols_out[...] = cols
    visible = (col_index < row_index) & (cols[:, 32:33] == idf)
    for h in range(heads):
        kh = k[0, :, head_lanes(h)]
        kk = nt(kh, kh)
        between = jnp.where(visible, jnp.exp(cols[:, h : h + 1] - run8[h : h + 1]), 0.0)
        a = between * br8[h : h + 1] * (cols[:, 40 + h : 41 + h] * kk)
        a_s[h] = a.astype(BF16)
    ri = lax.broadcasted_iota(jnp.int32, (half, half), 0)
    ci = lax.broadcasted_iota(jnp.int32, (half, half), 1)
    eye = jnp.where(ri == ci, 1.0, 0.0)

    def level_mask(k_bits):
        rb, cb = ri >> k_bits, ci >> k_bits
        return jnp.where(((rb & 1) == 1) & (cb == rb - 1), 1.0, 0.0)

    def diag(h, b):
        return a_s[h, b * half : (b + 1) * half, b * half : (b + 1) * half]

    first = level_mask(0)
    for h in range(heads):
        for b in range(2):
            t_s[2 * h + b] = eye - diag(h, b).astype(F32) * first
    for bits in range(1, (half - 1).bit_length()):
        mask = level_mask(bits).astype(BF16)
        for h in range(heads):
            for b in range(2):
                t = t_s[2 * h + b]
                tb = t.astype(BF16)
                p = nn(diag(h, b) * mask, tb)
                t_s[2 * h + b] = t - nn(tb, p.astype(BF16))
    for h in range(heads):
        t11 = t_s[2 * h].astype(BF16)
        t22 = t_s[2 * h + 1].astype(BF16)
        p = nn(a_s[h, half:tokens, 0:half], t11)
        t_out[h, 0:half, 0:half] = t11
        t_out[h, half:tokens, half:tokens] = t22
        t_out[h, 0:half, half:tokens] = jnp.zeros((half, half), BF16)
        t_out[h, half:tokens, 0:half] = (-nn(t22, p.astype(BF16))).astype(BF16)
    er = lax.broadcasted_iota(jnp.int32, (HEAD, HEAD), 0)
    ec = lax.broadcasted_iota(jnp.int32, (HEAD, HEAD), 1)
    for h in range(heads):
        kf = k[0, :, head_lanes(h)].astype(F32)
        uk = nn(t_out[h], (cols[:, 16 + h : 17 + h] * kf).astype(BF16)).astype(BF16)
        uk_out[h] = uk
        kend = (cols[:, 8 + h : 9 + h] * kf).astype(BF16)
        kend_out[h] = kend
        scale = fs8[h : h + 1, tokens - 1 : tokens]
        m_out[h] = jnp.where(er == ec, scale, 0.0) - tn(kend, uk)


def values_body(v, rim, taps, ids, t, kend, m, mi_out, uv_out, x_s, tap_s):
    tokens = v.shape[1]
    features = v.shape[2]
    heads = taps.shape[1]
    count = taps.shape[2]
    first = lax.axis_index("ctx") == 0
    idf = ids[...].astype(F32)
    before = rim[0:1, features : features + 128].astype(F32)
    before = jnp.where(first, -1.0, before)
    longer = jnp.concatenate([before, idf], axis=1)
    keeps = [
        (pltpu.roll(longer, j, 1)[:, 128:] == idf).astype(F32) if j else jnp.ones_like(idf)
        for j in range(count)
    ]
    keep = jnp.concatenate(keeps, axis=0)
    tap_s[...] = jnp.zeros_like(tap_s)
    for h in range(heads):
        tap_s[8 * h : 8 * h + count] = taps[0, h] * keep
    cols = tap_s[...].T
    x_s[0:8] = rim[:, 0:features].astype(F32)[8:16]
    x_s[8 : 8 + tokens] = v[0].astype(F32)
    joined = jnp.where(before[0:1, 127:128] == idf[:, 0:1], 1.0, 0.0)
    for h in range(heads):
        conv = cols[:, 8 * h : 8 * h + 1] * x_s[8 : 8 + tokens, head_lanes(h)]
        for j in range(1, count):
            conv = conv + cols[:, 8 * h + j : 8 * h + j + 1] * x_s[8 - j : 8 - j + tokens, head_lanes(h)]
        values = conv / (1.0 + jnp.exp(-conv))
        uv = nn(t[h], values.astype(BF16)).astype(BF16)
        uv_out[h] = uv
        mi_out[h] = (joined * m[h]).astype(BF16)
        mi_out[heads + h] = tn(kend[h], uv).astype(BF16)


def queries_body(q, k, rim, ids, rows, cols_in, uk, uv, lw, local_out, reader_out, lw_out, lw_s):
    tokens = q.shape[1]
    features = q.shape[2]
    heads = uk.shape[0]
    first = lax.axis_index("ctx") == 0
    idf = ids[...].astype(F32)
    before = jnp.where(first, -1.0, rim[0:1, features : features + 128].astype(F32))
    joined = jnp.where(before[0:1, 127:128] == idf[:, 0:1], 1.0, 0.0)
    row_index = lax.broadcasted_iota(jnp.int32, (tokens, tokens), 0)
    col_index = lax.broadcasted_iota(jnp.int32, (tokens, tokens), 1)
    cols = cols_in[...]
    visible = (col_index <= row_index) & (cols[:, 32:33] == idf)
    lw_s[...] = jnp.zeros_like(lw_s)
    lw_s[0:heads] = lw[0]
    lw_out[...] = lw_s[...].T
    for h in range(heads):
        qh = q[0, :, head_lanes(h)]
        qf = qh.astype(F32)
        norm = lax.rsqrt(jnp.sum(qf * qf, axis=1, keepdims=True) + EPSILON)
        qk = nt(qh, k[0, :, head_lanes(h)])
        between = jnp.where(visible, jnp.exp(cols[:, h : h + 1] - rows[h : h + 1]), 0.0)
        reading = (between * rows[8 + h : 9 + h] * (norm * qk)).astype(BF16)
        local_out[h] = nn(reading, uv[h])
        carried = nn(reading, uk[h])
        reader = (cols[:, 24 + h : 25 + h] * norm) * qf - carried
        reader_out[h] = (joined * reader).astype(BF16)


def teacher_body(q, ids, own, r2, r4, x0, x2, x4, out, full, k_s, v_s, id_s, bias_s):
    tokens = q.shape[1]
    heads = q.shape[2] // HEAD
    halves = tokens // 128
    index = lax.axis_index("ctx")
    odd = lax.rem(index, 2) == 1
    idf = ids[...].astype(F32)

    def place(slot, source):
        k_s[slot * tokens : (slot + 1) * tokens] = source[0:tokens]
        v_s[slot * tokens : (slot + 1) * tokens] = source[tokens : 2 * tokens]
        behind = 4 - slot
        valid = index >= behind
        names = source[2 * tokens : 2 * tokens + 16].astype(F32)
        for i in range(halves):
            at = (slot * halves + i) * 128
            id_s[:, at : at + 128] = jnp.where(valid, names[i : i + 1], -1.0)

    place(0, r4)
    place(2, r2)
    place(4, own)

    @pl.when(odd)
    def _():
        place(1, x2)
        place(3, x0)

    @pl.when(jnp.logical_not(odd))
    def _():
        place(1, x4)
        place(3, x2)

    width = 5 * tokens
    id_col = jnp.broadcast_to(idf, (128, tokens)).T[:, 0:1]
    same = id_col == id_s[...]
    row_index = lax.broadcasted_iota(jnp.int32, (tokens, width), 0)
    col_index = lax.broadcasted_iota(jnp.int32, (tokens, width), 1) - 4 * tokens
    bias_s[...] = jnp.where(same & (col_index <= row_index), 0.0, MASKED)
    scale = math.log2(math.e) / math.sqrt(HEAD)
    span = width - (halves - 1) * 128
    for h in range(heads):
        for r in range(halves):
            qt = q[0, r * 128 : (r + 1) * 128, head_lanes(h)]
            s = nt(qt, k_s[r * 128 : r * 128 + span])
            s = s * scale + bias_s[r * 128 : (r + 1) * 128, r * 128 : r * 128 + span]
            largest = jnp.max(s, axis=1, keepdims=True)
            w = jnp.exp2(s - largest)
            total = jnp.sum(w, axis=1, keepdims=True)
            o = nn(w.astype(BF16), v_s[r * 128 : r * 128 + span]) / total
            full[r * 128 : (r + 1) * 128, head_lanes(h)] = o
            out[0, r * 128 : (r + 1) * 128, head_lanes(h)] = o.astype(BF16)


def chip_body(own, other, m_out, i_out):
    heads = m_out.shape[0]
    odd = lax.rem(lax.axis_index("ctx"), 2) == 1
    for h in range(heads):
        m_own, m_other = own[h], other[h]
        i_own, i_other = own[heads + h], other[heads + h]
        later_m = jnp.where(odd, m_own, m_other)
        later_i = jnp.where(odd, i_own, i_other)
        early_m = jnp.where(odd, m_other, m_own)
        early_i = jnp.where(odd, i_other, i_own)
        m_out[h] = nn(later_m, early_m).astype(BF16)
        i_out[h] = (nn(later_m, early_i) + later_i.astype(F32)).astype(BF16)


def join_body(m, i, arriving, out):
    for h in range(m.shape[0]):
        out[h] = (nn(m[h], arriving[h]) + i[h].astype(F32)).astype(BF16)


def finish_body(arriving, other, local, reader, gain, teacher, lw, out, sums):
    heads = arriving.shape[0]
    odd = lax.rem(lax.axis_index("ctx"), 2) == 1
    total = jnp.zeros(teacher[:, 0:HEAD].shape, F32)
    for h in range(heads):
        s = arriving[h]
        stepped = (nn(other[h], s) + other[heads + h].astype(F32)).astype(BF16)
        s = jnp.where(odd, stepped, s)
        o = local[h] + nn(reader[h], s)
        mean = jnp.sum(o * o, axis=1, keepdims=True) * (1.0 / HEAD)
        student = o * lax.rsqrt(mean + EPSILON) * gain[:, head_lanes(h)]
        out[0, :, head_lanes(h)] = student.astype(BF16)
        difference = student - teacher[:, head_lanes(h)]
        total = total + lw[:, h : h + 1] * (difference * difference)
    partial = jnp.sum(jnp.sum(total, axis=0, keepdims=True), axis=1, keepdims=True)
    sums[...] = jnp.broadcast_to(partial, sums.shape)


def on_device(
    student_q,
    student_k,
    student_v,
    beta,
    log_decay,
    kernel,
    out_gain,
    teacher_q,
    teacher_k,
    teacher_v,
    segment_ids,
    loss_weight,
):
    _, tokens, features = student_q.shape
    heads = beta.shape[1]
    shards = lax.axis_size("ctx")
    everyone = shards * lax.axis_size("head") * lax.axis_size("dp")

    def rotated(block, distance):
        return lax.ppermute(block, "ctx", [(i, (i + distance) % shards) for i in range(shards)])

    def swapped(block):
        return lax.ppermute(block, "ctx", [(i, i ^ 1) for i in range(shards)])

    kv, rim = call(
        pack_body,
        [((2 * tokens + 16, HEAD), BF16), ((16, features + 128), BF16)],
        teacher_k,
        teacher_v,
        student_v,
        segment_ids,
    )
    rim = rotated(rim, 1)
    r2 = rotated(kv, 2)
    r4 = rotated(kv, 4)
    t, uk, kend, m0, rows, cols = call(
        keys_body,
        [
            ((heads, tokens, tokens), BF16),
            ((heads, tokens, HEAD), BF16),
            ((heads, tokens, HEAD), BF16),
            ((heads, HEAD, HEAD), F32),
            ((16, tokens), F32),
            ((tokens, 128), F32),
        ],
        student_k,
        beta,
        log_decay,
        segment_ids,
        scratch=[
            ((2, 8, tokens), F32),
            ((heads, tokens, tokens), BF16),
            ((2 * heads, tokens // 2, tokens // 2), F32),
        ],
        flops=4 * 10**9,
    )
    mi, uv = call(
        values_body,
        [((2 * heads, HEAD, HEAD), BF16), ((heads, tokens, HEAD), BF16)],
        student_v,
        rim,
        kernel,
        segment_ids,
        t,
        kend,
        m0,
        scratch=[((8 + tokens, features), F32), ((128, tokens), F32)],
        flops=2 * 10**9,
    )
    mi_other = swapped(mi)
    local, reader, lw = call(
        queries_body,
        [
            ((heads, tokens, HEAD), F32),
            ((heads, tokens, HEAD), BF16),
            ((tokens, 128), F32),
        ],
        student_q,
        student_k,
        rim,
        segment_ids,
        rows,
        cols,
        uk,
        uv,
        loss_weight,
        scratch=[((128, tokens), F32)],
        flops=2 * 10**9,
    )
    x0, x2, x4 = swapped(kv), swapped(r2), swapped(r4)
    m_chip, i_chip = call(
        chip_body,
        [((heads, HEAD, HEAD), BF16), ((heads, HEAD, HEAD), BF16)],
        mi,
        mi_other,
        flops=10**8,
    )
    behind = rotated(i_chip, 2)
    teacher_out, teacher = call(
        teacher_body,
        [((1, tokens, features), BF16), ((tokens, features), F32)],
        teacher_q,
        segment_ids,
        kv,
        r2,
        r4,
        x0,
        x2,
        x4,
        scratch=[
            ((5 * tokens, HEAD), BF16),
            ((5 * tokens, HEAD), BF16),
            ((1, 5 * tokens), F32),
            ((tokens, 5 * tokens), F32),
        ],
        flops=5 * 10**9,
    )
    (joined,) = call(
        join_body, [((heads, HEAD, HEAD), BF16)], m_chip, i_chip, behind, flops=10**8
    )
    arriving = rotated(joined, 2)
    student_out, sums = call(
        finish_body,
        [((1, tokens, features), BF16), ((everyone, 128), F32)],
        arriving,
        mi_other,
        local,
        reader,
        out_gain.reshape(1, features),
        teacher,
        lw,
        flops=10**9,
    )
    gathered = lax.all_to_all(sums, ("ctx", "head", "dp"), 0, 0, tiled=True)
    loss = jnp.sum(gathered[:, 0]) / (everyone * heads * tokens * HEAD)
    return (student_out, teacher_out, loss)


def solution(mesh):
    placed = (
        P("dp", "ctx", "head"),
        P("dp", "ctx", "head"),
        P("dp", "ctx", "head"),
        P("dp", "head", "ctx"),
        P("dp", "head", "ctx"),
        P("dp", "head", None, "ctx"),
        P("head"),
        P("dp", "ctx", "head"),
        P("dp", "ctx", "head"),
        P("dp", "ctx", "head"),
        P("dp", "ctx"),
        P("dp", "head", "ctx"),
    )
    return jax.shard_map(
        on_device,
        mesh=mesh,
        in_specs=placed,
        out_specs=(P("dp", "ctx", "head"), P("dp", "ctx", "head"), P()),
        check_vma=False,
    )
```

time: 326 us -> 69 us (0.21); the launches traced: 322 us -> 68.6 us
  matrix products: 90.6 us -> 0 us
  blocking collectives: 117 us -> 26.4 us
  other arithmetic: 30.9 us -> 0.63 us
  starting transfers between devices: 35.3 us -> 11.8 us
  local copies, waits for them, and re-layouts: 23.3 us -> 4.75 us
  Pallas kernels: 0 us -> 17.8 us
  waiting for transfers between devices: 20.6 us -> 4.62 us
    dot_general x49 -> x0, matrix products: 90.6 us -> none  [the longest x18 34.2 us: matmul(): return jnp.dot(left, right, precision=PRECISE)]
    psum x1 -> x0, blocking collectives: 79.5 us -> none  [on_device(): summed = lax.psum(partial_loss, ('ctx', 'head', 'dp'))]
    all_gather x3 -> x0, blocking collectives: 37.3 us -> none  [the longest x1 14.4 us: on_device(): value_rows = lax.all_gather(teacher_v, 'ctx', axis=1, tiled=True)]
    all_to_all x0 -> x1, blocking collectives: none -> 26.4 us  [on_device(): gathered = lax.all_to_all(sums, ('ctx', 'head', 'dp'), 0, 0, tiled=True)]
    ppermute x9, starting transfers between devices: 35.3 us -> 11.8 us  [the longest x5 6.06 us: rotated(): lax.ppermute(block, 'ctx', [(i, (i + distance) % shards) for i in range(s...]
    pallas_call x0 -> x8, Pallas kernels: none -> 17.8 us  [call(): pl.pallas_call(body, out_shape=[jax.ShapeDtypeStruct(s, d) for s, d in ou...]
    ppermute x9, waiting for transfers between devices: 20.6 us -> 4.62 us  [the longest x5 4.61 us: rotated(): lax.ppermute(block, 'ctx', [(i, (i + distance) % shards) for i in range(s...]
    convert_element_type x18 -> x0, other arithmetic: 11.7 us -> none  [the longest x7 6.78 us: advance(): from_behind(leaving.astype(jnp.bfloat16), 'ctx', 1).astype(leaving.dtype)]
  transfers between devices with their start and end apart: 9 -> 9, of which waited for: 7 -> 4; matrix products, arithmetic and copies ran while one was open for 27% -> 0% of each run, Pallas kernels for 0% -> 20%
where the time goes in v1:
time: 69 us; the launch traced here: 68.6 us
  blocking collectives  26.4 us (38%)
  Pallas kernels  17.8 us (26%)
  starting transfers between devices  11.8 us (17%)
  local copies, waits for them, and re-layouts  4.75 us (7%)
  waiting for transfers between devices  4.62 us (7%)
  between operations  2.57 us (4%)
    all_to_all x1, blocking collectives, on_device(): gathered = lax.all_to_all(sums, ('ctx', 'head', 'dp'), 0, 0, tiled=True)  26.4 us
    pallas_call x8, Pallas kernels, call(): pl.pallas_call(body, out_shape=[jax.ShapeDtypeStruct(s, d) for s, d in ou...  17.8 us
    ppermute x5, starting transfers between devices, rotated(): lax.ppermute(block, 'ctx', [(i, (i + distance) % shards) for i in range(s...  6.06 us
    ppermute x4, starting transfers between devices, swapped(): return lax.ppermute(block, 'ctx', [(i, i ^ 1) for i in range(shards)])  5.78 us
    unnamed x31, local copies, waits for them, and re-layouts  4.75 us
    ppermute x5, waiting for transfers between devices, rotated(): lax.ppermute(block, 'ctx', [(i, (i + distance) % shards) for i in range(s...  4.61 us
  transfers between devices with their start and end apart: 9, of which 4 were waited for; matrix products, arithmetic and copies ran while one was open for 0% of the time, Pallas kernels for 20%

profile of v1, /device:TPU:1, one launch (start us, length us, event | category | flops | bytes accessed | tf_op | source)
XLA Modules:
  0.0 68.6 jit_solution(14946438320946469360)
XLA Ops:
  0.6 0.0 copy-start
  0.6 1.0 %copy-done = bf16[1,256,896]{2,1,0:T(8,128)(2,1)S(1)} copy-done((bf16[1,256,896]{2,1,0:T(8,128)(2,1)S(1)}, bf16[1,256,896]{2,1,0:T(8,128)(2,1)}, u32[]{:S(2)}) %copy-start) | copy-done | bytes 458776
  1.7 0.0 copy-start.2
  1.7 0.8 %copy-done.2 = bf16[1,256,128]{2,1,0:T(8,128)(2,1)S(1)} copy-done((bf16[1,256,128]{2,1,0:T(8,128)(2,1)S(1)}, bf16[1,256,128]{2,1,0:T(8,128)(2,1)}, u32[]{:S(2)}) %copy-start.2) | copy-done | bytes 65560
  2.5 0.0 copy-start.3
  2.5 0.8 %copy-done.3 = bf16[1,256,128]{2,1,0:T(8,128)(2,1)S(1)} copy-done((bf16[1,256,128]{2,1,0:T(8,128)(2,1)S(1)}, bf16[1,256,128]{2,1,0:T(8,128)(2,1)}, u32[]{:S(2)}) %copy-start.3) | copy-done | bytes 65560
  3.3 0.0 copy-start.4
  3.3 0.7 copy-done.4
  4.0 0.0 copy-start.10
  4.0 0.0 copy-start.6
  4.0 0.0 copy-start.11
  4.0 2.6 %collective-permute-start = (bf16[16,1024]{1,0:T(8,128)(2,1)S(1)}, bf16[16,1024]{1,0:T(8,128)(2,1)S(1)}, u32[]{:S(2)}, u32[]{:S(2)}) collective-permute-start(bf16[16,1024]{1,0:T(8,128)(2,1)S(1)} %get-tuple-element.22), channel_id=1, source_target_pairs={{0,32},{32,64},{64,96},{96,128},{128,160},{160,192},{192,224},{224... | collective-permute-start | bytes 98312 | tf_op jit(solution)/shard_map/ppermute | solution.py:322
  6.7 0.0 copy-done.10
  6.7 0.0 copy-done.11
  6.7 0.0 copy-start.5
  6.7 0.0 copy-done.6
  6.7 0.7 copy-done.5
  7.3 0.0 copy-start.1
  7.3 0.0 copy-start.9
  7.4 5.1 %shard_map.140 = (bf16[7,256,256]{2,1,0:T(8,128)(2,1)S(1)}, bf16[7,256,128]{2,1,0:T(8,128)(2,1)S(1)}, bf16[7,256,128]{2,1,0:T(8,128)(2,1)S(1)}, f32[7,128,128]{2...) custom-call(bf16[1,256,896]{2,1,0:T(8,128)(2,1)S(1)} %copy-done.6, f32[1,7,256]{2,1,0:T(8,128)S(1)} %copy.18.beta, ...), custom_call_target="tpu_custom_call" | custom-call | flops 4000000000 | tf_op jit(solution)/shard_map/pallas_call | solution.py:37
  12.4 0.0 collective-permute-done.rim
  12.4 0.0 copy-done.1
  12.4 0.0 copy-done.9
  12.4 2.1 %shard_map.141 = (bf16[14,128,128]{2,1,0:T(8,128)(2,1)S(1)}, bf16[7,256,128]{2,1,0:T(8,128)(2,1)S(1)}) custom-call(bf16[1,256,896]{2,1,0:T(8,128)(2,1)S(1)} %copy-done.1, bf16[16,1024]{1,0:T(8,128)(2,1)S(1)} %collective-permute-done.rim, f32[1,7,4,256]{3,2,1,0:T(4,128)S(1)} %copy-done.9, s32[1,256]{1,0:T(1,128)S(1)} %copy-done.5, ...), custom_call_target="tpu_custom_call" | custom-call | flops 2000000000 | tf_op jit(solution)/shard_map/pallas_call | solution.py:37
  14.6 1.5 %collective-permute-start.1 = (bf16[14,128,128]{2,1,0:T(8,128)(2,1)S(1)}, bf16[14,128,128]{2,1,0:T(8,128)(2,1)S(1)}, u32[]{:S(2)}, u32[]{:S(2)}) collective-permute-start(bf16[14,128,128]{2,1,0:T(8,128)(2,1)S(1)} %get-tuple-element.26.own), channel_id=1, source_target_pairs={{0,32},{32,0},{64,96},{96,64},{128,160},{160,128},{192,224},{224,1... | collective-permute-start | bytes 1376264 | tf_op jit(solution)/shard_map/ppermute | solution.py:325
  16.1 0.0 copy-start.12
  16.1 0.0 copy-start.7
  16.1 0.0 collective-permute-start.4
  16.1 3.1 %collective-permute-start.5 = (bf16[528,128]{1,0:T(8,128)(2,1)S(1)}, bf16[528,128]{1,0:T(8,128)(2,1)S(1)}, u32[]{:S(2)}, u32[]{:S(2)}) collective-permute-start(bf16[528,128]{1,0:T(8,128)(2,1)S(1)} %get-tuple-element.35.own), channel_id=1, source_target_pairs={{0,128},{32,160},{64,192},{96,224},{128,0},{160,32},{192,64},{224,... | collective-permute-start | bytes 405512 | tf_op jit(solution)/shard_map/ppermute | solution.py:322
  19.2 0.0 collective-permute-done.1.other
  19.2 0.3 shard_map.142
  19.5 0.0 copy-start.13
  19.5 0.3 collective-permute-start.2
  19.8 0.9 %collective-permute-start.6 = (bf16[528,128]{1,0:T(8,128)(2,1)S(1)}, bf16[528,128]{1,0:T(8,128)(2,1)S(1)}, u32[]{:S(2)}, u32[]{:S(2)}) collective-permute-start(bf16[528,128]{1,0:T(8,128)(2,1)S(1)} %get-tuple-element.35.own), channel_id=1, source_target_pairs={{0,32},{32,0},{64,96},{96,64},{128,160},{160,128},{192,224},{224,1... | collective-permute-start | bytes 405512 | tf_op jit(solution)/shard_map/ppermute | solution.py:325
  20.7 0.0 copy-done.12
  20.7 0.0 copy-done.13
  20.7 1.8 %collective-permute-done.4.r2 = bf16[528,128]{1,0:T(8,128)(2,1)S(1)} collective-permute-done((bf16[528,128]{1,0:T(8,128)(2,1)S(1)}, bf16[528,128]{1,0:T(8,128)(2,1)S(1)}, u32[]{:S(2)}, u32[]{:S(2)}) %collective-permute-start.4) | collective-permute-done | bytes 135200 | tf_op jit(solution)/shard_map/ppermute | solution.py:322
  22.5 1.3 %collective-permute-start.7 = (bf16[528,128]{1,0:T(8,128)(2,1)S(1)}, bf16[528,128]{1,0:T(8,128)(2,1)S(1)}, u32[]{:S(2)}, u32[]{:S(2)}) collective-permute-start(bf16[528,128]{1,0:T(8,128)(2,1)S(1)} %collective-permute-done.4.r2), channel_id=1, source_target_pairs={{0,32},{32,0},{64,96},{96,64},{128,160},{160,128},{192,224},{224,1... | collective-permute-start | bytes 405512 | tf_op jit(solution)/shard_map/ppermute | solution.py:325
  23.8 1.7 %collective-permute-done.5.r4 = bf16[528,128]{1,0:T(8,128)(2,1)S(1)} collective-permute-done((bf16[528,128]{1,0:T(8,128)(2,1)S(1)}, bf16[528,128]{1,0:T(8,128)(2,1)S(1)}, u32[]{:S(2)}, u32[]{:S(2)}) %collective-permute-start.5) | collective-permute-done | bytes 135200 | tf_op jit(solution)/shard_map/ppermute | solution.py:322
  25.4 2.1 %collective-permute-start.8 = (bf16[528,128]{1,0:T(8,128)(2,1)S(1)}, bf16[528,128]{1,0:T(8,128)(2,1)S(1)}, u32[]{:S(2)}, u32[]{:S(2)}) collective-permute-start(bf16[528,128]{1,0:T(8,128)(2,1)S(1)} %collective-permute-done.5.r4), channel_id=1, source_target_pairs={{0,32},{32,0},{64,96},{96,64},{128,160},{160,128},{192,224},{224,1... | collective-permute-start | bytes 405512 | tf_op jit(solution)/shard_map/ppermute | solution.py:325
  27.5 0.0 copy-done.7
  27.5 1.7 %shard_map.144 = (f32[7,256,128]{2,1,0:T(8,128)S(1)}, bf16[7,256,128]{2,1,0:T(8,128)(2,1)S(1)}, f32[256,128]{1,0:T(8,128)S(1)}) custom-call(bf16[1,256,896]{2,1,0:T(8,128)(2,1)S(1)} %copy-done.7, bf16[1,256,896]{2,1,0:T(8,128)(2,1)S(1)} %copy-done.6, bf16[16,1024]{1,0:T(8,128)(2,1)S(1)} %collective-permute-done.rim, s32[1,256]{1,0:T(1,128)S(1)} %copy-done.5, ...), custom_call_target="tpu_custom_call" | custom-call | flops 2000000000 | tf_op jit(solution)/shard_map/pallas_call | solution.py:37
  29.2 1.1 %collective-permute-done.2.arriving = bf16[7,128,128]{2,1,0:T(8,128)(2,1)S(1)} collective-permute-done((bf16[7,128,128]{2,1,0:T(8,128)(2,1)S(1)}, bf16[7,128,128]{2,1,0:T(8,128)(2,1)S(1)}, u32[]{:S(2)}, u32[]{:S(2)}) %collective-permute-start.2) | collective-permute-done | bytes 229408 | tf_op jit(solution)/shard_map/ppermute | solution.py:322
  30.3 0.0 copy-start.8
  30.3 0.2 shard_map.143
  30.5 0.1 collective-permute-start.3
  30.6 0.0 collective-permute-done.6.x0
  30.6 0.0 collective-permute-done.7.x2
  30.6 0.0 collective-permute-done.8.x4
  30.7 0.7 copy-done.8
  31.3 6.6 %shard_map.145 = (bf16[1,256,896]{2,1,0:T(8,128)(2,1)}, f32[256,896]{1,0:T(8,128)S(1)}) custom-call(bf16[1,256,896]{2,1,0:T(8,128)(2,1)S(1)} %copy-done.8, s32[1,256]{1,0:T(1,128)S(1)} %copy-done.5, bf16[528,128]{1,0:T(8,128)(2,1)S(1)} %get-tuple-element.35.own, bf16[528,128]{1,0:T(8,128)(2,1)S(1)} %collective-permute-done.4.r2, ...), custom_call_target="tpu_custom_call" | custom-call | flops 5000000000 | tf_op jit(solution)/shard_map/pallas_call | solution.py:37
  38.0 0.1 collective-permute-done.3.arriving
  38.1 1.8 %shard_map.146 = (bf16[1,256,896]{2,1,0:T(8,128)(2,1)}, f32[256,128]{1,0:T(8,128)S(1)}) custom-call(bf16[7,128,128]{2,1,0:T(8,128)(2,1)S(1)} %collective-permute-done.3.arriving, bf16[14,128,128]{2,1,0:T(8,128)(2,1)S(1)} %collective-permute-done.1.other, f32[7,256,128]{2,1,0:T(8,128)S(1)} %get-tuple-element.33.local, ...), custom_call_target="tpu_custom_call" | custom-call | flops 1000000000 | tf_op jit(solution)/shard_map/pallas_call | solution.py:37
  39.8 26.4 %all_to_all.12 = f32[256,1,128]{2,1,0:T(1,128)S(1)} all-to-all(f32[256,1,128]{2,1,0:T(1,128)S(1)} %bitcast.4), channel_id=1, replica_groups=mesh['ctx'=8,'head'=4,'dp'=8] {'ctx','head','dp'}, dimensions={0} | all-to-all | bytes 262144 | tf_op jit(solution)/shard_map/all_to_all | solution.py:436
  66.2 0.6 slice_reduce_fusion
  (5 shorter events, 0.0 us)
Async XLA Ops:
  0.6 1.0 %copy-start = (bf16[1,256,896]{2,1,0:T(8,128)(2,1)S(1)}, bf16[1,256,896]{2,1,0:T(8,128)(2,1)}, u32[]{:S(2)}) copy-start(bf16[1,256,896]{2,1,0:T(8,128)(2,1)} %v.1) | copy-start | bytes 1376260
  1.7 0.8 %copy-start.2 = (bf16[1,256,128]{2,1,0:T(8,128)(2,1)S(1)}, bf16[1,256,128]{2,1,0:T(8,128)(2,1)}, u32[]{:S(2)}) copy-start(bf16[1,256,128]{2,1,0:T(8,128)(2,1)} %tk.1) | copy-start | bytes 196612
  2.5 0.8 %copy-start.3 = (bf16[1,256,128]{2,1,0:T(8,128)(2,1)S(1)}, bf16[1,256,128]{2,1,0:T(8,128)(2,1)}, u32[]{:S(2)}) copy-start(bf16[1,256,128]{2,1,0:T(8,128)(2,1)} %tv.1) | copy-start | bytes 196612
  3.3 0.7 copy-start.4
  4.0 2.6 %copy-start.10 = (f32[1,7,256]{2,0,1:T(1,128)S(1)}, f32[1,7,256]{2,0,1:T(1,128)}, u32[]{:S(2)}) copy-start(f32[1,7,256]{2,0,1:T(1,128)} %param.15) | copy-start | bytes 21508
  4.0 2.7 %copy-start.6 = (bf16[1,256,896]{2,1,0:T(8,128)(2,1)S(1)}, bf16[1,256,896]{2,1,0:T(8,128)(2,1)}, u32[]{:S(2)}) copy-start(bf16[1,256,896]{2,1,0:T(8,128)(2,1)} %k.3) | copy-start | bytes 1376260
  4.0 2.6 %copy-start.11 = (f32[1,7,256]{2,0,1:T(1,128)S(1)}, f32[1,7,256]{2,0,1:T(1,128)}, u32[]{:S(2)}) copy-start(f32[1,7,256]{2,0,1:T(1,128)} %param.16) | copy-start | bytes 21508
  4.0 8.4 %collective-permute-start = (bf16[16,1024]{1,0:T(8,128)(2,1)S(1)}, bf16[16,1024]{1,0:T(8,128)(2,1)S(1)}, u32[]{:S(2)}, u32[]{:S(2)}) collective-permute-start(bf16[16,1024]{1,0:T(8,128)(2,1)S(1)} %get-tuple-element.22), channel_id=1, source_target_pairs={{0,32},{32,64},{64,96},{96,128},{128,160},{160,192},{192,224},{224... | collective-permute-start | bytes 98312 | tf_op jit(solution)/shard_map/ppermute | solution.py:322
  6.7 0.7 copy-start.5
  7.3 5.1 %copy-start.1 = (bf16[1,256,896]{2,1,0:T(8,128)(2,1)S(1)}, bf16[1,256,896]{2,1,0:T(8,128)(2,1)}, u32[]{:S(2)}) copy-start(bf16[1,256,896]{2,1,0:T(8,128)(2,1)} %v.1) | copy-start | bytes 1376260
  7.3 5.1 %copy-start.9 = (f32[1,7,4,256]{3,2,1,0:T(4,128)S(1)}, f32[1,7,4,256]{3,2,1,0:T(4,128)}, u32[]{:S(2)}) copy-start(f32[1,7,4,256]{3,2,1,0:T(4,128)} %taps.1) | copy-start | bytes 86020
  14.6 4.6 %collective-permute-start.1 = (bf16[14,128,128]{2,1,0:T(8,128)(2,1)S(1)}, bf16[14,128,128]{2,1,0:T(8,128)(2,1)S(1)}, u32[]{:S(2)}, u32[]{:S(2)}) collective-permute-start(bf16[14,128,128]{2,1,0:T(8,128)(2,1)S(1)} %get-tuple-element.26.own), channel_id=1, source_target_pairs={{0,32},{32,0},{64,96},{96,64},{128,160},{160,128},{192,224},{224,1... | collective-permute-start | bytes 1376264 | tf_op jit(solution)/shard_map/ppermute | solution.py:325
  16.1 4.6 %copy-start.12 = (f32[1,7,256]{2,0,1:T(1,128)S(1)}, f32[1,7,256]{2,0,1:T(1,128)}, u32[]{:S(2)}) copy-start(f32[1,7,256]{2,0,1:T(1,128)} %param.23) | copy-start | bytes 21508
  16.1 11.4 %copy-start.7 = (bf16[1,256,896]{2,1,0:T(8,128)(2,1)S(1)}, bf16[1,256,896]{2,1,0:T(8,128)(2,1)}, u32[]{:S(2)}) copy-start(bf16[1,256,896]{2,1,0:T(8,128)(2,1)} %q.2) | copy-start | bytes 1376260
  16.1 6.4 %collective-permute-start.4 = (bf16[528,128]{1,0:T(8,128)(2,1)S(1)}, bf16[528,128]{1,0:T(8,128)(2,1)S(1)}, u32[]{:S(2)}, u32[]{:S(2)}) collective-permute-start(bf16[528,128]{1,0:T(8,128)(2,1)S(1)} %get-tuple-element.35.own), channel_id=1, source_target_pairs={{0,64},{32,96},{64,128},{96,160},{128,192},{160,224},{192,0},{224,... | collective-permute-start | bytes 405512 | tf_op jit(solution)/shard_map/ppermute | solution.py:322
  16.1 9.3 %collective-permute-start.5 = (bf16[528,128]{1,0:T(8,128)(2,1)S(1)}, bf16[528,128]{1,0:T(8,128)(2,1)S(1)}, u32[]{:S(2)}, u32[]{:S(2)}) collective-permute-start(bf16[528,128]{1,0:T(8,128)(2,1)S(1)} %get-tuple-element.35.own), channel_id=1, source_target_pairs={{0,128},{32,160},{64,192},{96,224},{128,0},{160,32},{192,64},{224,... | collective-permute-start | bytes 405512 | tf_op jit(solution)/shard_map/ppermute | solution.py:322
  19.5 1.2 %copy-start.13 = (f32[896]{0:T(1024)S(1)}, f32[896]{0:T(1024)}, u32[]{:S(2)}) copy-start(f32[896]{0:T(1024)} %param.18) | copy-start | bytes 10756
  19.5 10.8 %collective-permute-start.2 = (bf16[7,128,128]{2,1,0:T(8,128)(2,1)S(1)}, bf16[7,128,128]{2,1,0:T(8,128)(2,1)S(1)}, u32[]{:S(2)}, u32[]{:S(2)}) collective-permute-start(bf16[7,128,128]{2,1,0:T(8,128)(2,1)S(1)} %get-tuple-element.28.i), channel_id=1, source_target_pairs={{0,64},{32,96},{64,128},{96,160},{128,192},{160,224},{192,0},{224,... | collective-permute-start | bytes 688136 | tf_op jit(solution)/shard_map/ppermute | solution.py:322
  19.8 10.9 %collective-permute-start.6 = (bf16[528,128]{1,0:T(8,128)(2,1)S(1)}, bf16[528,128]{1,0:T(8,128)(2,1)S(1)}, u32[]{:S(2)}, u32[]{:S(2)}) collective-permute-start(bf16[528,128]{1,0:T(8,128)(2,1)S(1)} %get-tuple-element.35.own), channel_id=1, source_target_pairs={{0,32},{32,0},{64,96},{96,64},{128,160},{160,128},{192,224},{224,1... | collective-permute-start | bytes 405512 | tf_op jit(solution)/shard_map/ppermute | solution.py:325
  22.5 8.2 %collective-permute-start.7 = (bf16[528,128]{1,0:T(8,128)(2,1)S(1)}, bf16[528,128]{1,0:T(8,128)(2,1)S(1)}, u32[]{:S(2)}, u32[]{:S(2)}) collective-permute-start(bf16[528,128]{1,0:T(8,128)(2,1)S(1)} %collective-permute-done.4.r2), channel_id=1, source_target_pairs={{0,32},{32,0},{64,96},{96,64},{128,160},{160,128},{192,224},{224,1... | collective-permute-start | bytes 405512 | tf_op jit(solution)/shard_map/ppermute | solution.py:325
  25.4 5.2 %collective-permute-start.8 = (bf16[528,128]{1,0:T(8,128)(2,1)S(1)}, bf16[528,128]{1,0:T(8,128)(2,1)S(1)}, u32[]{:S(2)}, u32[]{:S(2)}) collective-permute-start(bf16[528,128]{1,0:T(8,128)(2,1)S(1)} %collective-permute-done.5.r4), channel_id=1, source_target_pairs={{0,32},{32,0},{64,96},{96,64},{128,160},{160,128},{192,224},{224,1... | collective-permute-start | bytes 405512 | tf_op jit(solution)/shard_map/ppermute | solution.py:325
  30.3 1.0 %copy-start.8 = (bf16[1,256,896]{2,1,0:T(8,128)(2,1)S(1)}, bf16[1,256,896]{2,1,0:T(8,128)(2,1)}, u32[]{:S(2)}) copy-start(bf16[1,256,896]{2,1,0:T(8,128)(2,1)} %q.3) | copy-start | bytes 1376260
  30.5 7.5 %collective-permute-start.3 = (bf16[7,128,128]{2,1,0:T(8,128)(2,1)S(1)}, bf16[7,128,128]{2,1,0:T(8,128)(2,1)S(1)}, u32[]{:S(2)}, u32[]{:S(2)}) collective-permute-start(bf16[7,128,128]{2,1,0:T(8,128)(2,1)S(1)} %shard_map.143), channel_id=1, source_target_pairs={{0,64},{32,96},{64,128},{96,160},{128,192},{160,224},{192,0},{224,... | collective-permute-start | bytes 688136 | tf_op jit(solution)/shard_map/ppermute | solution.py:322

commit v2 on v1

--- a/solution.py
+++ b/solution.py
@@ -1,3 +1,4 @@
+import functools
 import math
 
 import jax
@@ -13,6 +14,7 @@
 F32 = jnp.float32
 BF16 = jnp.bfloat16
 VMEM_BYTES = 32 * 1024 * 1024
+PACK_VMEM = 62 * 1024 * 1024
 
 
 def nn(a, b, precision=None):
@@ -33,40 +35,57 @@
     return slice(h * HEAD, (h + 1) * HEAD)
 
 
-def call(body, outs, *args, scratch=(), flops=0):
+def call(body, outs, *args, scratch=(), hbm=(), flops=0, vmem=VMEM_BYTES):
+    buffers = [pltpu.VMEM(s, d) for s, d in scratch]
+    if hbm:
+        buffers.append(pltpu.SemaphoreType.DMA((len(hbm),)))
     return pl.pallas_call(
         body,
         out_shape=[jax.ShapeDtypeStruct(s, d) for s, d in outs],
-        in_specs=[pl.BlockSpec(memory_space=pltpu.VMEM)] * len(args),
+        in_specs=[
+            pl.BlockSpec(memory_space=pltpu.HBM if i in hbm else pltpu.VMEM)
+            for i in range(len(args))
+        ],
         out_specs=[pl.BlockSpec(memory_space=pltpu.VMEM)] * len(outs),
-        scratch_shapes=[pltpu.VMEM(s, d) for s, d in scratch],
-        compiler_params=pltpu.CompilerParams(vmem_limit_bytes=VMEM_BYTES),
+        scratch_shapes=buffers,
+        compiler_params=pltpu.CompilerParams(vmem_limit_bytes=vmem),
         cost_estimate=pl.CostEstimate(flops=flops, bytes_accessed=0, transcendentals=0),
     )(*args)
 
 
-def pack_body(tk, tv, sv, ids, kv, rim):
+def pack_body(tk, tv, sv, ids, kv, rim, id_s, sems):
     tokens = tk.shape[1]
-    kv[0:tokens] = tk[0]
-    kv[tokens : 2 * tokens] = tv[0]
-    idf = ids[...].astype(F32)
+    features = sv.shape[2]
+    moves = [
+        pltpu.make_async_copy(ids, id_s, sems.at[0]),
+        pltpu.make_async_copy(
+            sv.at[0, tokens - 16 : tokens, :], rim.at[:, 0:features], sems.at[1]
+        ),
+        pltpu.make_async_copy(tk.at[0], kv.at[0:tokens], sems.at[2]),
+        pltpu.make_async_copy(tv.at[0], kv.at[tokens : 2 * tokens], sems.at[3]),
+    ]
+    for move in moves:
+        move.start()
+    moves[0].wait()
+    idf = id_s[...].astype(F32)
     rows = lax.broadcasted_iota(jnp.int32, (16, 128), 0)
     block = jnp.zeros((16, 128), F32)
     for i in range(tokens // 128):
         block = jnp.where(rows == i, idf[:, i * 128 : (i + 1) * 128], block)
     kv[2 * tokens : 2 * tokens + 16] = block.astype(BF16)
-    features = sv.shape[2]
-    rim[:, 0:features] = sv[0, tokens - 16 : tokens, :]
     rim[:, features : features + 128] = jnp.broadcast_to(
         idf[:, tokens - 128 : tokens], (16, 128)
     ).astype(BF16)
-
-
-def keys_body(k, beta, decay, ids, t_out, uk_out, kend_out, m_out, rows_out, cols_out, eight, a_s, t_s):
+    for move in moves[1:]:
+        move.wait()
+
+
+def keys_body(k, beta, decay, ids, t_out, uk_out, kend_out, m_out, rows_out, cols_out, eight, a_s, t_s, id_s, sems):
     tokens = k.shape[1]
-    heads = beta.shape[1]
+    heads = beta.shape[0]
     half = tokens // 2
-    idf = ids[...].astype(F32)
+    names = pltpu.make_async_copy(ids, id_s, sems.at[0])
+    names.start()
     lane = lax.broadcasted_iota(jnp.int32, (tokens, 128), 1)
     packed = jnp.zeros((tokens, 128), F32)
     for h in range(heads):
@@ -74,9 +93,12 @@
         norm = lax.rsqrt(jnp.sum(kf * kf, axis=1, keepdims=True) + EPSILON)
         packed = jnp.where(lane == h, norm, packed)
     r8 = packed.T[0:8]
+    names.wait()
+    idf = id_s[...].astype(F32)
     eight[...] = jnp.zeros_like(eight)
-    eight[0, 0:heads] = decay[0]
-    eight[1, 0:heads] = beta[0]
+    for h in range(heads):
+        eight[0, h : h + 1] = decay[h]
+        eight[1, h : h + 1] = beta[h]
     row_index = lax.broadcasted_iota(jnp.int32, (tokens, tokens), 0)
     col_index = lax.broadcasted_iota(jnp.int32, (tokens, tokens), 1)
     upto = jnp.where(row_index <= col_index, 1.0, 0.0)
@@ -92,7 +114,7 @@
         * br8
     )
     ids8 = jnp.broadcast_to(idf, (8, tokens))
-    rows_out[...] = jnp.concatenate([run8, br8], axis=0)
+    rows_out[...] = jnp.concatenate([run8, br8, ids8], axis=0)
     stacked = jnp.concatenate(
         [run8, wend8, fs8 * r8, fs8, ids8, r8, jnp.zeros((80, tokens), F32)], axis=0
     )
@@ -145,16 +167,16 @@
         kend = (cols[:, 8 + h : 9 + h] * kf).astype(BF16)
         kend_out[h] = kend
         scale = fs8[h : h + 1, tokens - 1 : tokens]
-        m_out[h] = jnp.where(er == ec, scale, 0.0) - tn(kend, uk)
-
-
-def values_body(v, rim, taps, ids, t, kend, m, mi_out, uv_out, x_s, tap_s):
+        m_out[h] = jnp.where(er == ec, scale, 0.0) - tn(uk, kend)
+
+
+def values_body(v, rim, taps, rows, t, kend, m, after, afters, mi_out, uv_out, x_s, tap_s):
     tokens = v.shape[1]
     features = v.shape[2]
     heads = taps.shape[1]
     count = taps.shape[2]
     first = lax.axis_index("ctx") == 0
-    idf = ids[...].astype(F32)
+    idf = rows[16:17]
     before = rim[0:1, features : features + 128].astype(F32)
     before = jnp.where(first, -1.0, before)
     longer = jnp.concatenate([before, idf], axis=1)
@@ -178,15 +200,15 @@
         uv = nn(t[h], values.astype(BF16)).astype(BF16)
         uv_out[h] = uv
         mi_out[h] = (joined * m[h]).astype(BF16)
-        mi_out[heads + h] = tn(kend[h], uv).astype(BF16)
-
-
-def queries_body(q, k, rim, ids, rows, cols_in, uk, uv, lw, local_out, reader_out, lw_out, lw_s):
+        mi_out[heads + h] = tn(uv, kend[h]).astype(BF16)
+
+
+def queries_body(q, k, rim, rows, cols_in, uk, uv, lw, local_out, reader_out, lw_out, lw_s):
     tokens = q.shape[1]
     features = q.shape[2]
     heads = uk.shape[0]
     first = lax.axis_index("ctx") == 0
-    idf = ids[...].astype(F32)
+    idf = rows[16:17]
     before = jnp.where(first, -1.0, rim[0:1, features : features + 128].astype(F32))
     joined = jnp.where(before[0:1, 127:128] == idf[:, 0:1], 1.0, 0.0)
     row_index = lax.broadcasted_iota(jnp.int32, (tokens, tokens), 0)
@@ -194,7 +216,8 @@
     cols = cols_in[...]
     visible = (col_index <= row_index) & (cols[:, 32:33] == idf)
     lw_s[...] = jnp.zeros_like(lw_s)
-    lw_s[0:heads] = lw[0]
+    for h in range(heads):
+        lw_s[h : h + 1] = lw[h]
     lw_out[...] = lw_s[...].T
     for h in range(heads):
         qh = q[0, :, head_lanes(h)]
@@ -209,14 +232,14 @@
         reader_out[h] = (joined * reader).astype(BF16)
 
 
-def teacher_body(q, ids, own, r2, r4, x0, x2, x4, out, full, k_s, v_s, id_s, bias_s):
+def teacher_body(first_head, last_head, q, cols_in, own, r2, r4, x0, x2, x4, *refs):
+    out, full, k_s, v_s, id_s, bias_s = refs[-6:]
+    if first_head:
+        out[0, :, 0 : first_head * HEAD] = refs[0][0, :, 0 : first_head * HEAD]
     tokens = q.shape[1]
-    heads = q.shape[2] // HEAD
     halves = tokens // 128
     index = lax.axis_index("ctx")
     odd = lax.rem(index, 2) == 1
-    idf = ids[...].astype(F32)
-
     def place(slot, source):
         k_s[slot * tokens : (slot + 1) * tokens] = source[0:tokens]
         v_s[slot * tokens : (slot + 1) * tokens] = source[tokens : 2 * tokens]
@@ -242,58 +265,65 @@
         place(3, x2)
 
     width = 5 * tokens
-    id_col = jnp.broadcast_to(idf, (128, tokens)).T[:, 0:1]
+    id_col = cols_in[:, 32:33]
     same = id_col == id_s[...]
     row_index = lax.broadcasted_iota(jnp.int32, (tokens, width), 0)
     col_index = lax.broadcasted_iota(jnp.int32, (tokens, width), 1) - 4 * tokens
     bias_s[...] = jnp.where(same & (col_index <= row_index), 0.0, MASKED)
     scale = math.log2(math.e) / math.sqrt(HEAD)
     span = width - (halves - 1) * 128
-    for h in range(heads):
+    for h in range(first_head, last_head):
+        at = head_lanes(h - first_head)
         for r in range(halves):
-            qt = q[0, r * 128 : (r + 1) * 128, head_lanes(h)]
-            s = nt(qt, k_s[r * 128 : r * 128 + span])
-            s = s * scale + bias_s[r * 128 : (r + 1) * 128, r * 128 : r * 128 + span]
+            rows = slice(r * 128, (r + 1) * 128)
+            cols = slice(r * 128, r * 128 + span)
+            s = nt(q[0, rows, head_lanes(h)], k_s[cols])
+            s = s * scale + bias_s[rows, cols]
             largest = jnp.max(s, axis=1, keepdims=True)
             w = jnp.exp2(s - largest)
             total = jnp.sum(w, axis=1, keepdims=True)
-            o = nn(w.astype(BF16), v_s[r * 128 : r * 128 + span]) / total
-            full[r * 128 : (r + 1) * 128, head_lanes(h)] = o
-            out[0, r * 128 : (r + 1) * 128, head_lanes(h)] = o.astype(BF16)
-
-
-def chip_body(own, other, m_out, i_out):
-    heads = m_out.shape[0]
-    odd = lax.rem(lax.axis_index("ctx"), 2) == 1
-    for h in range(heads):
-        m_own, m_other = own[h], other[h]
-        i_own, i_other = own[heads + h], other[heads + h]
-        later_m = jnp.where(odd, m_own, m_other)
-        later_i = jnp.where(odd, i_own, i_other)
-        early_m = jnp.where(odd, m_other, m_own)
-        early_i = jnp.where(odd, i_other, i_own)
-        m_out[h] = nn(later_m, early_m).astype(BF16)
-        i_out[h] = (nn(later_m, early_i) + later_i.astype(F32)).astype(BF16)
-
-
-def join_body(m, i, arriving, out):
+            o = nn(w.astype(BF16), v_s[cols]) / total
+            full[rows, at] = o
+            out[0, rows, head_lanes(h)] = o.astype(BF16)
+
+
+def is_odd():
+    return lax.rem(lax.axis_index("ctx"), 2) == 1
+
+
+def chip_body(own, other, after, arrived, m_out, i_out):
+    heads, rows, _ = i_out.shape
+    odd = is_odd()
+    for h in range(heads):
+        later_m = jnp.where(odd, own[h], other[h])
+        early_m = jnp.where(odd, other[h], own[h])
+        later_i = jnp.where(odd, own[heads + h, rows:], other[heads + h, 0:rows])
+        early_i = jnp.where(odd, other[heads + h, rows:], own[heads + h, 0:rows])
+        m_out[h] = nn(early_m, later_m).astype(BF16)
+        i_out[h] = (nn(early_i, later_m) + later_i.astype(F32)).astype(BF16)
+
+
+def join_body(m, i, arriving, after, out):
     for h in range(m.shape[0]):
-        out[h] = (nn(m[h], arriving[h]) + i[h].astype(F32)).astype(BF16)
-
-
-def finish_body(arriving, other, local, reader, gain, teacher, lw, out, sums):
-    heads = arriving.shape[0]
-    odd = lax.rem(lax.axis_index("ctx"), 2) == 1
-    total = jnp.zeros(teacher[:, 0:HEAD].shape, F32)
-    for h in range(heads):
-        s = arriving[h]
-        stepped = (nn(other[h], s) + other[heads + h].astype(F32)).astype(BF16)
+        out[h] = (nn(arriving[h], m[h]) + i[h].astype(F32)).astype(BF16)
+
+
+def finish_body(mine, theirs, other, local, reader, gain, teacher_a, teacher_b, lw, out, sums):
+    heads = mine.shape[0]
+    odd = is_odd()
+    split = teacher_a.shape[1] // HEAD
+    total = jnp.zeros(lw.shape, F32)
+    for h in range(heads):
+        a, b = mine[h], theirs[h]
+        s = jnp.concatenate([jnp.where(odd, b, a), jnp.where(odd, a, b)], axis=0)
+        stepped = (nn(s, other[h]) + other[heads + h].astype(F32)).astype(BF16)
         s = jnp.where(odd, stepped, s)
-        o = local[h] + nn(reader[h], s)
+        o = local[h] + nt(reader[h], s)
         mean = jnp.sum(o * o, axis=1, keepdims=True) * (1.0 / HEAD)
         student = o * lax.rsqrt(mean + EPSILON) * gain[:, head_lanes(h)]
         out[0, :, head_lanes(h)] = student.astype(BF16)
-        difference = student - teacher[:, head_lanes(h)]
+        teacher = teacher_a[:, head_lanes(h)] if h < split else teacher_b[:, head_lanes(h - split)]
+        difference = student - teacher
         total = total + lw[:, h : h + 1] * (difference * difference)
     partial = jnp.sum(jnp.sum(total, axis=0, keepdims=True), axis=1, keepdims=True)
     sums[...] = jnp.broadcast_to(partial, sums.shape)
@@ -324,6 +354,13 @@
     def swapped(block):
         return lax.ppermute(block, "ctx", [(i, i ^ 1) for i in range(shards)])
 
+    def by_head(block):
+        return block.reshape(heads, 1, tokens)
+
+    def crossed(block):
+        route = [(i, ((i + 2) % shards) ^ 1) for i in range(shards)]
+        return lax.ppermute(block, "ctx", route)
+
     kv, rim = call(
         pack_body,
         [((2 * tokens + 16, HEAD), BF16), ((16, features + 128), BF16)],
@@ -331,10 +368,13 @@
         teacher_v,
         student_v,
         segment_ids,
+        scratch=[((1, tokens), jnp.int32)],
+        hbm=(0, 1, 2, 3),
+        vmem=PACK_VMEM,
     )
     rim = rotated(rim, 1)
     r2 = rotated(kv, 2)
-    r4 = rotated(kv, 4)
+    x0 = swapped(kv)
     t, uk, kend, m0, rows, cols = call(
         keys_body,
         [
@@ -342,34 +382,40 @@
             ((heads, tokens, HEAD), BF16),
             ((heads, tokens, HEAD), BF16),
             ((heads, HEAD, HEAD), F32),
-            ((16, tokens), F32),
+            ((24, tokens), F32),
             ((tokens, 128), F32),
         ],
         student_k,
-        beta,
-        log_decay,
+        by_head(beta),
+        by_head(log_decay),
         segment_ids,
         scratch=[
             ((2, 8, tokens), F32),
             ((heads, tokens, tokens), BF16),
             ((2 * heads, tokens // 2, tokens // 2), F32),
+            ((1, tokens), jnp.int32),
         ],
-        flops=4 * 10**9,
-    )
+        hbm=(3,),
+        flops=5 * 10**8,
+    )
+    r4 = rotated(kv, 4)
     mi, uv = call(
         values_body,
         [((2 * heads, HEAD, HEAD), BF16), ((heads, tokens, HEAD), BF16)],
         student_v,
         rim,
         kernel,
-        segment_ids,
+        rows,
         t,
         kend,
         m0,
+        r2,
+        r4,
         scratch=[((8 + tokens, features), F32), ((128, tokens), F32)],
-        flops=2 * 10**9,
+        flops=2 * 10**8,
     )
     mi_other = swapped(mi)
+    x2 = swapped(r2)
     local, reader, lw = call(
         queries_body,
         [
@@ -380,58 +426,67 @@
         student_q,
         student_k,
         rim,
-        segment_ids,
         rows,
         cols,
         uk,
         uv,
-        loss_weight,
+        by_head(loss_weight),
         scratch=[((128, tokens), F32)],
-        flops=2 * 10**9,
-    )
-    x0, x2, x4 = swapped(kv), swapped(r2), swapped(r4)
+        flops=2 * 10**8,
+    )
     m_chip, i_chip = call(
         chip_body,
-        [((heads, HEAD, HEAD), BF16), ((heads, HEAD, HEAD), BF16)],
+        [((heads, HEAD, HEAD), BF16), ((heads, HEAD // 2, HEAD), BF16)],
         mi,
         mi_other,
-        flops=10**8,
+        lw,
+        r4,
     )
     behind = rotated(i_chip, 2)
-    teacher_out, teacher = call(
-        teacher_body,
-        [((1, tokens, features), BF16), ((tokens, features), F32)],
-        teacher_q,
-        segment_ids,
-        kv,
-        r2,
-        r4,
-        x0,
-        x2,
-        x4,
-        scratch=[
-            ((5 * tokens, HEAD), BF16),
-            ((5 * tokens, HEAD), BF16),
-            ((1, 5 * tokens), F32),
-            ((tokens, 5 * tokens), F32),
-        ],
-        flops=5 * 10**9,
-    )
+    x4 = swapped(r4)
+
+    def attend(first_head, last_head, *earlier):
+        count = last_head - first_head
+        return call(
+            functools.partial(teacher_body, first_head, last_head),
+            [((1, tokens, features), BF16), ((tokens, count * HEAD), F32)],
+            teacher_q,
+            cols,
+            kv,
+            r2,
+            r4,
+            x0,
+            x2,
+            x4,
+            *earlier,
+            flops=count * 10**8,
+            scratch=[
+                ((5 * tokens, HEAD), BF16),
+                ((5 * tokens, HEAD), BF16),
+                ((1, 5 * tokens), F32),
+                ((tokens, 5 * tokens), F32),
+            ],
+        )
+
+    teacher_out, teacher_a = attend(0, 3)
     (joined,) = call(
-        join_body, [((heads, HEAD, HEAD), BF16)], m_chip, i_chip, behind, flops=10**8
-    )
-    arriving = rotated(joined, 2)
+        join_body, [((heads, HEAD // 2, HEAD), BF16)], m_chip, i_chip, behind, teacher_a
+    )
+    mine = rotated(joined, 2)
+    theirs = crossed(joined)
+    teacher_out, teacher_b = attend(3, heads, teacher_out)
     student_out, sums = call(
         finish_body,
         [((1, tokens, features), BF16), ((everyone, 128), F32)],
-        arriving,
+        mine,
+        theirs,
         mi_other,
         local,
         reader,
         out_gain.reshape(1, features),
-        teacher,
+        teacher_a,
+        teacher_b,
         lw,
-        flops=10**9,
     )
     gathered = lax.all_to_all(sums, ("ctx", "head", "dp"), 0, 0, tiled=True)
     loss = jnp.sum(gathered[:, 0]) / (everyone * heads * tokens * HEAD)

time: 69 us -> 65.2 us (0.945)
  local copies, waits for them, and re-layouts: 4.75 us -> 1.08 us
  Pallas kernels: 17.8 us -> 20.4 us
  starting transfers between devices: 11.8 us -> 9.53 us
  blocking collectives: 26.4 us -> 24.7 us
  waiting for transfers between devices: 4.62 us -> 6.05 us
    ppermute x4, starting transfers between devices: 5.78 us -> 1.11 us  [swapped(): return lax.ppermute(block, 'ctx', [(i, i ^ 1) for i in range(shards)])]
    unnamed x31 -> x22, local copies, waits for them, and re-layouts: 4.75 us -> 1.08 us
    pallas_call x8 -> x9, Pallas kernels: 17.8 us -> 20.4 us  [call(): pl.pallas_call(body, out_shape=[jax.ShapeDtypeStruct(s, d) for s, d in ou...]
    ppermute x5, starting transfers between devices: 6.06 us -> 8.34 us  [rotated(): lax.ppermute(block, 'ctx', [(i, (i + distance) % shards) for i in range(s...]
    all_to_all x1, blocking collectives: 26.4 us -> 24.7 us  [on_device(): gathered = lax.all_to_all(sums, ('ctx', 'head', 'dp'), 0, 0, tiled=True)]
    ppermute x0 -> x1, waiting for transfers between devices: none -> 0.85 us  [crossed(): return lax.ppermute(block, 'ctx', route)]
  transfers between devices with their start and end apart: 9 -> 10, of which waited for: 4 -> 3; matrix products, arithmetic and copies ran while one was open for 0% -> 0% of each run, Pallas kernels for 20% -> 22%
where the time goes in v2:
time: 65.2 us; the launch traced here: 65 us
  blocking collectives  24.7 us (38%)
  Pallas kernels  20.4 us (31%)
  starting transfers between devices  9.53 us (15%)
  waiting for transfers between devices  6.05 us (9%)
  between operations  2.59 us (4%)
  local copies, waits for them, and re-layouts  1.08 us (2%)
    all_to_all x1, blocking collectives, on_device(): gathered = lax.all_to_all(sums, ('ctx', 'head', 'dp'), 0, 0, tiled=True)  24.7 us
    pallas_call x9, Pallas kernels, call(): pl.pallas_call(body, out_shape=[jax.ShapeDtypeStruct(s, d) for s, d in ou...  20.4 us
    ppermute x5, starting transfers between devices, rotated(): lax.ppermute(block, 'ctx', [(i, (i + distance) % shards) for i in range(s...  8.34 us
    ppermute x5, waiting for transfers between devices, rotated(): lax.ppermute(block, 'ctx', [(i, (i + distance) % shards) for i in range(s...  5.19 us
  transfers between devices with their start and end apart: 10, of which 3 were waited for; matrix products, arithmetic and copies ran while one was open for 0% of the time, Pallas kernels for 22%

profile of v2, /device:TPU:1, one launch (start us, length us, event | category | flops | bytes accessed | tf_op | source)
XLA Modules:
  0.0 65.0 jit_solution(14283630602203214445)
XLA Ops:
  0.6 0.0 copy-start.3
  0.6 0.0 copy-start.8
  0.7 0.0 copy-start.9
  0.7 1.7 %shard_map.139 = (bf16[528,128]{1,0:T(8,128)(2,1)}, bf16[16,1024]{1,0:T(8,128)(2,1)}) custom-call(bf16[1,256,128]{2,1,0:T(8,128)(2,1)} %tk.1, bf16[1,256,128]{2,1,0:T(8,128)(2,1)} %tv.1, bf16[1,256,896]{2,1,0:T(8,128)(2,1)} %v.1, s32[1,256]{1,0:T(1,128)} %ids.3), custom_call_target="tpu_custom_call" | custom-call | tf_op jit(solution)/shard_map/pallas_call | solution.py:42
  2.3 3.7 %collective-permute-start.2 = (bf16[528,128]{1,0:T(8,128)(2,1)}, bf16[528,128]{1,0:T(8,128)(2,1)S(1)}, u32[]{:S(2)}, u32[]{:S(2)}) collective-permute-start(bf16[528,128]{1,0:T(8,128)(2,1)} %get-tuple-element.29.own), channel_id=1, source_target_pairs={{0,128},{32,160},{64,192},{96,224},{128,0},{160,32},{192,64},{224,... | collective-permute-start | bytes 405512 | tf_op jit(solution)/shard_map/ppermute | solution.py:352
  6.0 0.3 collective-permute-start.1
  6.3 2.4 %collective-permute-start = (bf16[16,1024]{1,0:T(8,128)(2,1)}, bf16[16,1024]{1,0:T(8,128)(2,1)S(1)}, u32[]{:S(2)}, u32[]{:S(2)}) collective-permute-start(bf16[16,1024]{1,0:T(8,128)(2,1)} %get-tuple-element.24), channel_id=1, source_target_pairs={{0,32},{32,64},{64,96},{96,128},{128,160},{160,192},{192,224},{224... | collective-permute-start | bytes 98312 | tf_op jit(solution)/shard_map/ppermute | solution.py:352
  8.7 0.0 copy-start.7
  8.7 0.0 copy-done.3
  8.7 0.0 copy-done.8
  8.8 0.0 copy-done.9
  8.8 0.7 %copy-done.7 = s32[1,256]{1,0:T(1,128)S(1)} copy-done((s32[1,256]{1,0:T(1,128)S(1)}, s32[1,256]{1,0:T(1,128)}, u32[]{:S(2)}) %copy-start.7) | copy-done | bytes 1048
  9.4 0.0 copy-start.1
  9.4 0.0 copy-start.5
  9.4 5.5 %shard_map.140 = (bf16[7,256,256]{2,1,0:T(8,128)(2,1)S(1)}, bf16[7,256,128]{2,1,0:T(8,128)(2,1)S(1)}, bf16[7,256,128]{2,1,0:T(8,128)(2,1)S(1)}, f32[7,128,128]{2...) custom-call(bf16[1,256,896]{2,1,0:T(8,128)(2,1)S(1)} %copy-done.3, f32[7,1,256]{2,1,0:T(1,128)S(1)} %bitcast.9, ...), custom_call_target="tpu_custom_call" | custom-call | flops 500000000 | tf_op jit(solution)/shard_map/pallas_call | solution.py:42
  15.0 0.0 collective-permute-done.rim
  15.0 0.0 collective-permute-done.2.afters.arrived.r4
  15.0 0.0 collective-permute-done.1.after.r2
  15.0 0.0 copy-done.1
  15.0 0.0 copy-done.5
  15.0 0.0 copy-start.2
  15.0 0.0 copy-start.4
  15.0 2.5 %shard_map.141 = (bf16[14,128,128]{2,1,0:T(8,128)(2,1)S(1)}, bf16[7,256,128]{2,1,0:T(8,128)(2,1)S(1)}) custom-call(bf16[1,256,896]{2,1,0:T(8,128)(2,1)S(1)} %copy-done.1, bf16[16,1024]{1,0:T(8,128)(2,1)S(1)} %collective-permute-done.rim, f32[1,7,4,256]{3,2,1,0:T(4,128)S(1)} %copy-done.5, f32[24,256]{1,0:T(8,128)S(1)} %get-tuple-element.25.rows, ...), custom_call_target="tpu_custom_call" | custom-call | flops 200000000 | tf_op jit(solution)/shard_map/pallas_call | solution.py:42
  17.5 0.0 copy-start.6
  17.5 0.3 collective-permute-start.3
  17.8 0.0 copy-done.2
  17.8 0.3 collective-permute-start.5
  18.1 0.2 collective-permute-start.7
  18.3 0.3 collective-permute-start.6
  18.6 0.0 copy-done.4
  18.7 0.0 copy-done.6
  18.7 1.7 %shard_map.142 = (f32[7,256,128]{2,1,0:T(8,128)S(1)}, bf16[7,256,128]{2,1,0:T(8,128)(2,1)S(1)}, f32[256,128]{1,0:T(8,128)S(1)}) custom-call(bf16[1,256,896]{2,1,0:T(8,128)(2,1)S(1)} %copy-done.4, bf16[1,256,896]{2,1,0:T(8,128)(2,1)S(1)} %copy-done.3, bf16[16,1024]{1,0:T(8,128)(2,1)S(1)} %collective-permute-done.rim, f32[24,256]{1,0:T(8,128)S(1)} %get-tuple-element.25.rows, ...), custom_call_target="tpu_custom_call" | custom-call | flops 200000000 | tf_op jit(solution)/shard_map/pallas_call | solution.py:42
  20.3 0.0 collective-permute-done.3.other
  20.4 0.0 copy-start
  20.4 0.3 shard_map.143
  20.7 0.3 collective-permute-start.4
  21.0 0.0 collective-permute-done.5.x0
  21.0 0.0 collective-permute-done.7.x4
  21.0 0.0 collective-permute-done.6.x2
  21.0 0.4 copy-done
  21.4 2.6 %shard_map.144 = (bf16[1,256,896]{2,1,0:T(8,128)(2,1)S(1)}, f32[256,384]{1,0:T(8,128)S(1)}) custom-call(bf16[1,256,896]{2,1,0:T(8,128)(2,1)S(1)} %copy-done, f32[256,128]{1,0:T(8,128)S(1)} %get-tuple-element.31.cols_in, bf16[528,128]{1,0:T(8,128)(2,1)S(1)} %copy-done.2, bf16[528,128]{1,0:T(8,128)(2,1)S(1)} %collective-permute-done.1.after.r2, ...), custom_call_target="tpu_custom_call" | custom-call | flops 300000000 | tf_op jit(solution)/shard_map/pallas_call | solution.py:42
  24.0 2.7 %collective-permute-done.4.arriving = bf16[7,64,128]{2,1,0:T(8,128)(2,1)S(1)} collective-permute-done((bf16[7,64,128]{2,1,0:T(8,128)(2,1)S(1)}, bf16[7,64,128]{2,1,0:T(8,128)(2,1)S(1)}, u32[]{:S(2)}, u32[]{:S(2)}) %collective-permute-start.4) | collective-permute-done | bytes 114720 | tf_op jit(solution)/shard_map/ppermute | solution.py:352
  26.7 0.0 copy-start.10
  26.7 0.2 shard_map.145
  26.9 0.1 collective-permute-start.9
  27.0 1.6 %collective-permute-start.8 = (bf16[7,64,128]{2,1,0:T(8,128)(2,1)S(1)}, bf16[7,64,128]{2,1,0:T(8,128)(2,1)S(1)}, u32[]{:S(2)}, u32[]{:S(2)}) collective-permute-start(bf16[7,64,128]{2,1,0:T(8,128)(2,1)S(1)} %shard_map.145), channel_id=1, source_target_pairs={{0,64},{32,96},{64,128},{96,160},{128,192},{160,224},{192,0},{224,... | collective-permute-start | bytes 344072 | tf_op jit(solution)/shard_map/ppermute | solution.py:352
  28.6 0.0 copy-done.10
  28.6 4.2 %shard_map.146 = (bf16[1,256,896]{2,1,0:T(8,128)(2,1)}, f32[256,512]{1,0:T(8,128)S(1)}) custom-call(bf16[1,256,896]{2,1,0:T(8,128)(2,1)S(1)} %copy-done, f32[256,128]{1,0:T(8,128)S(1)} %get-tuple-element.31.cols_in, bf16[528,128]{1,0:T(8,128)(2,1)S(1)} %copy-done.2, bf16[528,128]{1,0:T(8,128)(2,1)S(1)} %collective-permute-done.1.after.r2, ...), custom_call_target="tpu_custom_call" | custom-call | flops 400000000 | tf_op jit(solution)/shard_map/pallas_call | solution.py:42
  32.8 0.9 %collective-permute-done.9.theirs = bf16[7,64,128]{2,1,0:T(8,128)(2,1)S(1)} collective-permute-done((bf16[7,64,128]{2,1,0:T(8,128)(2,1)S(1)}, bf16[7,64,128]{2,1,0:T(8,128)(2,1)S(1)}, u32[]{:S(2)}, u32[]{:S(2)}) %collective-permute-start.9) | collective-permute-done | bytes 114720 | tf_op jit(solution)/shard_map/ppermute | solution.py:362
  33.6 2.5 %collective-permute-done.8.mine = bf16[7,64,128]{2,1,0:T(8,128)(2,1)S(1)} collective-permute-done((bf16[7,64,128]{2,1,0:T(8,128)(2,1)S(1)}, bf16[7,64,128]{2,1,0:T(8,128)(2,1)S(1)}, u32[]{:S(2)}, u32[]{:S(2)}) %collective-permute-start.8) | collective-permute-done | bytes 114720 | tf_op jit(solution)/shard_map/ppermute | solution.py:352
  36.1 1.8 %shard_map.147 = (bf16[1,256,896]{2,1,0:T(8,128)(2,1)}, f32[256,128]{1,0:T(8,128)S(1)}) custom-call(bf16[7,64,128]{2,1,0:T(8,128)(2,1)S(1)} %collective-permute-done.8.mine, bf16[7,64,128]{2,1,0:T(8,128)(2,1)S(1)} %collective-permute-done.9.theirs, bf16[14,128,128]{2,1,0:T(8,128)(2,1)S(1)} %collective-permute-done.3.other, ...), custom_call_target="tpu_custom_call" | custom-call | tf_op jit(solution)/shard_map/pallas_call | solution.py:42
  37.9 24.7 %all_to_all.12 = f32[256,1,128]{2,1,0:T(1,128)S(1)} all-to-all(f32[256,1,128]{2,1,0:T(1,128)S(1)} %bitcast.7), channel_id=1, replica_groups=mesh['ctx'=8,'head'=4,'dp'=8] {'ctx','head','dp'}, dimensions={0} | all-to-all | bytes 262144 | tf_op jit(solution)/shard_map/all_to_all | solution.py:491
  62.6 0.6 slice_reduce_fusion
  (1 shorter events, 0.0 us)
Async XLA Ops:
  0.6 8.1 %copy-start.3 = (bf16[1,256,896]{2,1,0:T(8,128)(2,1)S(1)}, bf16[1,256,896]{2,1,0:T(8,128)(2,1)}, u32[]{:S(2)}) copy-start(bf16[1,256,896]{2,1,0:T(8,128)(2,1)} %k.3) | copy-start | bytes 1376260
  0.6 8.1 %copy-start.8 = (f32[1,7,256]{2,0,1:T(1,128)S(1)}, f32[1,7,256]{2,0,1:T(1,128)}, u32[]{:S(2)}) copy-start(f32[1,7,256]{2,0,1:T(1,128)} %param.15) | copy-start | bytes 21508
  0.7 8.1 %copy-start.9 = (f32[1,7,256]{2,0,1:T(1,128)S(1)}, f32[1,7,256]{2,0,1:T(1,128)}, u32[]{:S(2)}) copy-start(f32[1,7,256]{2,0,1:T(1,128)} %param.16) | copy-start | bytes 21508
  2.3 12.6 %collective-permute-start.2 = (bf16[528,128]{1,0:T(8,128)(2,1)}, bf16[528,128]{1,0:T(8,128)(2,1)S(1)}, u32[]{:S(2)}, u32[]{:S(2)}) collective-permute-start(bf16[528,128]{1,0:T(8,128)(2,1)} %get-tuple-element.29.own), channel_id=1, source_target_pairs={{0,128},{32,160},{64,192},{96,224},{128,0},{160,32},{192,64},{224,... | collective-permute-start | bytes 405512 | tf_op jit(solution)/shard_map/ppermute | solution.py:352
  6.0 9.0 %collective-permute-start.1 = (bf16[528,128]{1,0:T(8,128)(2,1)}, bf16[528,128]{1,0:T(8,128)(2,1)S(1)}, u32[]{:S(2)}, u32[]{:S(2)}) collective-permute-start(bf16[528,128]{1,0:T(8,128)(2,1)} %get-tuple-element.29.own), channel_id=1, source_target_pairs={{0,64},{32,96},{64,128},{96,160},{128,192},{160,224},{192,0},{224,... | collective-permute-start | bytes 405512 | tf_op jit(solution)/shard_map/ppermute | solution.py:352
  6.3 8.7 %collective-permute-start = (bf16[16,1024]{1,0:T(8,128)(2,1)}, bf16[16,1024]{1,0:T(8,128)(2,1)S(1)}, u32[]{:S(2)}, u32[]{:S(2)}) collective-permute-start(bf16[16,1024]{1,0:T(8,128)(2,1)} %get-tuple-element.24), channel_id=1, source_target_pairs={{0,32},{32,64},{64,96},{96,128},{128,160},{160,192},{192,224},{224... | collective-permute-start | bytes 98312 | tf_op jit(solution)/shard_map/ppermute | solution.py:352
  8.7 0.7 %copy-start.7 = (s32[1,256]{1,0:T(1,128)S(1)}, s32[1,256]{1,0:T(1,128)}, u32[]{:S(2)}) copy-start(s32[1,256]{1,0:T(1,128)} %ids.3) | copy-start | bytes 3076
  9.4 5.6 %copy-start.1 = (bf16[1,256,896]{2,1,0:T(8,128)(2,1)S(1)}, bf16[1,256,896]{2,1,0:T(8,128)(2,1)}, u32[]{:S(2)}) copy-start(bf16[1,256,896]{2,1,0:T(8,128)(2,1)} %v.1) | copy-start | bytes 1376260
  9.4 5.6 %copy-start.5 = (f32[1,7,4,256]{3,2,1,0:T(4,128)S(1)}, f32[1,7,4,256]{3,2,1,0:T(4,128)}, u32[]{:S(2)}) copy-start(f32[1,7,4,256]{3,2,1,0:T(4,128)} %taps.1) | copy-start | bytes 86020
  15.0 2.8 %copy-start.2 = (bf16[528,128]{1,0:T(8,128)(2,1)S(1)}, bf16[528,128]{1,0:T(8,128)(2,1)}, u32[]{:S(2)}) copy-start(bf16[528,128]{1,0:T(8,128)(2,1)} %get-tuple-element.29.own) | copy-start | bytes 405508
  15.0 3.6 %copy-start.4 = (bf16[1,256,896]{2,1,0:T(8,128)(2,1)S(1)}, bf16[1,256,896]{2,1,0:T(8,128)(2,1)}, u32[]{:S(2)}) copy-start(bf16[1,256,896]{2,1,0:T(8,128)(2,1)} %q.3) | copy-start | bytes 1376260
  17.5 1.1 %copy-start.6 = (f32[1,7,256]{2,0,1:T(1,128)S(1)}, f32[1,7,256]{2,0,1:T(1,128)}, u32[]{:S(2)}) copy-start(f32[1,7,256]{2,0,1:T(1,128)} %param.23) | copy-start | bytes 21508
  17.5 2.8 %collective-permute-start.3 = (bf16[14,128,128]{2,1,0:T(8,128)(2,1)S(1)}, bf16[14,128,128]{2,1,0:T(8,128)(2,1)S(1)}, u32[]{:S(2)}, u32[]{:S(2)}) collective-permute-start(bf16[14,128,128]{2,1,0:T(8,128)(2,1)S(1)} %get-tuple-element.30.own), channel_id=1, source_target_pairs={{0,32},{32,0},{64,96},{96,64},{128,160},{160,128},{192,224},{224,1... | collective-permute-start | bytes 1376264 | tf_op jit(solution)/shard_map/ppermute | solution.py:355
  17.8 3.2 %collective-permute-start.5 = (bf16[528,128]{1,0:T(8,128)(2,1)S(1)}, bf16[528,128]{1,0:T(8,128)(2,1)S(1)}, u32[]{:S(2)}, u32[]{:S(2)}) collective-permute-start(bf16[528,128]{1,0:T(8,128)(2,1)S(1)} %copy-done.2), channel_id=1, source_target_pairs={{0,32},{32,0},{64,96},{96,64},{128,160},{160,128},{192,224},{224,1... | collective-permute-start | bytes 405512 | tf_op jit(solution)/shard_map/ppermute | solution.py:355
  18.1 2.9 %collective-permute-start.7 = (bf16[528,128]{1,0:T(8,128)(2,1)S(1)}, bf16[528,128]{1,0:T(8,128)(2,1)S(1)}, u32[]{:S(2)}, u32[]{:S(2)}) collective-permute-start(bf16[528,128]{1,0:T(8,128)(2,1)S(1)} %collective-permute-done.2.afters.arrived.r4), channel_id=1, source_target_pairs={{0,32},{32,0},{64,96},{96,64},{128,160},{160,128},{192,224},{224,1... | collective-permute-start | bytes 405512 | tf_op jit(solution)/shard_map/ppermute | solution.py:355
  18.3 2.7 %collective-permute-start.6 = (bf16[528,128]{1,0:T(8,128)(2,1)S(1)}, bf16[528,128]{1,0:T(8,128)(2,1)S(1)}, u32[]{:S(2)}, u32[]{:S(2)}) collective-permute-start(bf16[528,128]{1,0:T(8,128)(2,1)S(1)} %collective-permute-done.1.after.r2), channel_id=1, source_target_pairs={{0,32},{32,0},{64,96},{96,64},{128,160},{160,128},{192,224},{224,1... | collective-permute-start | bytes 405512 | tf_op jit(solution)/shard_map/ppermute | solution.py:355
  20.4 1.0 %copy-start = (bf16[1,256,896]{2,1,0:T(8,128)(2,1)S(1)}, bf16[1,256,896]{2,1,0:T(8,128)(2,1)}, u32[]{:S(2)}) copy-start(bf16[1,256,896]{2,1,0:T(8,128)(2,1)} %q.5) | copy-start | bytes 1376260
  20.7 6.0 %collective-permute-start.4 = (bf16[7,64,128]{2,1,0:T(8,128)(2,1)S(1)}, bf16[7,64,128]{2,1,0:T(8,128)(2,1)S(1)}, u32[]{:S(2)}, u32[]{:S(2)}) collective-permute-start(bf16[7,64,128]{2,1,0:T(8,128)(2,1)S(1)} %get-tuple-element.36.i), channel_id=1, source_target_pairs={{0,64},{32,96},{64,128},{96,160},{128,192},{160,224},{192,0},{224,... | collective-permute-start | bytes 344072 | tf_op jit(solution)/shard_map/ppermute | solution.py:352
  26.7 1.9 %copy-start.10 = (f32[896]{0:T(1024)S(1)}, f32[896]{0:T(1024)}, u32[]{:S(2)}) copy-start(f32[896]{0:T(1024)} %param.18) | copy-start | bytes 10756
  26.9 6.7 %collective-permute-start.9 = (bf16[7,64,128]{2,1,0:T(8,128)(2,1)S(1)}, bf16[7,64,128]{2,1,0:T(8,128)(2,1)S(1)}, u32[]{:S(2)}, u32[]{:S(2)}) collective-permute-start(bf16[7,64,128]{2,1,0:T(8,128)(2,1)S(1)} %shard_map.145), channel_id=1, source_target_pairs={{0,96},{32,64},{64,160},{96,128},{128,224},{160,192},{192,32},{224... | collective-permute-start | bytes 344072 | tf_op jit(solution)/shard_map/ppermute | solution.py:362
  27.0 9.1 %collective-permute-start.8 = (bf16[7,64,128]{2,1,0:T(8,128)(2,1)S(1)}, bf16[7,64,128]{2,1,0:T(8,128)(2,1)S(1)}, u32[]{:S(2)}, u32[]{:S(2)}) collective-permute-start(bf16[7,64,128]{2,1,0:T(8,128)(2,1)S(1)} %shard_map.145), channel_id=1, source_target_pairs={{0,64},{32,96},{64,128},{96,160},{128,192},{160,224},{192,0},{224,... | collective-permute-start | bytes 344072 | tf_op jit(solution)/shard_map/ppermute | solution.py:352

commit v3 on v2

v3 whole, which is shorter than its diff:
```python
import functools
import math

import jax
import jax.numpy as jnp
from jax import lax
from jax.experimental import pallas as pl
from jax.experimental.pallas import tpu as pltpu
from jax.sharding import PartitionSpec as P

EPSILON = 1e-06
MASKED = -1e30
HEAD = 128
F32 = jnp.float32
BF16 = jnp.bfloat16
VMEM_BYTES = 32 * 1024 * 1024
PACK_VMEM = 62 * 1024 * 1024


def nn(a, b, precision=None):
    return lax.dot_general(
        a, b, (((1,), (0,)), ((), ())), precision=precision, preferred_element_type=F32
    )


def nt(a, b):
    return lax.dot_general(a, b, (((1,), (1,)), ((), ())), preferred_element_type=F32)


def tn(a, b):
    return lax.dot_general(a, b, (((0,), (0,)), ((), ())), preferred_element_type=F32)


def head_lanes(h):
    return slice(h * HEAD, (h + 1) * HEAD)


def call(body, outs, *args, scratch=(), hbm=(), hbm_out=(), copies=0, flops=0, vmem=VMEM_BYTES):
    buffers = [pltpu.VMEM(s, d) for s, d in scratch]
    copies = copies or len(hbm)
    if copies:
        buffers.append(pltpu.SemaphoreType.DMA((copies,)))
    return pl.pallas_call(
        body,
        out_shape=[jax.ShapeDtypeStruct(s, d) for s, d in outs],
        in_specs=[
            pl.BlockSpec(memory_space=pltpu.HBM if i in hbm else pltpu.VMEM)
            for i in range(len(args))
        ],
        out_specs=[
            pl.BlockSpec(memory_space=pltpu.HBM if i in hbm_out else pltpu.VMEM)
            for i in range(len(outs))
        ],
        scratch_shapes=buffers,
        compiler_params=pltpu.CompilerParams(vmem_limit_bytes=vmem),
        cost_estimate=pl.CostEstimate(flops=flops, bytes_accessed=0, transcendentals=0),
    )(*args)


def pack_body(tk, tv, sv, ids, kv, rim, id_s, sems):
    tokens = tk.shape[1]
    features = sv.shape[2]
    moves = [
        pltpu.make_async_copy(ids, id_s, sems.at[0]),
        pltpu.make_async_copy(
            sv.at[0, tokens - 16 : tokens, :], rim.at[:, 0:features], sems.at[1]
        ),
        pltpu.make_async_copy(tk.at[0], kv.at[0:tokens], sems.at[2]),
        pltpu.make_async_copy(tv.at[0], kv.at[tokens : 2 * tokens], sems.at[3]),
    ]
    for move in moves:
        move.start()
    moves[0].wait()
    idf = id_s[...].astype(F32)
    rows = lax.broadcasted_iota(jnp.int32, (16, 128), 0)
    block = jnp.zeros((16, 128), F32)
    for i in range(tokens // 128):
        block = jnp.where(rows == i, idf[:, i * 128 : (i + 1) * 128], block)
    kv[2 * tokens : 2 * tokens + 16] = block.astype(BF16)
    rim[:, features : features + 128] = jnp.broadcast_to(
        idf[:, tokens - 128 : tokens], (16, 128)
    ).astype(BF16)
    for move in moves[1:]:
        move.wait()


def eye(n):
    rows = lax.broadcasted_iota(jnp.int32, (n, n), 0)
    cols = lax.broadcasted_iota(jnp.int32, (n, n), 1)
    return jnp.where(rows == cols, 1.0, 0.0)


def keys_body(k, beta, decay, ids, t_out, uk_out, m_out, rows_out, cols_out, eight, a_s, c_s, t_s, beta_s, decay_s, id_s, sems):
    tokens = k.shape[1]
    heads = beta.shape[0]
    half = tokens // 2
    small = c_s.shape[1]
    moves = [
        pltpu.make_async_copy(source, target, sems.at[i])
        for i, (source, target) in enumerate(((beta, beta_s), (decay, decay_s), (ids, id_s)))
    ]
    for move in moves:
        move.start()
    lane = lax.broadcasted_iota(jnp.int32, (tokens, 128), 1)
    packed = jnp.zeros((tokens, 128), F32)
    for h in range(heads):
        kf = k[0, :, head_lanes(h)].astype(F32)
        norm = lax.rsqrt(jnp.sum(kf * kf, axis=1, keepdims=True) + EPSILON)
        packed = jnp.where(lane == h, norm, packed)
    r8 = packed.T[0:8]
    for move in moves:
        move.wait()
    idf = id_s[...].astype(F32)
    eight[...] = jnp.zeros_like(eight)
    for h in range(heads):
        eight[0, h : h + 1] = decay_s[h]
        eight[1, h : h + 1] = beta_s[h]
    row_index = lax.broadcasted_iota(jnp.int32, (tokens, tokens), 0)
    col_index = lax.broadcasted_iota(jnp.int32, (tokens, tokens), 1)
    upto = jnp.where(row_index <= col_index, 1.0, 0.0)
    run8 = nn(eight[0], upto, lax.Precision.HIGHEST)
    br8 = eight[1] * r8
    fs8 = jnp.where(idf == idf[:, 0:1], jnp.exp(run8), 0.0)
    fsr8 = fs8 * r8
    wend8 = (
        jnp.where(
            idf == idf[:, tokens - 1 : tokens],
            jnp.exp(run8[:, tokens - 1 : tokens] - run8),
            0.0,
        )
        * br8
    )
    ids8 = jnp.broadcast_to(idf, (8, tokens))
    rows_out[...] = jnp.concatenate([run8, br8, ids8, wend8], axis=0)
    stacked = jnp.concatenate([run8, r8, fs8, ids8, jnp.zeros((96, tokens), F32)], axis=0)
    cols = stacked.T
    cols_out[...] = cols

    rh = lax.broadcasted_iota(jnp.int32, (half, half), 0)
    ch = lax.broadcasted_iota(jnp.int32, (half, half), 1)
    below = ch < rh
    cl = lax.broadcasted_iota(jnp.int32, (small, half), 1)
    owns = [(cl // small) == i for i in range(half // small)]
    for h in range(heads):
        kh = k[0, :, head_lanes(h)]
        for at, (i, j) in enumerate(((0, 0), (1, 0), (1, 1))):
            ri, rj = slice(i * half, (i + 1) * half), slice(j * half, (j + 1) * half)
            kk = nt(kh[ri], kh[rj])
            seen = cols[ri, 24:25] == idf[:, rj]
            if i == j:
                seen = seen & below
            between = jnp.where(seen, jnp.exp(cols[ri, h : h + 1] - run8[h : h + 1, rj]), 0.0)
            a = between * br8[h : h + 1, rj] * (cols[ri, 8 + h : 9 + h] * kk)
            a_s[h, at] = a.astype(BF16)
            if i == j:
                c = jnp.zeros((small, half), F32)
                for n, own in enumerate(owns):
                    c = jnp.where(own, a[n * small : (n + 1) * small], c)
                c_s[2 * h + i] = c

    rs = lax.broadcasted_iota(jnp.int32, (small, half), 0)
    cs = cl % small
    blocks = [(h, b) for h in range(heads) for b in range(2)]
    inside = jnp.where((rh // small) == (ch // small), 1.0, 0.0)
    inside16 = inside.astype(BF16)

    def merges(r, c, bits):
        rb, cb = r >> bits, c >> bits
        return jnp.where(((rb & 1) == 1) & (cb == rb - 1), 1.0, 0.0)

    def spread(x):
        return jnp.concatenate([x] * (half // small), axis=0) * inside16

    unit = jnp.where(rs == cs, 1.0, 0.0)
    first = merges(rs, cs, 0)
    ts = [unit - c_s[n] * first for n in range(len(blocks))]
    for bits in range(1, (small - 1).bit_length()):
        mask = merges(rs, cs, bits)
        tb = [t.astype(BF16) for t in ts]
        ps = [nn((c_s[n] * mask).astype(BF16), spread(tb[n])) for n in range(len(blocks))]
        ts = [t - nn(tb[n], spread(ps[n].astype(BF16))) for n, t in enumerate(ts)]
    for n, t in enumerate(ts):
        t_s[n] = jnp.concatenate([t] * (half // small), axis=0) * inside
    for bits in range((small - 1).bit_length(), (half - 1).bit_length()):
        size = 1 << bits
        odd = [slice(i * size, (i + 1) * size) for i in range(1, half // size, 2)]
        mask = merges(rh, ch, bits).astype(BF16)
        tb = [t_s[n].astype(BF16) for n in range(len(blocks))]
        ps = [
            nn(jnp.concatenate([(a_s[h, 2 * b, r] * mask[r]) for r in odd], axis=0), tb[n])
            for n, (h, b) in enumerate(blocks)
        ]
        changes = []
        for n in range(len(blocks)):
            p = ps[n].astype(BF16)
            pieces = []
            for i in range(len(odd)):
                pieces += [jnp.zeros((size, half), BF16), p[i * size : (i + 1) * size]]
            changes.append(
                nn(
                    jnp.concatenate([tb[n][r] for r in odd], axis=0),
                    jnp.concatenate(pieces, axis=0),
                )
            )
        for n in range(len(blocks)):
            for i, r in enumerate(odd):
                t_s[n, r] = t_s[n, r] - changes[n][i * size : (i + 1) * size]
    tb = [t_s[n].astype(BF16) for n in range(len(blocks))]
    one = eye(HEAD)
    one16 = one.astype(BF16)
    keys = [k[0, :, head_lanes(h)] for h in range(heads)]
    xs = [nt(one16, keys[h]) for h in range(heads)]
    ps = [nn(a_s[h, 1], tb[2 * h]).astype(BF16) for h in range(heads)]
    t21 = [(-nn(tb[2 * h + 1], ps[h])).astype(BF16) for h in range(heads)]
    for h in range(heads):
        t_out[h, 0:half, 0:half] = tb[2 * h]
        t_out[h, half:tokens, half:tokens] = tb[2 * h + 1]
        t_out[h, 0:half, half:tokens] = jnp.zeros((half, half), BF16)
        t_out[h, half:tokens, 0:half] = t21[h]
    none = jnp.zeros((half, half), BF16)
    ts = [
        jnp.concatenate(
            [
                jnp.concatenate([tb[2 * h], none], axis=1),
                jnp.concatenate([t21[h], tb[2 * h + 1]], axis=1),
            ],
            axis=0,
        )
        for h in range(heads)
    ]
    uks = [nt((xs[h] * fsr8[h : h + 1]).astype(BF16), ts[h]) for h in range(heads)]
    ms = [nn((uks[h] * wend8[h : h + 1]).astype(BF16), keys[h]) for h in range(heads)]
    for h in range(heads):
        uk_out[h] = uks[h].astype(BF16)
        m_out[h] = one * fs8[h : h + 1, tokens - 1 : tokens] - ms[h]


def values_body(v, rim, taps, rows, t, k, m, after, mi_out, uv_out):
    features = v.shape[2]
    heads = taps.shape[1]
    count = taps.shape[2]
    first = lax.axis_index("ctx") == 0
    idf = rows[16:17]
    before = rim[0:1, features : features + 128].astype(F32)
    before = jnp.where(first, -1.0, before)
    longer = jnp.concatenate([before, idf], axis=1)
    keep = [
        jnp.where(pltpu.roll(longer, j, 1)[:, 128:] == idf, 1.0, 0.0) for j in range(1, count)
    ]
    joined = jnp.where(before[0:1, 127:128] == idf[:, 0:1], 1.0, 0.0)
    one16 = eye(HEAD).astype(BF16)
    empty = jnp.zeros((112, HEAD), BF16)
    every = range(heads)
    keys = [k[0, :, head_lanes(h)] for h in every]
    owns = [nt(one16, v[0, :, head_lanes(h)]) for h in every]
    rims = [nt(one16, jnp.concatenate([empty, rim[:, head_lanes(h)]], axis=0)) for h in every]
    values = []
    for h in every:
        whole = jnp.concatenate([rims[h], owns[h]], axis=1)
        conv = taps[0, h, 0:1] * owns[h]
        for j in range(1, count):
            conv = conv + (taps[0, h, j : j + 1] * keep[j - 1]) * pltpu.roll(whole, j, 1)[:, 128:]
        values.append((conv / (1.0 + jnp.exp(-conv))).astype(BF16))
    uvs = [nt(values[h], t[h]) for h in every]
    ends = [nn((uvs[h] * rows[24 + h : 25 + h]).astype(BF16), keys[h]) for h in every]
    for h in every:
        uv_out[h] = uvs[h].astype(BF16)
        mi_out[h] = (joined * m[h]).astype(BF16)
        mi_out[heads + h] = ends[h].astype(BF16)


def queries_body(q, k, rim, rows, cols_in, uk, uv, lw, local_out, reader_out, lw_out, lw_s):
    tokens = q.shape[1]
    features = q.shape[2]
    heads = uk.shape[0]
    first = lax.axis_index("ctx") == 0
    idf = rows[16:17]
    before = jnp.where(first, -1.0, rim[0:1, features : features + 128].astype(F32))
    joined = jnp.where(before[0:1, 127:128] == idf[:, 0:1], 1.0, 0.0)
    row_index = lax.broadcasted_iota(jnp.int32, (tokens, tokens), 0)
    col_index = lax.broadcasted_iota(jnp.int32, (tokens, tokens), 1)
    cols = cols_in[...]
    visible = (col_index <= row_index) & (cols[:, 24:25] == idf)
    lw_s[...] = jnp.zeros_like(lw_s)
    for h in range(heads):
        lw_s[h : h + 1] = lw[h]
    lw_out[...] = lw_s[...].T
    every = range(heads)
    qs = [q[0, :, head_lanes(h)] for h in every]
    qks = [nt(qs[h], k[0, :, head_lanes(h)]) for h in every]
    norms, readings = [], []
    for h in every:
        qf = qs[h].astype(F32)
        norms.append(lax.rsqrt(jnp.sum(qf * qf, axis=1, keepdims=True) + EPSILON))
        between = jnp.where(visible, jnp.exp(cols[:, h : h + 1] - rows[h : h + 1]), 0.0)
        readings.append((between * rows[8 + h : 9 + h] * (norms[h] * qks[h])).astype(BF16))
    both = [nt(readings[h], jnp.concatenate([uv[h], uk[h]], axis=0)) for h in every]
    for h in every:
        local_out[h] = both[h][:, 0:HEAD]
        reader = (cols[:, 16 + h : 17 + h] * norms[h]) * qs[h].astype(F32) - both[h][:, HEAD:]
        reader_out[h] = (joined * reader).astype(BF16)


def teacher_body(first_head, last_head, q, cols_in, own, r2, r4, x0, x2, x4, *refs):
    out, full, k_s, v_s, id_s, bias_s = refs[-6:]
    if first_head:
        out[0, :, 0 : first_head * HEAD] = refs[0][0, :, 0 : first_head * HEAD]
    tokens = q.shape[1]
    halves = tokens // 128
    index = lax.axis_index("ctx")
    odd = lax.rem(index, 2) == 1
    def place(slot, source):
        k_s[slot * tokens : (slot + 1) * tokens] = source[0:tokens]
        v_s[slot * tokens : (slot + 1) * tokens] = source[tokens : 2 * tokens]
        behind = 4 - slot
        valid = index >= behind
        names = source[2 * tokens : 2 * tokens + 16].astype(F32)
        for i in range(halves):
            at = (slot * halves + i) * 128
            id_s[:, at : at + 128] = jnp.where(valid, names[i : i + 1], -1.0)

    place(0, r4)
    place(2, r2)
    place(4, own)

    @pl.when(odd)
    def _():
        place(1, x2)
        place(3, x0)

    @pl.when(jnp.logical_not(odd))
    def _():
        place(1, x4)
        place(3, x2)

    width = 5 * tokens
    id_col = cols_in[:, 24:25]
    same = id_col == id_s[...]
    row_index = lax.broadcasted_iota(jnp.int32, (tokens, width), 0)
    col_index = lax.broadcasted_iota(jnp.int32, (tokens, width), 1) - 4 * tokens
    bias_s[...] = jnp.where(same & (col_index <= row_index), 0.0, MASKED)
    scale = math.log2(math.e) / math.sqrt(HEAD)
    span = width - (halves - 1) * 128
    tiles = [(h, r) for h in range(first_head, last_head) for r in range(halves)]

    def scores(h, r):
        return nt(q[0, r * 128 : (r + 1) * 128, head_lanes(h)], k_s[r * 128 : r * 128 + span])

    ahead = 2
    ss = [scores(*tile) for tile in tiles[:ahead]]
    for n, (h, r) in enumerate(tiles):
        if n + ahead < len(tiles):
            ss.append(scores(*tiles[n + ahead]))
        at = head_lanes(h - first_head)
        rows = slice(r * 128, (r + 1) * 128)
        cols = slice(r * 128, r * 128 + span)
        s = ss[n] * scale + bias_s[rows, cols]
        largest = jnp.max(s, axis=1, keepdims=True)
        w = jnp.exp2(s - largest)
        total = jnp.sum(w, axis=1, keepdims=True)
        o = nn(w.astype(BF16), v_s[cols]) / total
        full[rows, at] = o
        out[0, rows, head_lanes(h)] = o.astype(BF16)


def is_odd():
    return lax.rem(lax.axis_index("ctx"), 2) == 1


def chip_body(own, other, m_out, i_out):
    heads, rows, _ = i_out.shape
    every = range(heads)
    odd = is_odd()
    later_m = [jnp.where(odd, own[h], other[h]) for h in every]
    early_m = [jnp.where(odd, other[h], own[h]) for h in every]
    early_i = [jnp.where(odd, other[heads + h, rows:], own[heads + h, 0:rows]) for h in every]
    ms = [nn(early_m[h], later_m[h]) for h in every]
    ends = [nn(early_i[h], later_m[h]) for h in every]
    for h in every:
        later_i = jnp.where(odd, own[heads + h, rows:], other[heads + h, 0:rows])
        m_out[h] = ms[h].astype(BF16)
        i_out[h] = (ends[h] + later_i.astype(F32)).astype(BF16)


def join_body(m, i, arriving, after, out):
    every = range(m.shape[0])
    ends = [nn(arriving[h], m[h]) for h in every]
    for h in every:
        out[h] = (ends[h] + i[h].astype(F32)).astype(BF16)


def finish_body(mine, theirs, other, local, reader, gain, teachers, lw, out, sums):
    heads = mine.shape[0]
    every = range(heads)
    odd = is_odd()
    total = jnp.zeros(lw.shape, F32)
    states = []
    for h in every:
        a, b = mine[h], theirs[h]
        states.append(jnp.concatenate([jnp.where(odd, b, a), jnp.where(odd, a, b)], axis=0))
    steps = [nn(states[h], other[h]) for h in every]
    for h in every:
        step = (steps[h] + other[heads + h].astype(F32)).astype(BF16)
        states[h] = jnp.where(odd, step, states[h])
    os = [local[h] + nt(reader[h], states[h]) for h in every]
    for h in every:
        mean = jnp.sum(os[h] * os[h], axis=1, keepdims=True) * (1.0 / HEAD)
        student = os[h] * lax.rsqrt(mean + EPSILON) * gain[:, head_lanes(h)]
        out[0, :, head_lanes(h)] = student.astype(BF16)
        difference = student - teachers[:, head_lanes(h)]
        total = total + lw[:, h : h + 1] * (difference * difference)
    partial = jnp.sum(jnp.sum(total, axis=0, keepdims=True), axis=1, keepdims=True)
    sums[...] = jnp.broadcast_to(partial, sums.shape)


def on_device(
    student_q,
    student_k,
    student_v,
    beta,
    log_decay,
    kernel,
    out_gain,
    teacher_q,
    teacher_k,
    teacher_v,
    segment_ids,
    loss_weight,
):
    _, tokens, features = student_q.shape
    heads = beta.shape[1]
    shards = lax.axis_size("ctx")
    everyone = shards * lax.axis_size("head") * lax.axis_size("dp")

    def rotated(block, distance):
        return lax.ppermute(block, "ctx", [(i, (i + distance) % shards) for i in range(shards)])

    def swapped(block):
        return lax.ppermute(block, "ctx", [(i, i ^ 1) for i in range(shards)])

    def by_head(block):
        return block.reshape(heads, 1, tokens)

    def crossed(block):
        route = [(i, ((i + 2) % shards) ^ 1) for i in range(shards)]
        return lax.ppermute(block, "ctx", route)

    kv, rim = call(
        pack_body,
        [((2 * tokens + 16, HEAD), BF16), ((16, features + 128), BF16)],
        teacher_k,
        teacher_v,
        student_v,
        segment_ids,
        scratch=[((1, tokens), jnp.int32)],
        hbm=(0, 1, 2, 3),
        vmem=PACK_VMEM,
    )
    rim = rotated(rim, 1)
    r2 = rotated(kv, 2)
    x0 = swapped(kv)
    t, uk, m0, rows, cols = call(
        keys_body,
        [
            ((heads, tokens, tokens), BF16),
            ((heads, HEAD, tokens), BF16),
            ((heads, HEAD, HEAD), F32),
            ((32, tokens), F32),
            ((tokens, 128), F32),
        ],
        student_k,
        by_head(beta),
        by_head(log_decay),
        segment_ids,
        scratch=[
            ((2, 8, tokens), F32),
            ((heads, 3, tokens // 2, tokens // 2), BF16),
            ((2 * heads, 32, tokens // 2), F32),
            ((2 * heads, tokens // 2, tokens // 2), F32),
            ((heads, 1, tokens), F32),
            ((heads, 1, tokens), F32),
            ((1, tokens), jnp.int32),
        ],
        hbm=(1, 2, 3),
        flops=5 * 10**8,
    )
    r4 = rotated(r2, 2)
    mi, uv = call(
        values_body,
        [((2 * heads, HEAD, HEAD), BF16), ((heads, HEAD, tokens), BF16)],
        student_v,
        rim,
        kernel,
        rows,
        t,
        student_k,
        m0,
        r2,
        flops=2 * 10**8,
    )
    mi_other = swapped(mi)
    x2 = swapped(r2)
    local, reader, lw = call(
        queries_body,
        [
            ((heads, tokens, HEAD), F32),
            ((heads, tokens, HEAD), BF16),
            ((tokens, 128), F32),
        ],
        student_q,
        student_k,
        rim,
        rows,
        cols,
        uk,
        uv,
        by_head(loss_weight),
        scratch=[((128, tokens), F32)],
        flops=2 * 10**8,
    )
    m_chip, i_chip = call(
        chip_body,
        [((heads, HEAD, HEAD), BF16), ((heads, HEAD // 2, HEAD), BF16)],
        mi,
        mi_other,
    )
    behind = rotated(i_chip, 2)
    x4 = swapped(r4)

    def attend(first_head, last_head, *earlier):
        count = last_head - first_head
        return call(
            functools.partial(teacher_body, first_head, last_head),
            [((1, tokens, features), BF16), ((tokens, count * HEAD), F32)],
            teacher_q,
            cols,
            kv,
            r2,
            r4,
            x0,
            x2,
            x4,
            *earlier,
            flops=count * 10**8,
            scratch=[
                ((5 * tokens, HEAD), BF16),
                ((5 * tokens, HEAD), BF16),
                ((1, 5 * tokens), F32),
                ((tokens, 5 * tokens), F32),
            ],
        )

    (joined,) = call(
        join_body, [((heads, HEAD // 2, HEAD), BF16)], m_chip, i_chip, behind, lw
    )
    mine = rotated(joined, 2)
    theirs = crossed(joined)
    teacher_out, teacher = attend(0, heads)
    student_out, sums = call(
        finish_body,
        [((1, tokens, features), BF16), ((everyone, 128), F32)],
        mine,
        theirs,
        mi_other,
        local,
        reader,
        out_gain.reshape(1, features),
        teacher,
        lw,
    )
    gathered = lax.all_to_all(sums, ("ctx", "head", "dp"), 0, 0, tiled=True)
    loss = jnp.sum(gathered[:, 0]) / (everyone * heads * tokens * HEAD)
    return (student_out, teacher_out, loss)


def solution(mesh):
    placed = (
        P("dp", "ctx", "head"),
        P("dp", "ctx", "head"),
        P("dp", "ctx", "head"),
        P("dp", "head", "ctx"),
        P("dp", "head", "ctx"),
        P("dp", "head", None, "ctx"),
        P("head"),
        P("dp", "ctx", "head"),
        P("dp", "ctx", "head"),
        P("dp", "ctx", "head"),
        P("dp", "ctx"),
        P("dp", "head", "ctx"),
    )
    return jax.shard_map(
        on_device,
        mesh=mesh,
        in_specs=placed,
        out_specs=(P("dp", "ctx", "head"), P("dp", "ctx", "head"), P()),
        check_vma=False,
    )
```

time: 65.2 us -> 60.4 us (0.926)
  Pallas kernels: 20.4 us -> 15.1 us
  starting transfers between devices: 9.53 us -> 10.3 us
    pallas_call x9 -> x8, Pallas kernels: 20.4 us -> 15.1 us  [call(): pl.pallas_call(body, out_shape=[jax.ShapeDtypeStruct(s, d) for s, d in ou...]
    ppermute x5, starting transfers between devices: 8.34 us -> 5.45 us  [rotated(): lax.ppermute(block, 'ctx', [(i, (i + distance) % shards) for i in range(s...]
    ppermute x5, waiting for transfers between devices: 5.19 us -> 2.85 us  [rotated(): lax.ppermute(block, 'ctx', [(i, (i + distance) % shards) for i in range(s...]
    ppermute x4, starting transfers between devices: 1.11 us -> 3.19 us  [swapped(): return lax.ppermute(block, 'ctx', [(i, i ^ 1) for i in range(shards)])]
    ppermute x1, waiting for transfers between devices: 0.85 us -> 2.56 us  [crossed(): return lax.ppermute(block, 'ctx', route)]
    ppermute x1, starting transfers between devices: 0.08 us -> 1.69 us  [crossed(): return lax.ppermute(block, 'ctx', route)]
    ppermute x4, waiting for transfers between devices: 0.01 us -> 1.23 us  [swapped(): return lax.ppermute(block, 'ctx', [(i, i ^ 1) for i in range(shards)])]
  transfers between devices with their start and end apart: 10 -> 10, of which waited for: 3 -> 3; matrix products, arithmetic and copies ran while one was open for 0% -> 0% of each run, Pallas kernels for 22% -> 17%
where the time goes in v3:
time: 60.4 us; the launch traced here: 60.2 us
  blocking collectives  24.3 us (40%)
  Pallas kernels  15.1 us (25%)
  starting transfers between devices  10.3 us (17%)
  waiting for transfers between devices  6.65 us (11%)
  between operations  2.58 us (4%)
  local copies, waits for them, and re-layouts  0.72 us (1%)
  other arithmetic  0.63 us (1%)
    all_to_all x1, blocking collectives, on_device(): gathered = lax.all_to_all(sums, ('ctx', 'head', 'dp'), 0, 0, tiled=True)  24.3 us
    pallas_call x8, Pallas kernels, call(): pl.pallas_call(body, out_shape=[jax.ShapeDtypeStruct(s, d) for s, d in ou...  15.1 us
    ppermute x5, starting transfers between devices, rotated(): lax.ppermute(block, 'ctx', [(i, (i + distance) % shards) for i in range(s...  5.45 us
    ppermute x4, starting transfers between devices, swapped(): return lax.ppermute(block, 'ctx', [(i, i ^ 1) for i in range(shards)])  3.19 us
    ppermute x5, waiting for transfers between devices, rotated(): lax.ppermute(block, 'ctx', [(i, (i + distance) % shards) for i in range(s...  2.85 us
    ppermute x1, waiting for transfers between devices, crossed(): return lax.ppermute(block, 'ctx', route)  2.56 us
    ppermute x1, starting transfers between devices, crossed(): return lax.ppermute(block, 'ctx', route)  1.69 us
    ppermute x4, waiting for transfers between devices, swapped(): return lax.ppermute(block, 'ctx', [(i, i ^ 1) for i in range(shards)])  1.23 us
  transfers between devices with their start and end apart: 10, of which 3 were waited for; matrix products, arithmetic and copies ran while one was open for 0% of the time, Pallas kernels for 17%

profile of v3, /device:TPU:1, one launch (start us, length us, event | category | flops | bytes accessed | tf_op | source)
XLA Modules:
  0.0 60.2 jit_solution(10445572432920904569)
XLA Ops:
  0.6 0.0 copy-start.1
  0.6 0.0 copy-start.8
  0.7 0.0 copy-start.9
  0.7 1.7 %shard_map.139 = (bf16[528,128]{1,0:T(8,128)(2,1)}, bf16[16,1024]{1,0:T(8,128)(2,1)}) custom-call(bf16[1,256,128]{2,1,0:T(8,128)(2,1)} %tk.1, bf16[1,256,128]{2,1,0:T(8,128)(2,1)} %tv.1, bf16[1,256,896]{2,1,0:T(8,128)(2,1)} %v.1, s32[1,256]{1,0:T(1,128)} %ids.3), custom_call_target="tpu_custom_call" | custom-call | tf_op jit(solution)/shard_map/pallas_call | solution.py:43
  2.3 2.1 %collective-permute-start.1 = (bf16[528,128]{1,0:T(8,128)(2,1)}, bf16[528,128]{1,0:T(8,128)(2,1)S(1)}, u32[]{:S(2)}, u32[]{:S(2)}) collective-permute-start(bf16[528,128]{1,0:T(8,128)(2,1)} %get-tuple-element.25.own), channel_id=1, source_target_pairs={{0,64},{32,96},{64,128},{96,160},{128,192},{160,224},{192,0},{224,... | collective-permute-start | bytes 405512 | tf_op jit(solution)/shard_map/ppermute | solution.py:436
  4.4 2.1 %collective-permute-start = (bf16[16,1024]{1,0:T(8,128)(2,1)}, bf16[16,1024]{1,0:T(8,128)(2,1)S(1)}, u32[]{:S(2)}, u32[]{:S(2)}) collective-permute-start(bf16[16,1024]{1,0:T(8,128)(2,1)} %get-tuple-element.21), channel_id=1, source_target_pairs={{0,32},{32,64},{64,96},{96,128},{128,160},{160,192},{192,224},{224... | collective-permute-start | bytes 98312 | tf_op jit(solution)/shard_map/ppermute | solution.py:436
  6.5 0.0 copy-start.5
  6.5 0.0 copy-done.1
  6.5 0.0 copy-done.8
  6.5 0.0 copy-done.9
  6.5 0.7 %copy-done.5 = s32[1,256]{1,0:T(1,128)S(1)} copy-done((s32[1,256]{1,0:T(1,128)S(1)}, s32[1,256]{1,0:T(1,128)}, u32[]{:S(2)}) %copy-start.5) | copy-done | bytes 1048
  7.2 0.0 copy-start
  7.2 0.0 copy-start.3
  7.2 4.1 %shard_map.140 = (bf16[7,256,256]{2,1,0:T(8,128)(2,1)S(1)}, bf16[7,128,256]{2,1,0:T(8,128)(2,1)S(1)}, f32[7,128,128]{2,1,0:T(8,128)S(1)}, f32[32,256]{1,0:T(8,128)S(1)}, f32[256,128]{1,0:T(8,128)S(1)}) custom-call(bf16[1,256,896]{2,1,0:T(8,128)(2,1)S(1)} %copy-done.1, f32[7,1,256]{2,1,0:T(1,128)S(1)} %bitcast.9, f32[7,1,256]{2,1,0:T(1,128)S(1)} %bitcast.10, ...), custom_call_target="tpu_custom_call" | custom-call | flops 500000000 | tf_op jit(solution)/shard_map/pallas_call | solution.py:43
  11.2 0.0 collective-permute-done.rim
  11.3 0.0 collective-permute-done.1.after.r2
  11.3 0.0 copy-done
  11.3 0.0 copy-done.3
  11.3 1.6 %shard_map.141 = (bf16[14,128,128]{2,1,0:T(8,128)(2,1)S(1)}, bf16[7,128,256]{2,1,0:T(8,128)(2,1)S(1)}) custom-call(bf16[1,256,896]{2,1,0:T(8,128)(2,1)S(1)} %copy-done, bf16[16,1024]{1,0:T(8,128)(2,1)S(1)} %collective-permute-done.rim, f32[1,7,4,256]{3,2,1,0:T(4,128)S(1)} %copy-done.3, f32[32,256]{1,0:T(8,128)S(1)} %get-tuple-element.22.rows, ...), custom_call_target="tpu_custom_call" | custom-call | flops 200000000 | tf_op jit(solution)/shard_map/pallas_call | solution.py:43
  12.9 0.0 copy-start.7
  12.9 0.0 copy-start.2
  12.9 0.9 %collective-permute-start.2 = (bf16[14,128,128]{2,1,0:T(8,128)(2,1)S(1)}, bf16[14,128,128]{2,1,0:T(8,128)(2,1)S(1)}, u32[]{:S(2)}, u32[]{:S(2)}) collective-permute-start(bf16[14,128,128]{2,1,0:T(8,128)(2,1)S(1)} %get-tuple-element.26.own), channel_id=1, source_target_pairs={{0,32},{32,0},{64,96},{96,64},{128,160},{160,128},{192,224},{224,1... | collective-permute-start | bytes 1376264 | tf_op jit(solution)/shard_map/ppermute | solution.py:439
  13.8 0.2 collective-permute-start.6
  14.0 1.2 %collective-permute-done.2.other = bf16[14,128,128]{2,1,0:T(8,128)(2,1)S(1)} collective-permute-done((bf16[14,128,128]{2,1,0:T(8,128)(2,1)S(1)}, bf16[14,128,128]{2,1,0:T(8,128)(2,1)S(1)}, u32[]{:S(2)}, u32[]{:S(2)}) %collective-permute-start.2) | collective-permute-done | bytes 458784 | tf_op jit(solution)/shard_map/ppermute | solution.py:439
  15.2 0.3 shard_map.142
  15.5 0.0 copy-start.4
  15.5 0.8 %collective-permute-start.3 = (bf16[7,64,128]{2,1,0:T(8,128)(2,1)S(1)}, bf16[7,64,128]{2,1,0:T(8,128)(2,1)S(1)}, u32[]{:S(2)}, u32[]{:S(2)}) collective-permute-start(bf16[7,64,128]{2,1,0:T(8,128)(2,1)S(1)} %get-tuple-element.28.i), channel_id=1, source_target_pairs={{0,64},{32,96},{64,128},{96,160},{128,192},{160,224},{192,0},{224,... | collective-permute-start | bytes 344072 | tf_op jit(solution)/shard_map/ppermute | solution.py:436
  16.3 0.0 copy-done.7
  16.3 1.0 %collective-permute-start.7 = (bf16[528,128]{1,0:T(8,128)(2,1)S(1)}, bf16[528,128]{1,0:T(8,128)(2,1)S(1)}, u32[]{:S(2)}, u32[]{:S(2)}) collective-permute-start(bf16[528,128]{1,0:T(8,128)(2,1)S(1)} %copy-done.7), channel_id=1, source_target_pairs={{0,32},{32,0},{64,96},{96,64},{128,160},{160,128},{192,224},{224,1... | collective-permute-start | bytes 405512 | tf_op jit(solution)/shard_map/ppermute | solution.py:439
  17.3 0.0 collective-permute-start.8
  17.3 2.8 %collective-permute-done.6.r4 = bf16[528,128]{1,0:T(8,128)(2,1)S(1)} collective-permute-done((bf16[528,128]{1,0:T(8,128)(2,1)S(1)}, bf16[528,128]{1,0:T(8,128)(2,1)S(1)}, u32[]{:S(2)}, u32[]{:S(2)}) %collective-permute-start.6) | collective-permute-done | bytes 135200 | tf_op jit(solution)/shard_map/ppermute | solution.py:436
  20.1 1.3 %collective-permute-start.9 = (bf16[528,128]{1,0:T(8,128)(2,1)S(1)}, bf16[528,128]{1,0:T(8,128)(2,1)S(1)}, u32[]{:S(2)}, u32[]{:S(2)}) collective-permute-start(bf16[528,128]{1,0:T(8,128)(2,1)S(1)} %collective-permute-done.6.r4), channel_id=1, source_target_pairs={{0,32},{32,0},{64,96},{96,64},{128,160},{160,128},{192,224},{224,1... | collective-permute-start | bytes 405512 | tf_op jit(solution)/shard_map/ppermute | solution.py:439
  21.5 0.0 copy-done.2
  21.5 0.0 copy-done.4
  21.5 1.3 %shard_map.143 = (f32[7,256,128]{2,1,0:T(8,128)S(1)}, bf16[7,256,128]{2,1,0:T(8,128)(2,1)S(1)}, f32[256,128]{1,0:T(8,128)S(1)}) custom-call(bf16[1,256,896]{2,1,0:T(8,128)(2,1)S(1)} %copy-done.2, bf16[1,256,896]{2,1,0:T(8,128)(2,1)S(1)} %copy-done.1, bf16[16,1024]{1,0:T(8,128)(2,1)S(1)} %collective-permute-done.rim, f32[32,256]{1,0:T(8,128)S(1)} %get-tuple-element.22.rows, ...), custom_call_target="tpu_custom_call" | custom-call | flops 200000000 | tf_op jit(solution)/shard_map/pallas_call | solution.py:43
  22.8 0.0 copy-start.6
  22.8 0.0 collective-permute-done.3.arriving
  22.9 0.0 copy-start.10
  22.9 0.2 shard_map.144
  23.1 0.3 collective-permute-start.4
  23.3 1.7 %collective-permute-start.5 = (bf16[7,64,128]{2,1,0:T(8,128)(2,1)S(1)}, bf16[7,64,128]{2,1,0:T(8,128)(2,1)S(1)}, u32[]{:S(2)}, u32[]{:S(2)}) collective-permute-start(bf16[7,64,128]{2,1,0:T(8,128)(2,1)S(1)} %shard_map.144), channel_id=1, source_target_pairs={{0,96},{32,64},{64,160},{96,128},{128,224},{160,192},{192,32},{224... | collective-permute-start | bytes 344072 | tf_op jit(solution)/shard_map/ppermute | solution.py:446
  25.0 0.0 copy-done.10
  25.0 0.0 collective-permute-done.7.x0
  25.0 0.0 collective-permute-done.8.x2
  25.1 0.0 collective-permute-done.9.x4
  25.1 0.0 copy-done.6
  25.1 4.2 %shard_map.145 = (bf16[1,256,896]{2,1,0:T(8,128)(2,1)}, f32[256,896]{1,0:T(8,128)S(1)}) custom-call(bf16[1,256,896]{2,1,0:T(8,128)(2,1)S(1)} %copy-done.6, f32[256,128]{1,0:T(8,128)S(1)} %get-tuple-element.29.cols_in, bf16[528,128]{1,0:T(8,128)(2,1)S(1)} %copy-done.7, bf16[528,128]{1,0:T(8,128)(2,1)S(1)} %collective-permute-done.1.after.r2, ...), custom_call_target="tpu_custom_call" | custom-call | flops 700000000 | tf_op jit(solution)/shard_map/pallas_call | solution.py:43
  29.3 0.0 collective-permute-done.4.mine
  29.3 2.6 %collective-permute-done.5.theirs = bf16[7,64,128]{2,1,0:T(8,128)(2,1)S(1)} collective-permute-done((bf16[7,64,128]{2,1,0:T(8,128)(2,1)S(1)}, bf16[7,64,128]{2,1,0:T(8,128)(2,1)S(1)}, u32[]{:S(2)}, u32[]{:S(2)}) %collective-permute-start.5) | collective-permute-done | bytes 114720 | tf_op jit(solution)/shard_map/ppermute | solution.py:446
  31.9 1.7 %shard_map.146 = (bf16[1,256,896]{2,1,0:T(8,128)(2,1)}, f32[256,128]{1,0:T(8,128)S(1)}) custom-call(bf16[7,64,128]{2,1,0:T(8,128)(2,1)S(1)} %collective-permute-done.4.mine, bf16[7,64,128]{2,1,0:T(8,128)(2,1)S(1)} %collective-permute-done.5.theirs, bf16[14,128,128]{2,1,0:T(8,128)(2,1)S(1)} %collective-permute-done.2.other, ...), custom_call_target="tpu_custom_call" | custom-call | tf_op jit(solution)/shard_map/pallas_call | solution.py:43
  33.6 24.3 %all_to_all.12 = f32[256,1,128]{2,1,0:T(1,128)S(1)} all-to-all(f32[256,1,128]{2,1,0:T(1,128)S(1)} %bitcast.7), channel_id=1, replica_groups=mesh['ctx'=8,'head'=4,'dp'=8] {'ctx','head','dp'}, dimensions={0} | all-to-all | bytes 262144 | tf_op jit(solution)/shard_map/all_to_all | solution.py:571
  57.8 0.6 %slice_reduce_fusion = f32[]{:T(128)} fusion(f32[256,128]{1,0:T(8,128)S(1)} %bitcast.11), kind=kLoop, calls=%fused_computation | loop fusion | flops 255 | bytes 1028 | tf_op jit(solution)/shard_map/reduce_sum | solution.py:572
  (1 shorter events, 0.0 us)
Async XLA Ops:
  0.6 5.9 %copy-start.1 = (bf16[1,256,896]{2,1,0:T(8,128)(2,1)S(1)}, bf16[1,256,896]{2,1,0:T(8,128)(2,1)}, u32[]{:S(2)}) copy-start(bf16[1,256,896]{2,1,0:T(8,128)(2,1)} %k.5) | copy-start | bytes 1376260
  0.6 5.9 %copy-start.8 = (f32[1,7,256]{2,0,1:T(1,128)S(1)}, f32[1,7,256]{2,0,1:T(1,128)}, u32[]{:S(2)}) copy-start(f32[1,7,256]{2,0,1:T(1,128)} %param.15) | copy-start | bytes 21508
  0.7 5.8 %copy-start.9 = (f32[1,7,256]{2,0,1:T(1,128)S(1)}, f32[1,7,256]{2,0,1:T(1,128)}, u32[]{:S(2)}) copy-start(f32[1,7,256]{2,0,1:T(1,128)} %param.16) | copy-start | bytes 21508
  2.3 8.9 %collective-permute-start.1 = (bf16[528,128]{1,0:T(8,128)(2,1)}, bf16[528,128]{1,0:T(8,128)(2,1)S(1)}, u32[]{:S(2)}, u32[]{:S(2)}) collective-permute-start(bf16[528,128]{1,0:T(8,128)(2,1)} %get-tuple-element.25.own), channel_id=1, source_target_pairs={{0,64},{32,96},{64,128},{96,160},{128,192},{160,224},{192,0},{224,... | collective-permute-start | bytes 405512 | tf_op jit(solution)/shard_map/ppermute | solution.py:436
  4.4 6.8 %collective-permute-start = (bf16[16,1024]{1,0:T(8,128)(2,1)}, bf16[16,1024]{1,0:T(8,128)(2,1)S(1)}, u32[]{:S(2)}, u32[]{:S(2)}) collective-permute-start(bf16[16,1024]{1,0:T(8,128)(2,1)} %get-tuple-element.21), channel_id=1, source_target_pairs={{0,32},{32,64},{64,96},{96,128},{128,160},{160,192},{192,224},{224... | collective-permute-start | bytes 98312 | tf_op jit(solution)/shard_map/ppermute | solution.py:436
  6.5 0.7 %copy-start.5 = (s32[1,256]{1,0:T(1,128)S(1)}, s32[1,256]{1,0:T(1,128)}, u32[]{:S(2)}) copy-start(s32[1,256]{1,0:T(1,128)} %ids.3) | copy-start | bytes 3076
  7.2 4.1 %copy-start = (bf16[1,256,896]{2,1,0:T(8,128)(2,1)S(1)}, bf16[1,256,896]{2,1,0:T(8,128)(2,1)}, u32[]{:S(2)}) copy-start(bf16[1,256,896]{2,1,0:T(8,128)(2,1)} %v.1) | copy-start | bytes 1376260
  7.2 4.1 %copy-start.3 = (f32[1,7,4,256]{3,2,1,0:T(4,128)S(1)}, f32[1,7,4,256]{3,2,1,0:T(4,128)}, u32[]{:S(2)}) copy-start(f32[1,7,4,256]{3,2,1,0:T(4,128)} %taps.1) | copy-start | bytes 86020
  12.9 3.4 %copy-start.7 = (bf16[528,128]{1,0:T(8,128)(2,1)S(1)}, bf16[528,128]{1,0:T(8,128)(2,1)}, u32[]{:S(2)}) copy-start(bf16[528,128]{1,0:T(8,128)(2,1)} %get-tuple-element.25.own) | copy-start | bytes 405508
  12.9 8.6 %copy-start.2 = (bf16[1,256,896]{2,1,0:T(8,128)(2,1)S(1)}, bf16[1,256,896]{2,1,0:T(8,128)(2,1)}, u32[]{:S(2)}) copy-start(bf16[1,256,896]{2,1,0:T(8,128)(2,1)} %q.2) | copy-start | bytes 1376260
  12.9 2.3 %collective-permute-start.2 = (bf16[14,128,128]{2,1,0:T(8,128)(2,1)S(1)}, bf16[14,128,128]{2,1,0:T(8,128)(2,1)S(1)}, u32[]{:S(2)}, u32[]{:S(2)}) collective-permute-start(bf16[14,128,128]{2,1,0:T(8,128)(2,1)S(1)} %get-tuple-element.26.own), channel_id=1, source_target_pairs={{0,32},{32,0},{64,96},{96,64},{128,160},{160,128},{192,224},{224,1... | collective-permute-start | bytes 1376264 | tf_op jit(solution)/shard_map/ppermute | solution.py:439
  13.8 6.4 %collective-permute-start.6 = (bf16[528,128]{1,0:T(8,128)(2,1)S(1)}, bf16[528,128]{1,0:T(8,128)(2,1)S(1)}, u32[]{:S(2)}, u32[]{:S(2)}) collective-permute-start(bf16[528,128]{1,0:T(8,128)(2,1)S(1)} %collective-permute-done.1.after.r2), channel_id=1, source_target_pairs={{0,64},{32,96},{64,128},{96,160},{128,192},{160,224},{192,0},{224,... | collective-permute-start | bytes 405512 | tf_op jit(solution)/shard_map/ppermute | solution.py:436
  15.5 6.0 %copy-start.4 = (f32[1,7,256]{2,0,1:T(1,128)S(1)}, f32[1,7,256]{2,0,1:T(1,128)}, u32[]{:S(2)}) copy-start(f32[1,7,256]{2,0,1:T(1,128)} %param.23) | copy-start | bytes 21508
  15.5 7.3 %collective-permute-start.3 = (bf16[7,64,128]{2,1,0:T(8,128)(2,1)S(1)}, bf16[7,64,128]{2,1,0:T(8,128)(2,1)S(1)}, u32[]{:S(2)}, u32[]{:S(2)}) collective-permute-start(bf16[7,64,128]{2,1,0:T(8,128)(2,1)S(1)} %get-tuple-element.28.i), channel_id=1, source_target_pairs={{0,64},{32,96},{64,128},{96,160},{128,192},{160,224},{192,0},{224,... | collective-permute-start | bytes 344072 | tf_op jit(solution)/shard_map/ppermute | solution.py:436
  16.3 8.7 %collective-permute-start.7 = (bf16[528,128]{1,0:T(8,128)(2,1)S(1)}, bf16[528,128]{1,0:T(8,128)(2,1)S(1)}, u32[]{:S(2)}, u32[]{:S(2)}) collective-permute-start(bf16[528,128]{1,0:T(8,128)(2,1)S(1)} %copy-done.7), channel_id=1, source_target_pairs={{0,32},{32,0},{64,96},{96,64},{128,160},{160,128},{192,224},{224,1... | collective-permute-start | bytes 405512 | tf_op jit(solution)/shard_map/ppermute | solution.py:439
  17.3 7.7 %collective-permute-start.8 = (bf16[528,128]{1,0:T(8,128)(2,1)S(1)}, bf16[528,128]{1,0:T(8,128)(2,1)S(1)}, u32[]{:S(2)}, u32[]{:S(2)}) collective-permute-start(bf16[528,128]{1,0:T(8,128)(2,1)S(1)} %collective-permute-done.1.after.r2), channel_id=1, source_target_pairs={{0,32},{32,0},{64,96},{96,64},{128,160},{160,128},{192,224},{224,1... | collective-permute-start | bytes 405512 | tf_op jit(solution)/shard_map/ppermute | solution.py:439
  20.1 4.9 %collective-permute-start.9 = (bf16[528,128]{1,0:T(8,128)(2,1)S(1)}, bf16[528,128]{1,0:T(8,128)(2,1)S(1)}, u32[]{:S(2)}, u32[]{:S(2)}) collective-permute-start(bf16[528,128]{1,0:T(8,128)(2,1)S(1)} %collective-permute-done.6.r4), channel_id=1, source_target_pairs={{0,32},{32,0},{64,96},{96,64},{128,160},{160,128},{192,224},{224,1... | collective-permute-start | bytes 405512 | tf_op jit(solution)/shard_map/ppermute | solution.py:439
  22.8 2.2 %copy-start.6 = (bf16[1,256,896]{2,1,0:T(8,128)(2,1)S(1)}, bf16[1,256,896]{2,1,0:T(8,128)(2,1)}, u32[]{:S(2)}) copy-start(bf16[1,256,896]{2,1,0:T(8,128)(2,1)} %q.3) | copy-start | bytes 1376260
  22.9 2.2 %copy-start.10 = (f32[896]{0:T(1024)S(1)}, f32[896]{0:T(1024)}, u32[]{:S(2)}) copy-start(f32[896]{0:T(1024)} %param.18) | copy-start | bytes 10756
  23.1 6.2 %collective-permute-start.4 = (bf16[7,64,128]{2,1,0:T(8,128)(2,1)S(1)}, bf16[7,64,128]{2,1,0:T(8,128)(2,1)S(1)}, u32[]{:S(2)}, u32[]{:S(2)}) collective-permute-start(bf16[7,64,128]{2,1,0:T(8,128)(2,1)S(1)} %shard_map.144), channel_id=1, source_target_pairs={{0,64},{32,96},{64,128},{96,160},{128,192},{160,224},{192,0},{224,... | collective-permute-start | bytes 344072 | tf_op jit(solution)/shard_map/ppermute | solution.py:436
  23.3 8.5 %collective-permute-start.5 = (bf16[7,64,128]{2,1,0:T(8,128)(2,1)S(1)}, bf16[7,64,128]{2,1,0:T(8,128)(2,1)S(1)}, u32[]{:S(2)}, u32[]{:S(2)}) collective-permute-start(bf16[7,64,128]{2,1,0:T(8,128)(2,1)S(1)} %shard_map.144), channel_id=1, source_target_pairs={{0,96},{32,64},{64,160},{96,128},{128,224},{160,192},{192,32},{224... | collective-permute-start | bytes 344072 | tf_op jit(solution)/shard_map/ppermute | solution.py:446

commit v4 on v3

--- a/solution.py
+++ b/solution.py
@@ -367,7 +367,7 @@
     return lax.rem(lax.axis_index("ctx"), 2) == 1
 
 
-def chip_body(own, other, m_out, i_out):
+def chip_body(own, other, after, m_out, i_out):
     heads, rows, _ = i_out.shape
     every = range(heads)
     odd = is_odd()
@@ -382,18 +382,17 @@
         i_out[h] = (ends[h] + later_i.astype(F32)).astype(BF16)
 
 
-def join_body(m, i, arriving, after, out):
+def join_body(m, i, arriving, out):
     every = range(m.shape[0])
     ends = [nn(arriving[h], m[h]) for h in every]
     for h in every:
         out[h] = (ends[h] + i[h].astype(F32)).astype(BF16)
 
 
-def finish_body(mine, theirs, other, local, reader, gain, teachers, lw, out, sums):
+def finish_body(mine, theirs, other, local, reader, gain, teachers, lw, out, sums, out_s, student_s, sems):
     heads = mine.shape[0]
     every = range(heads)
     odd = is_odd()
-    total = jnp.zeros(lw.shape, F32)
     states = []
     for h in every:
         a, b = mine[h], theirs[h]
@@ -402,15 +401,26 @@
     for h in every:
         step = (steps[h] + other[heads + h].astype(F32)).astype(BF16)
         states[h] = jnp.where(odd, step, states[h])
-    os = [local[h] + nt(reader[h], states[h]) for h in every]
-    for h in every:
-        mean = jnp.sum(os[h] * os[h], axis=1, keepdims=True) * (1.0 / HEAD)
-        student = os[h] * lax.rsqrt(mean + EPSILON) * gain[:, head_lanes(h)]
-        out[0, :, head_lanes(h)] = student.astype(BF16)
-        difference = student - teachers[:, head_lanes(h)]
+    half = lw.shape[0] // 2
+    moves = []
+    for r in range(2):
+        rows = slice(r * half, (r + 1) * half)
+        os = [local[h, rows] + nt(reader[h, rows], states[h]) for h in every]
+        for h in every:
+            mean = jnp.sum(os[h] * os[h], axis=1, keepdims=True) * (1.0 / HEAD)
+            student = os[h] * lax.rsqrt(mean + EPSILON) * gain[:, head_lanes(h)]
+            student_s[rows, head_lanes(h)] = student
+            out_s[rows, head_lanes(h)] = student.astype(BF16)
+        moves.append(pltpu.make_async_copy(out_s.at[rows], out.at[0, rows], sems.at[r]))
+        moves[r].start()
+    total = jnp.zeros(lw.shape, F32)
+    for h in every:
+        difference = student_s[:, head_lanes(h)] - teachers[:, head_lanes(h)]
         total = total + lw[:, h : h + 1] * (difference * difference)
     partial = jnp.sum(jnp.sum(total, axis=0, keepdims=True), axis=1, keepdims=True)
     sums[...] = jnp.broadcast_to(partial, sums.shape)
+    for move in moves:
+        move.wait()
 
 
 def on_device(
@@ -440,10 +450,6 @@
 
     def by_head(block):
         return block.reshape(heads, 1, tokens)
-
-    def crossed(block):
-        route = [(i, ((i + 2) % shards) ^ 1) for i in range(shards)]
-        return lax.ppermute(block, "ctx", route)
 
     kv, rim = call(
         pack_body,
@@ -523,6 +529,7 @@
         [((heads, HEAD, HEAD), BF16), ((heads, HEAD // 2, HEAD), BF16)],
         mi,
         mi_other,
+        lw,
     )
     behind = rotated(i_chip, 2)
     x4 = swapped(r4)
@@ -551,11 +558,12 @@
         )
 
     (joined,) = call(
-        join_body, [((heads, HEAD // 2, HEAD), BF16)], m_chip, i_chip, behind, lw
+        join_body, [((heads, HEAD // 2, HEAD), BF16)], m_chip, i_chip, behind
     )
     mine = rotated(joined, 2)
-    theirs = crossed(joined)
     teacher_out, teacher = attend(0, heads)
+    mine, teacher = lax.optimization_barrier((mine, teacher))
+    theirs = swapped(mine)
     student_out, sums = call(
         finish_body,
         [((1, tokens, features), BF16), ((everyone, 128), F32)],
@@ -567,6 +575,9 @@
         out_gain.reshape(1, features),
         teacher,
         lw,
+        scratch=[((tokens, features), BF16), ((tokens, features), F32)],
+        hbm_out=(0,),
+        copies=2,
     )
     gathered = lax.all_to_all(sums, ("ctx", "head", "dp"), 0, 0, tiled=True)
     loss = jnp.sum(gathered[:, 0]) / (everyone * heads * tokens * HEAD)

time: 60.4 us -> 60.1 us (level)
  waiting for transfers between devices: 6.65 us -> 4.15 us
  starting transfers between devices: 10.3 us -> 11.9 us
  blocking collectives: 24.3 us -> 25.1 us
    ppermute x1 -> x0, waiting for transfers between devices: 2.56 us -> none  [crossed(): return lax.ppermute(block, 'ctx', route)]
    ppermute x4 -> x5, starting transfers between devices: 3.19 us -> 5.17 us  [swapped(): return lax.ppermute(block, 'ctx', [(i, i ^ 1) for i in range(shards)])]
    ppermute x1 -> x0, starting transfers between devices: 1.69 us -> none  [crossed(): return lax.ppermute(block, 'ctx', route)]
    ppermute x5, starting transfers between devices: 5.45 us -> 6.68 us  [rotated(): lax.ppermute(block, 'ctx', [(i, (i + distance) % shards) for i in range(s...]
    all_to_all x1, blocking collectives: 24.3 us -> 25.1 us  [on_device(): gathered = lax.all_to_all(sums, ('ctx', 'head', 'dp'), 0, 0, tiled=True)]
    ppermute x4 -> x5, waiting for transfers between devices: 1.23 us -> 0.97 us  [swapped(): return lax.ppermute(block, 'ctx', [(i, i ^ 1) for i in range(shards)])]
  transfers between devices with their start and end apart: 10 -> 10, of which waited for: 3 -> 4; matrix products, arithmetic and copies ran while one was open for 0% -> 0% of each run, Pallas kernels for 17% -> 17%
where the time goes in v4:
time: 60.1 us; the launch traced here: 60 us
  blocking collectives  25.1 us (42%)
  Pallas kernels  14.9 us (25%)
  starting transfers between devices  11.9 us (20%)
  waiting for transfers between devices  4.15 us (7%)
  between operations  2.59 us (4%)
  local copies, waits for them, and re-layouts  0.72 us (1%)
  other arithmetic  0.63 us (1%)
    all_to_all x1, blocking collectives, on_device(): gathered = lax.all_to_all(sums, ('ctx', 'head', 'dp'), 0, 0, tiled=True)  25.1 us
    pallas_call x8, Pallas kernels, call(): pl.pallas_call(body, out_shape=[jax.ShapeDtypeStruct(s, d) for s, d in ou...  14.9 us
    ppermute x5, starting transfers between devices, rotated(): lax.ppermute(block, 'ctx', [(i, (i + distance) % shards) for i in range(s...  6.68 us
    ppermute x5, starting transfers between devices, swapped(): return lax.ppermute(block, 'ctx', [(i, i ^ 1) for i in range(shards)])  5.17 us
    ppermute x5, waiting for transfers between devices, rotated(): lax.ppermute(block, 'ctx', [(i, (i + distance) % shards) for i in range(s...  3.18 us
  transfers between devices with their start and end apart: 10, of which 4 were waited for; matrix products, arithmetic and copies ran while one was open for 0% of the time, Pallas kernels for 17%

profile of v4, /device:TPU:1, one launch (start us, length us, event | category | flops | bytes accessed | tf_op | source)
XLA Modules:
  0.0 60.0 jit_solution(10426628457906715722)
XLA Ops:
  0.6 0.0 copy-start.1
  0.6 0.0 copy-start.8
  0.7 0.0 copy-start.9
  0.7 1.7 %shard_map.139 = (bf16[528,128]{1,0:T(8,128)(2,1)}, bf16[16,1024]{1,0:T(8,128)(2,1)}) custom-call(bf16[1,256,128]{2,1,0:T(8,128)(2,1)} %tk.1, bf16[1,256,128]{2,1,0:T(8,128)(2,1)} %tv.1, bf16[1,256,896]{2,1,0:T(8,128)(2,1)} %v.1, s32[1,256]{1,0:T(1,128)} %ids.3), custom_call_target="tpu_custom_call" | custom-call | tf_op jit(solution)/shard_map/pallas_call | solution.py:43
  2.3 2.1 %collective-permute-start.1 = (bf16[528,128]{1,0:T(8,128)(2,1)}, bf16[528,128]{1,0:T(8,128)(2,1)S(1)}, u32[]{:S(2)}, u32[]{:S(2)}) collective-permute-start(bf16[528,128]{1,0:T(8,128)(2,1)} %get-tuple-element.27.own), channel_id=1, source_target_pairs={{0,64},{32,96},{64,128},{96,160},{128,192},{160,224},{192,0},{224,... | collective-permute-start | bytes 405512 | tf_op jit(solution)/shard_map/ppermute | solution.py:446
  4.4 2.1 %collective-permute-start = (bf16[16,1024]{1,0:T(8,128)(2,1)}, bf16[16,1024]{1,0:T(8,128)(2,1)S(1)}, u32[]{:S(2)}, u32[]{:S(2)}) collective-permute-start(bf16[16,1024]{1,0:T(8,128)(2,1)} %get-tuple-element.23), channel_id=1, source_target_pairs={{0,32},{32,64},{64,96},{96,128},{128,160},{160,192},{192,224},{224... | collective-permute-start | bytes 98312 | tf_op jit(solution)/shard_map/ppermute | solution.py:446
  6.5 0.0 copy-start.5
  6.5 0.0 copy-done.1
  6.5 0.0 copy-done.8
  6.5 0.0 copy-done.9
  6.5 0.7 %copy-done.5 = s32[1,256]{1,0:T(1,128)S(1)} copy-done((s32[1,256]{1,0:T(1,128)S(1)}, s32[1,256]{1,0:T(1,128)}, u32[]{:S(2)}) %copy-start.5) | copy-done | bytes 1048
  7.2 0.0 copy-start
  7.2 0.0 copy-start.3
  7.2 4.1 %shard_map.140 = (bf16[7,256,256]{2,1,0:T(8,128)(2,1)S(1)}, bf16[7,128,256]{2,1,0:T(8,128)(2,1)S(1)}, f32[7,128,128]{2,1,0:T(8,128)S(1)}, f32[32,256]{1,0:T(8,128)S(1)}, f32[256,128]{1,0:T(8,128)S(1)}) custom-call(bf16[1,256,896]{2,1,0:T(8,128)(2,1)S(1)} %copy-done.1, f32[7,1,256]{2,1,0:T(1,128)S(1)} %bitcast.9, f32[7,1,256]{2,1,0:T(1,128)S(1)} %bitcast.10, ...), custom_call_target="tpu_custom_call" | custom-call | flops 500000000 | tf_op jit(solution)/shard_map/pallas_call | solution.py:43
  11.3 0.0 collective-permute-done.rim
  11.3 0.0 collective-permute-done.1.after.r2
  11.3 0.0 copy-done
  11.3 0.0 copy-done.3
  11.3 0.0 copy-start.2
  11.3 1.6 %shard_map.141 = (bf16[14,128,128]{2,1,0:T(8,128)(2,1)S(1)}, bf16[7,128,256]{2,1,0:T(8,128)(2,1)S(1)}) custom-call(bf16[1,256,896]{2,1,0:T(8,128)(2,1)S(1)} %copy-done, bf16[16,1024]{1,0:T(8,128)(2,1)S(1)} %collective-permute-done.rim, f32[1,7,4,256]{3,2,1,0:T(4,128)S(1)} %copy-done.3, f32[32,256]{1,0:T(8,128)S(1)} %get-tuple-element.24.rows, ...), custom_call_target="tpu_custom_call" | custom-call | flops 200000000 | tf_op jit(solution)/shard_map/pallas_call | solution.py:43
  12.9 0.0 copy-start.4
  12.9 0.9 %collective-permute-start.2 = (bf16[14,128,128]{2,1,0:T(8,128)(2,1)S(1)}, bf16[14,128,128]{2,1,0:T(8,128)(2,1)S(1)}, u32[]{:S(2)}, u32[]{:S(2)}) collective-permute-start(bf16[14,128,128]{2,1,0:T(8,128)(2,1)S(1)} %get-tuple-element.28.own), channel_id=1, source_target_pairs={{0,32},{32,0},{64,96},{96,64},{128,160},{160,128},{192,224},{224,1... | collective-permute-start | bytes 1376264 | tf_op jit(solution)/shard_map/ppermute | solution.py:449
  13.8 0.2 collective-permute-start.5
  14.0 0.0 copy-done.2
  14.0 0.0 copy-done.4
  14.0 1.4 %shard_map.142 = (f32[7,256,128]{2,1,0:T(8,128)S(1)}, bf16[7,256,128]{2,1,0:T(8,128)(2,1)S(1)}, f32[256,128]{1,0:T(8,128)S(1)}) custom-call(bf16[1,256,896]{2,1,0:T(8,128)(2,1)S(1)} %copy-done.2, bf16[1,256,896]{2,1,0:T(8,128)(2,1)S(1)} %copy-done.1, bf16[16,1024]{1,0:T(8,128)(2,1)S(1)} %collective-permute-done.rim, f32[32,256]{1,0:T(8,128)S(1)} %get-tuple-element.24.rows, ...), custom_call_target="tpu_custom_call" | custom-call | flops 200000000 | tf_op jit(solution)/shard_map/pallas_call | solution.py:43
  15.4 0.0 collective-permute-done.2.other
  15.4 0.0 copy-start.7
  15.4 0.3 shard_map.143
  15.7 0.0 copy-start.6
  15.7 2.0 %collective-permute-start.3 = (bf16[7,64,128]{2,1,0:T(8,128)(2,1)S(1)}, bf16[7,64,128]{2,1,0:T(8,128)(2,1)S(1)}, u32[]{:S(2)}, u32[]{:S(2)}) collective-permute-start(bf16[7,64,128]{2,1,0:T(8,128)(2,1)S(1)} %get-tuple-element.34.i), channel_id=1, source_target_pairs={{0,64},{32,96},{64,128},{96,160},{128,192},{160,224},{192,0},{224,... | collective-permute-start | bytes 344072 | tf_op jit(solution)/shard_map/ppermute | solution.py:446
  17.7 0.0 copy-done.7
  17.7 1.0 %collective-permute-start.6 = (bf16[528,128]{1,0:T(8,128)(2,1)S(1)}, bf16[528,128]{1,0:T(8,128)(2,1)S(1)}, u32[]{:S(2)}, u32[]{:S(2)}) collective-permute-start(bf16[528,128]{1,0:T(8,128)(2,1)S(1)} %copy-done.7), channel_id=1, source_target_pairs={{0,32},{32,0},{64,96},{96,64},{128,160},{160,128},{192,224},{224,1... | collective-permute-start | bytes 405512 | tf_op jit(solution)/shard_map/ppermute | solution.py:449
  18.7 0.0 collective-permute-start.7
  18.7 1.4 %collective-permute-done.5.r4 = bf16[528,128]{1,0:T(8,128)(2,1)S(1)} collective-permute-done((bf16[528,128]{1,0:T(8,128)(2,1)S(1)}, bf16[528,128]{1,0:T(8,128)(2,1)S(1)}, u32[]{:S(2)}, u32[]{:S(2)}) %collective-permute-start.5) | collective-permute-done | bytes 135200 | tf_op jit(solution)/shard_map/ppermute | solution.py:446
  20.1 1.3 %collective-permute-start.8 = (bf16[528,128]{1,0:T(8,128)(2,1)S(1)}, bf16[528,128]{1,0:T(8,128)(2,1)S(1)}, u32[]{:S(2)}, u32[]{:S(2)}) collective-permute-start(bf16[528,128]{1,0:T(8,128)(2,1)S(1)} %collective-permute-done.5.r4), channel_id=1, source_target_pairs={{0,32},{32,0},{64,96},{96,64},{128,160},{160,128},{192,224},{224,1... | collective-permute-start | bytes 405512 | tf_op jit(solution)/shard_map/ppermute | solution.py:449
  21.5 1.1 %collective-permute-done.3.arriving = bf16[7,64,128]{2,1,0:T(8,128)(2,1)S(1)} collective-permute-done((bf16[7,64,128]{2,1,0:T(8,128)(2,1)S(1)}, bf16[7,64,128]{2,1,0:T(8,128)(2,1)S(1)}, u32[]{:S(2)}, u32[]{:S(2)}) %collective-permute-start.3) | collective-permute-done | bytes 114720 | tf_op jit(solution)/shard_map/ppermute | solution.py:446
  22.6 0.2 shard_map.144
  22.8 0.3 collective-permute-start.4
  23.1 0.0 collective-permute-done.6.x0
  23.1 0.0 collective-permute-done.7.x2
  23.1 0.0 collective-permute-done.8.x4
  23.1 0.0 copy-done.6
  23.1 0.0 copy-start.10
  23.1 4.2 %shard_map.145 = (bf16[1,256,896]{2,1,0:T(8,128)(2,1)}, f32[256,896]{1,0:T(8,128)S(1)}) custom-call(bf16[1,256,896]{2,1,0:T(8,128)(2,1)S(1)} %copy-done.6, f32[256,128]{1,0:T(8,128)S(1)} %get-tuple-element.29.cols_in, bf16[528,128]{1,0:T(8,128)(2,1)S(1)} %copy-done.7, bf16[528,128]{1,0:T(8,128)(2,1)S(1)} %collective-permute-done.1.after.r2, ...), custom_call_target="tpu_custom_call" | custom-call | flops 700000000 | tf_op jit(solution)/shard_map/pallas_call | solution.py:43
  27.3 0.6 %collective-permute-done.4.mine = bf16[7,64,128]{2,1,0:T(8,128)(2,1)S(1)} collective-permute-done((bf16[7,64,128]{2,1,0:T(8,128)(2,1)S(1)}, bf16[7,64,128]{2,1,0:T(8,128)(2,1)S(1)}, u32[]{:S(2)}, u32[]{:S(2)}) %collective-permute-start.4) | collective-permute-done | bytes 114720 | tf_op jit(solution)/shard_map/ppermute | solution.py:446
  27.9 2.0 %collective-permute-start.9 = (bf16[7,64,128]{2,1,0:T(8,128)(2,1)S(1)}, bf16[7,64,128]{2,1,0:T(8,128)(2,1)S(1)}, u32[]{:S(2)}, u32[]{:S(2)}) collective-permute-start(bf16[7,64,128]{2,1,0:T(8,128)(2,1)S(1)} %collective-permute-done.4.mine), channel_id=1, source_target_pairs={{0,32},{32,0},{64,96},{96,64},{128,160},{160,128},{192,224},{224,1... | collective-permute-start | bytes 344072 | tf_op jit(solution)/shard_map/ppermute | solution.py:449
  29.9 0.0 copy-done.10
  29.9 1.0 %collective-permute-done.9.theirs = bf16[7,64,128]{2,1,0:T(8,128)(2,1)S(1)} collective-permute-done((bf16[7,64,128]{2,1,0:T(8,128)(2,1)S(1)}, bf16[7,64,128]{2,1,0:T(8,128)(2,1)S(1)}, u32[]{:S(2)}, u32[]{:S(2)}) %collective-permute-start.9) | collective-permute-done | bytes 114720 | tf_op jit(solution)/shard_map/ppermute | solution.py:449
  30.9 1.5 %shard_map.146 = (bf16[1,256,896]{2,1,0:T(8,128)(2,1)}, f32[256,128]{1,0:T(8,128)S(1)}) custom-call(bf16[7,64,128]{2,1,0:T(8,128)(2,1)S(1)} %collective-permute-done.4.mine, bf16[7,64,128]{2,1,0:T(8,128)(2,1)S(1)} %collective-permute-done.9.theirs, bf16[14,128,128]{2,1,0:T(8,128)(2,1)S(1)} %collective-permute-done.2.other, ...), custom_call_target="tpu_custom_call" | custom-call | tf_op jit(solution)/shard_map/pallas_call | solution.py:43
  32.4 25.1 %all_to_all.12 = f32[256,1,128]{2,1,0:T(1,128)S(1)} all-to-all(f32[256,1,128]{2,1,0:T(1,128)S(1)} %bitcast.7), channel_id=1, replica_groups=mesh['ctx'=8,'head'=4,'dp'=8] {'ctx','head','dp'}, dimensions={0} | all-to-all | bytes 262144 | tf_op jit(solution)/shard_map/all_to_all | solution.py:582
  57.5 0.6 %slice_reduce_fusion = f32[]{:T(128)} fusion(f32[256,128]{1,0:T(8,128)S(1)} %bitcast.11), kind=kLoop, calls=%fused_computation | loop fusion | flops 255 | bytes 1028 | tf_op jit(solution)/shard_map/reduce_sum | solution.py:583
  (1 shorter events, 0.0 us)
Async XLA Ops:
  0.6 5.9 %copy-start.1 = (bf16[1,256,896]{2,1,0:T(8,128)(2,1)S(1)}, bf16[1,256,896]{2,1,0:T(8,128)(2,1)}, u32[]{:S(2)}) copy-start(bf16[1,256,896]{2,1,0:T(8,128)(2,1)} %k.5) | copy-start | bytes 1376260
  0.6 5.9 %copy-start.8 = (f32[1,7,256]{2,0,1:T(1,128)S(1)}, f32[1,7,256]{2,0,1:T(1,128)}, u32[]{:S(2)}) copy-start(f32[1,7,256]{2,0,1:T(1,128)} %param.15) | copy-start | bytes 21508
  0.7 5.8 %copy-start.9 = (f32[1,7,256]{2,0,1:T(1,128)S(1)}, f32[1,7,256]{2,0,1:T(1,128)}, u32[]{:S(2)}) copy-start(f32[1,7,256]{2,0,1:T(1,128)} %param.16) | copy-start | bytes 21508
  2.3 8.9 %collective-permute-start.1 = (bf16[528,128]{1,0:T(8,128)(2,1)}, bf16[528,128]{1,0:T(8,128)(2,1)S(1)}, u32[]{:S(2)}, u32[]{:S(2)}) collective-permute-start(bf16[528,128]{1,0:T(8,128)(2,1)} %get-tuple-element.27.own), channel_id=1, source_target_pairs={{0,64},{32,96},{64,128},{96,160},{128,192},{160,224},{192,0},{224,... | collective-permute-start | bytes 405512 | tf_op jit(solution)/shard_map/ppermute | solution.py:446
  4.4 6.8 %collective-permute-start = (bf16[16,1024]{1,0:T(8,128)(2,1)}, bf16[16,1024]{1,0:T(8,128)(2,1)S(1)}, u32[]{:S(2)}, u32[]{:S(2)}) collective-permute-start(bf16[16,1024]{1,0:T(8,128)(2,1)} %get-tuple-element.23), channel_id=1, source_target_pairs={{0,32},{32,64},{64,96},{96,128},{128,160},{160,192},{192,224},{224... | collective-permute-start | bytes 98312 | tf_op jit(solution)/shard_map/ppermute | solution.py:446
  6.5 0.7 %copy-start.5 = (s32[1,256]{1,0:T(1,128)S(1)}, s32[1,256]{1,0:T(1,128)}, u32[]{:S(2)}) copy-start(s32[1,256]{1,0:T(1,128)} %ids.3) | copy-start | bytes 3076
  7.2 4.1 %copy-start = (bf16[1,256,896]{2,1,0:T(8,128)(2,1)S(1)}, bf16[1,256,896]{2,1,0:T(8,128)(2,1)}, u32[]{:S(2)}) copy-start(bf16[1,256,896]{2,1,0:T(8,128)(2,1)} %v.1) | copy-start | bytes 1376260
  7.2 4.1 %copy-start.3 = (f32[1,7,4,256]{3,2,1,0:T(4,128)S(1)}, f32[1,7,4,256]{3,2,1,0:T(4,128)}, u32[]{:S(2)}) copy-start(f32[1,7,4,256]{3,2,1,0:T(4,128)} %taps.1) | copy-start | bytes 86020
  11.3 2.7 %copy-start.2 = (bf16[1,256,896]{2,1,0:T(8,128)(2,1)S(1)}, bf16[1,256,896]{2,1,0:T(8,128)(2,1)}, u32[]{:S(2)}) copy-start(bf16[1,256,896]{2,1,0:T(8,128)(2,1)} %q.2) | copy-start | bytes 1376260
  12.9 1.1 %copy-start.4 = (f32[1,7,256]{2,0,1:T(1,128)S(1)}, f32[1,7,256]{2,0,1:T(1,128)}, u32[]{:S(2)}) copy-start(f32[1,7,256]{2,0,1:T(1,128)} %param.23) | copy-start | bytes 21508
  12.9 2.5 %collective-permute-start.2 = (bf16[14,128,128]{2,1,0:T(8,128)(2,1)S(1)}, bf16[14,128,128]{2,1,0:T(8,128)(2,1)S(1)}, u32[]{:S(2)}, u32[]{:S(2)}) collective-permute-start(bf16[14,128,128]{2,1,0:T(8,128)(2,1)S(1)} %get-tuple-element.28.own), channel_id=1, source_target_pairs={{0,32},{32,0},{64,96},{96,64},{128,160},{160,128},{192,224},{224,1... | collective-permute-start | bytes 1376264 | tf_op jit(solution)/shard_map/ppermute | solution.py:449
  13.8 6.4 %collective-permute-start.5 = (bf16[528,128]{1,0:T(8,128)(2,1)S(1)}, bf16[528,128]{1,0:T(8,128)(2,1)S(1)}, u32[]{:S(2)}, u32[]{:S(2)}) collective-permute-start(bf16[528,128]{1,0:T(8,128)(2,1)S(1)} %collective-permute-done.1.after.r2), channel_id=1, source_target_pairs={{0,64},{32,96},{64,128},{96,160},{128,192},{160,224},{192,0},{224,... | collective-permute-start | bytes 405512 | tf_op jit(solution)/shard_map/ppermute | solution.py:446
  15.4 2.3 %copy-start.7 = (bf16[528,128]{1,0:T(8,128)(2,1)S(1)}, bf16[528,128]{1,0:T(8,128)(2,1)}, u32[]{:S(2)}) copy-start(bf16[528,128]{1,0:T(8,128)(2,1)} %get-tuple-element.27.own) | copy-start | bytes 405508
  15.7 7.4 %copy-start.6 = (bf16[1,256,896]{2,1,0:T(8,128)(2,1)S(1)}, bf16[1,256,896]{2,1,0:T(8,128)(2,1)}, u32[]{:S(2)}) copy-start(bf16[1,256,896]{2,1,0:T(8,128)(2,1)} %q.3) | copy-start | bytes 1376260
  15.7 6.9 %collective-permute-start.3 = (bf16[7,64,128]{2,1,0:T(8,128)(2,1)S(1)}, bf16[7,64,128]{2,1,0:T(8,128)(2,1)S(1)}, u32[]{:S(2)}, u32[]{:S(2)}) collective-permute-start(bf16[7,64,128]{2,1,0:T(8,128)(2,1)S(1)} %get-tuple-element.34.i), channel_id=1, source_target_pairs={{0,64},{32,96},{64,128},{96,160},{128,192},{160,224},{192,0},{224,... | collective-permute-start | bytes 344072 | tf_op jit(solution)/shard_map/ppermute | solution.py:446
  17.7 5.3 %collective-permute-start.6 = (bf16[528,128]{1,0:T(8,128)(2,1)S(1)}, bf16[528,128]{1,0:T(8,128)(2,1)S(1)}, u32[]{:S(2)}, u32[]{:S(2)}) collective-permute-start(bf16[528,128]{1,0:T(8,128)(2,1)S(1)} %copy-done.7), channel_id=1, source_target_pairs={{0,32},{32,0},{64,96},{96,64},{128,160},{160,128},{192,224},{224,1... | collective-permute-start | bytes 405512 | tf_op jit(solution)/shard_map/ppermute | solution.py:449
  18.7 4.4 %collective-permute-start.7 = (bf16[528,128]{1,0:T(8,128)(2,1)S(1)}, bf16[528,128]{1,0:T(8,128)(2,1)S(1)}, u32[]{:S(2)}, u32[]{:S(2)}) collective-permute-start(bf16[528,128]{1,0:T(8,128)(2,1)S(1)} %collective-permute-done.1.after.r2), channel_id=1, source_target_pairs={{0,32},{32,0},{64,96},{96,64},{128,160},{160,128},{192,224},{224,1... | collective-permute-start | bytes 405512 | tf_op jit(solution)/shard_map/ppermute | solution.py:449
  20.1 3.0 %collective-permute-start.8 = (bf16[528,128]{1,0:T(8,128)(2,1)S(1)}, bf16[528,128]{1,0:T(8,128)(2,1)S(1)}, u32[]{:S(2)}, u32[]{:S(2)}) collective-permute-start(bf16[528,128]{1,0:T(8,128)(2,1)S(1)} %collective-permute-done.5.r4), channel_id=1, source_target_pairs={{0,32},{32,0},{64,96},{96,64},{128,160},{160,128},{192,224},{224,1... | collective-permute-start | bytes 405512 | tf_op jit(solution)/shard_map/ppermute | solution.py:449
  22.8 5.1 %collective-permute-start.4 = (bf16[7,64,128]{2,1,0:T(8,128)(2,1)S(1)}, bf16[7,64,128]{2,1,0:T(8,128)(2,1)S(1)}, u32[]{:S(2)}, u32[]{:S(2)}) collective-permute-start(bf16[7,64,128]{2,1,0:T(8,128)(2,1)S(1)} %shard_map.144), channel_id=1, source_target_pairs={{0,64},{32,96},{64,128},{96,160},{128,192},{160,224},{192,0},{224,... | collective-permute-start | bytes 344072 | tf_op jit(solution)/shard_map/ppermute | solution.py:446
  23.1 6.8 %copy-start.10 = (f32[896]{0:T(1024)S(1)}, f32[896]{0:T(1024)}, u32[]{:S(2)}) copy-start(f32[896]{0:T(1024)} %param.18) | copy-start | bytes 10756
  27.9 3.0 %collective-permute-start.9 = (bf16[7,64,128]{2,1,0:T(8,128)(2,1)S(1)}, bf16[7,64,128]{2,1,0:T(8,128)(2,1)S(1)}, u32[]{:S(2)}, u32[]{:S(2)}) collective-permute-start(bf16[7,64,128]{2,1,0:T(8,128)(2,1)S(1)} %collective-permute-done.4.mine), channel_id=1, source_target_pairs={{0,32},{32,0},{64,96},{96,64},{128,160},{160,128},{192,224},{224,1... | collective-permute-start | bytes 344072 | tf_op jit(solution)/shard_map/ppermute | solution.py:449

commit v5 on v4

--- a/solution.py
+++ b/solution.py
@@ -423,6 +423,10 @@
         move.wait()
 
 
+def total_body(scale, parts, out):
+    out[...] = jnp.sum(parts[:, 0:1], axis=0, keepdims=True) * scale
+
+
 def on_device(
     student_q,
     student_k,
@@ -580,7 +584,9 @@
         copies=2,
     )
     gathered = lax.all_to_all(sums, ("ctx", "head", "dp"), 0, 0, tiled=True)
-    loss = jnp.sum(gathered[:, 0]) / (everyone * heads * tokens * HEAD)
+    scale = 1.0 / (everyone * heads * tokens * HEAD)
+    (loss,) = call(functools.partial(total_body, scale), [((1, 1), F32)], gathered)
+    loss = loss.reshape(())
     return (student_out, teacher_out, loss)
 
 

time: 60.1 us -> 58.3 us (0.970)
  between operations: 2.59 us -> 0.81 us
  other arithmetic: 0.63 us -> 0 us
    reduce_sum x1 -> x0, other arithmetic: 0.63 us -> none  [on_device(): loss = jnp.sum(gathered[:, 0]) / (everyone * heads * tokens * HEAD)]
    pallas_call x8 -> x9, Pallas kernels: 14.9 us -> 15.5 us  [call(): pl.pallas_call(body, out_shape=[jax.ShapeDtypeStruct(s, d) for s, d in ou...]
where the time goes in v5:
time: 58.3 us; the launch traced here: 58.1 us
  blocking collectives  25.1 us (43%)
  Pallas kernels  15.5 us (27%)
  starting transfers between devices  11.9 us (20%)
  waiting for transfers between devices  4.15 us (7%)
  between operations  0.81 us (1%)
  local copies, waits for them, and re-layouts  0.72 us (1%)
    all_to_all x1, blocking collectives, on_device(): gathered = lax.all_to_all(sums, ('ctx', 'head', 'dp'), 0, 0, tiled=True)  25.1 us
    pallas_call x9, Pallas kernels, call(): pl.pallas_call(body, out_shape=[jax.ShapeDtypeStruct(s, d) for s, d in ou...  15.5 us
    ppermute x5, starting transfers between devices, rotated(): lax.ppermute(block, 'ctx', [(i, (i + distance) % shards) for i in range(s...  6.68 us
    ppermute x5, starting transfers between devices, swapped(): return lax.ppermute(block, 'ctx', [(i, i ^ 1) for i in range(shards)])  5.17 us
    ppermute x5, waiting for transfers between devices, rotated(): lax.ppermute(block, 'ctx', [(i, (i + distance) % shards) for i in range(s...  3.18 us
  transfers between devices with their start and end apart: 10, of which 4 were waited for; matrix products, arithmetic and copies ran while one was open for 0% of the time, Pallas kernels for 17%

profile of v5, /device:TPU:1, one launch (start us, length us, event | category | flops | bytes accessed | tf_op | source)
XLA Modules:
  0.0 58.1 jit_solution(7329839059571227432)
XLA Ops:
  0.6 0.0 copy-start.1
  0.6 0.0 copy-start.8
  0.7 0.0 copy-start.9
  0.7 1.7 %shard_map.139 = (bf16[528,128]{1,0:T(8,128)(2,1)}, bf16[16,1024]{1,0:T(8,128)(2,1)}) custom-call(bf16[1,256,128]{2,1,0:T(8,128)(2,1)} %tk.1, bf16[1,256,128]{2,1,0:T(8,128)(2,1)} %tv.1, bf16[1,256,896]{2,1,0:T(8,128)(2,1)} %v.1, s32[1,256]{1,0:T(1,128)} %ids.3), custom_call_target="tpu_custom_call" | custom-call | tf_op jit(solution)/shard_map/pallas_call | solution.py:43
  2.3 2.1 %collective-permute-start.1 = (bf16[528,128]{1,0:T(8,128)(2,1)}, bf16[528,128]{1,0:T(8,128)(2,1)S(1)}, u32[]{:S(2)}, u32[]{:S(2)}) collective-permute-start(bf16[528,128]{1,0:T(8,128)(2,1)} %get-tuple-element.27.own), channel_id=1, source_target_pairs={{0,64},{32,96},{64,128},{96,160},{128,192},{160,224},{192,0},{224,... | collective-permute-start | bytes 405512 | tf_op jit(solution)/shard_map/ppermute | solution.py:450
  4.4 2.1 %collective-permute-start = (bf16[16,1024]{1,0:T(8,128)(2,1)}, bf16[16,1024]{1,0:T(8,128)(2,1)S(1)}, u32[]{:S(2)}, u32[]{:S(2)}) collective-permute-start(bf16[16,1024]{1,0:T(8,128)(2,1)} %get-tuple-element.23), channel_id=1, source_target_pairs={{0,32},{32,64},{64,96},{96,128},{128,160},{160,192},{192,224},{224... | collective-permute-start | bytes 98312 | tf_op jit(solution)/shard_map/ppermute | solution.py:450
  6.5 0.0 copy-start.5
  6.5 0.0 copy-done.1
  6.5 0.0 copy-done.8
  6.5 0.0 copy-done.9
  6.5 0.7 %copy-done.5 = s32[1,256]{1,0:T(1,128)S(1)} copy-done((s32[1,256]{1,0:T(1,128)S(1)}, s32[1,256]{1,0:T(1,128)}, u32[]{:S(2)}) %copy-start.5) | copy-done | bytes 1048
  7.2 0.0 copy-start
  7.2 0.0 copy-start.3
  7.2 4.1 %shard_map.140 = (bf16[7,256,256]{2,1,0:T(8,128)(2,1)S(1)}, bf16[7,128,256]{2,1,0:T(8,128)(2,1)S(1)}, f32[7,128,128]{2,1,0:T(8,128)S(1)}, f32[32,256]{1,0:T(8,128)S(1)}, f32[256,128]{1,0:T(8,128)S(1)}) custom-call(bf16[1,256,896]{2,1,0:T(8,128)(2,1)S(1)} %copy-done.1, f32[7,1,256]{2,1,0:T(1,128)S(1)} %bitcast.11, f32[7,1,256]{2,1,0:T(1,128)S(1)} %bitcast.12, ...), custom_call_target="tpu_custom_call" | custom-call | flops 500000000 | tf_op jit(solution)/shard_map/pallas_call | solution.py:43
  11.3 0.0 collective-permute-done.rim
  11.3 0.0 collective-permute-done.1.after.r2
  11.3 0.0 copy-done
  11.3 0.0 copy-done.3
  11.3 0.0 copy-start.2
  11.3 1.6 %shard_map.141 = (bf16[14,128,128]{2,1,0:T(8,128)(2,1)S(1)}, bf16[7,128,256]{2,1,0:T(8,128)(2,1)S(1)}) custom-call(bf16[1,256,896]{2,1,0:T(8,128)(2,1)S(1)} %copy-done, bf16[16,1024]{1,0:T(8,128)(2,1)S(1)} %collective-permute-done.rim, f32[1,7,4,256]{3,2,1,0:T(4,128)S(1)} %copy-done.3, f32[32,256]{1,0:T(8,128)S(1)} %get-tuple-element.24.rows, ...), custom_call_target="tpu_custom_call" | custom-call | flops 200000000 | tf_op jit(solution)/shard_map/pallas_call | solution.py:43
  12.9 0.0 copy-start.4
  12.9 0.9 %collective-permute-start.2 = (bf16[14,128,128]{2,1,0:T(8,128)(2,1)S(1)}, bf16[14,128,128]{2,1,0:T(8,128)(2,1)S(1)}, u32[]{:S(2)}, u32[]{:S(2)}) collective-permute-start(bf16[14,128,128]{2,1,0:T(8,128)(2,1)S(1)} %get-tuple-element.28.own), channel_id=1, source_target_pairs={{0,32},{32,0},{64,96},{96,64},{128,160},{160,128},{192,224},{224,1... | collective-permute-start | bytes 1376264 | tf_op jit(solution)/shard_map/ppermute | solution.py:453
  13.8 0.2 collective-permute-start.5
  14.0 0.0 copy-done.2
  14.0 0.0 copy-done.4
  14.0 1.4 %shard_map.142 = (f32[7,256,128]{2,1,0:T(8,128)S(1)}, bf16[7,256,128]{2,1,0:T(8,128)(2,1)S(1)}, f32[256,128]{1,0:T(8,128)S(1)}) custom-call(bf16[1,256,896]{2,1,0:T(8,128)(2,1)S(1)} %copy-done.2, bf16[1,256,896]{2,1,0:T(8,128)(2,1)S(1)} %copy-done.1, bf16[16,1024]{1,0:T(8,128)(2,1)S(1)} %collective-permute-done.rim, f32[32,256]{1,0:T(8,128)S(1)} %get-tuple-element.24.rows, ...), custom_call_target="tpu_custom_call" | custom-call | flops 200000000 | tf_op jit(solution)/shard_map/pallas_call | solution.py:43
  15.4 0.0 collective-permute-done.2.other
  15.4 0.0 copy-start.7
  15.4 0.3 shard_map.143
  15.7 0.0 copy-start.6
  15.7 2.0 %collective-permute-start.3 = (bf16[7,64,128]{2,1,0:T(8,128)(2,1)S(1)}, bf16[7,64,128]{2,1,0:T(8,128)(2,1)S(1)}, u32[]{:S(2)}, u32[]{:S(2)}) collective-permute-start(bf16[7,64,128]{2,1,0:T(8,128)(2,1)S(1)} %get-tuple-element.34.i), channel_id=1, source_target_pairs={{0,64},{32,96},{64,128},{96,160},{128,192},{160,224},{192,0},{224,... | collective-permute-start | bytes 344072 | tf_op jit(solution)/shard_map/ppermute | solution.py:450
  17.7 0.0 copy-done.7
  17.7 1.0 %collective-permute-start.6 = (bf16[528,128]{1,0:T(8,128)(2,1)S(1)}, bf16[528,128]{1,0:T(8,128)(2,1)S(1)}, u32[]{:S(2)}, u32[]{:S(2)}) collective-permute-start(bf16[528,128]{1,0:T(8,128)(2,1)S(1)} %copy-done.7), channel_id=1, source_target_pairs={{0,32},{32,0},{64,96},{96,64},{128,160},{160,128},{192,224},{224,1... | collective-permute-start | bytes 405512 | tf_op jit(solution)/shard_map/ppermute | solution.py:453
  18.7 0.0 collective-permute-start.7
  18.7 1.4 %collective-permute-done.5.r4 = bf16[528,128]{1,0:T(8,128)(2,1)S(1)} collective-permute-done((bf16[528,128]{1,0:T(8,128)(2,1)S(1)}, bf16[528,128]{1,0:T(8,128)(2,1)S(1)}, u32[]{:S(2)}, u32[]{:S(2)}) %collective-permute-start.5) | collective-permute-done | bytes 135200 | tf_op jit(solution)/shard_map/ppermute | solution.py:450
  20.1 1.3 %collective-permute-start.8 = (bf16[528,128]{1,0:T(8,128)(2,1)S(1)}, bf16[528,128]{1,0:T(8,128)(2,1)S(1)}, u32[]{:S(2)}, u32[]{:S(2)}) collective-permute-start(bf16[528,128]{1,0:T(8,128)(2,1)S(1)} %collective-permute-done.5.r4), channel_id=1, source_target_pairs={{0,32},{32,0},{64,96},{96,64},{128,160},{160,128},{192,224},{224,1... | collective-permute-start | bytes 405512 | tf_op jit(solution)/shard_map/ppermute | solution.py:453
  21.5 1.1 %collective-permute-done.3.arriving = bf16[7,64,128]{2,1,0:T(8,128)(2,1)S(1)} collective-permute-done((bf16[7,64,128]{2,1,0:T(8,128)(2,1)S(1)}, bf16[7,64,128]{2,1,0:T(8,128)(2,1)S(1)}, u32[]{:S(2)}, u32[]{:S(2)}) %collective-permute-start.3) | collective-permute-done | bytes 114720 | tf_op jit(solution)/shard_map/ppermute | solution.py:450
  22.6 0.2 shard_map.144
  22.8 0.3 collective-permute-start.4
  23.1 0.0 collective-permute-done.6.x0
  23.1 0.0 collective-permute-done.7.x2
  23.1 0.0 collective-permute-done.8.x4
  23.1 0.0 copy-done.6
  23.1 0.0 copy-start.10
  23.1 4.2 %shard_map.145 = (bf16[1,256,896]{2,1,0:T(8,128)(2,1)}, f32[256,896]{1,0:T(8,128)S(1)}) custom-call(bf16[1,256,896]{2,1,0:T(8,128)(2,1)S(1)} %copy-done.6, f32[256,128]{1,0:T(8,128)S(1)} %get-tuple-element.29.cols_in, bf16[528,128]{1,0:T(8,128)(2,1)S(1)} %copy-done.7, bf16[528,128]{1,0:T(8,128)(2,1)S(1)} %collective-permute-done.1.after.r2, ...), custom_call_target="tpu_custom_call" | custom-call | flops 700000000 | tf_op jit(solution)/shard_map/pallas_call | solution.py:43
  27.3 0.6 %collective-permute-done.4.mine = bf16[7,64,128]{2,1,0:T(8,128)(2,1)S(1)} collective-permute-done((bf16[7,64,128]{2,1,0:T(8,128)(2,1)S(1)}, bf16[7,64,128]{2,1,0:T(8,128)(2,1)S(1)}, u32[]{:S(2)}, u32[]{:S(2)}) %collective-permute-start.4) | collective-permute-done | bytes 114720 | tf_op jit(solution)/shard_map/ppermute | solution.py:450
  27.9 2.0 %collective-permute-start.9 = (bf16[7,64,128]{2,1,0:T(8,128)(2,1)S(1)}, bf16[7,64,128]{2,1,0:T(8,128)(2,1)S(1)}, u32[]{:S(2)}, u32[]{:S(2)}) collective-permute-start(bf16[7,64,128]{2,1,0:T(8,128)(2,1)S(1)} %collective-permute-done.4.mine), channel_id=1, source_target_pairs={{0,32},{32,0},{64,96},{96,64},{128,160},{160,128},{192,224},{224,1... | collective-permute-start | bytes 344072 | tf_op jit(solution)/shard_map/ppermute | solution.py:453
  29.9 0.0 copy-done.10
  29.9 1.0 %collective-permute-done.9.theirs = bf16[7,64,128]{2,1,0:T(8,128)(2,1)S(1)} collective-permute-done((bf16[7,64,128]{2,1,0:T(8,128)(2,1)S(1)}, bf16[7,64,128]{2,1,0:T(8,128)(2,1)S(1)}, u32[]{:S(2)}, u32[]{:S(2)}) %collective-permute-start.9) | collective-permute-done | bytes 114720 | tf_op jit(solution)/shard_map/ppermute | solution.py:453
  30.9 1.5 %shard_map.146 = (bf16[1,256,896]{2,1,0:T(8,128)(2,1)}, f32[256,128]{1,0:T(8,128)S(1)}) custom-call(bf16[7,64,128]{2,1,0:T(8,128)(2,1)S(1)} %collective-permute-done.4.mine, bf16[7,64,128]{2,1,0:T(8,128)(2,1)S(1)} %collective-permute-done.9.theirs, bf16[14,128,128]{2,1,0:T(8,128)(2,1)S(1)} %collective-permute-done.2.other, ...), custom_call_target="tpu_custom_call" | custom-call | tf_op jit(solution)/shard_map/pallas_call | solution.py:43
  32.4 25.1 %all_to_all.11 = f32[256,1,128]{2,1,0:T(1,128)S(1)} all-to-all(f32[256,1,128]{2,1,0:T(1,128)S(1)} %bitcast.9), channel_id=1, replica_groups=mesh['ctx'=8,'head'=4,'dp'=8] {'ctx','head','dp'}, dimensions={0} | all-to-all | bytes 262144 | tf_op jit(solution)/shard_map/all_to_all | solution.py:586
  57.5 0.6 shard_map.147
  (1 shorter events, 0.0 us)
Async XLA Ops:
  0.6 5.9 %copy-start.1 = (bf16[1,256,896]{2,1,0:T(8,128)(2,1)S(1)}, bf16[1,256,896]{2,1,0:T(8,128)(2,1)}, u32[]{:S(2)}) copy-start(bf16[1,256,896]{2,1,0:T(8,128)(2,1)} %k.5) | copy-start | bytes 1376260
  0.6 5.9 %copy-start.8 = (f32[1,7,256]{2,0,1:T(1,128)S(1)}, f32[1,7,256]{2,0,1:T(1,128)}, u32[]{:S(2)}) copy-start(f32[1,7,256]{2,0,1:T(1,128)} %param.15) | copy-start | bytes 21508
  0.7 5.8 %copy-start.9 = (f32[1,7,256]{2,0,1:T(1,128)S(1)}, f32[1,7,256]{2,0,1:T(1,128)}, u32[]{:S(2)}) copy-start(f32[1,7,256]{2,0,1:T(1,128)} %param.16) | copy-start | bytes 21508
  2.3 8.9 %collective-permute-start.1 = (bf16[528,128]{1,0:T(8,128)(2,1)}, bf16[528,128]{1,0:T(8,128)(2,1)S(1)}, u32[]{:S(2)}, u32[]{:S(2)}) collective-permute-start(bf16[528,128]{1,0:T(8,128)(2,1)} %get-tuple-element.27.own), channel_id=1, source_target_pairs={{0,64},{32,96},{64,128},{96,160},{128,192},{160,224},{192,0},{224,... | collective-permute-start | bytes 405512 | tf_op jit(solution)/shard_map/ppermute | solution.py:450
  4.4 6.8 %collective-permute-start = (bf16[16,1024]{1,0:T(8,128)(2,1)}, bf16[16,1024]{1,0:T(8,128)(2,1)S(1)}, u32[]{:S(2)}, u32[]{:S(2)}) collective-permute-start(bf16[16,1024]{1,0:T(8,128)(2,1)} %get-tuple-element.23), channel_id=1, source_target_pairs={{0,32},{32,64},{64,96},{96,128},{128,160},{160,192},{192,224},{224... | collective-permute-start | bytes 98312 | tf_op jit(solution)/shard_map/ppermute | solution.py:450
  6.5 0.7 %copy-start.5 = (s32[1,256]{1,0:T(1,128)S(1)}, s32[1,256]{1,0:T(1,128)}, u32[]{:S(2)}) copy-start(s32[1,256]{1,0:T(1,128)} %ids.3) | copy-start | bytes 3076
  7.2 4.1 %copy-start = (bf16[1,256,896]{2,1,0:T(8,128)(2,1)S(1)}, bf16[1,256,896]{2,1,0:T(8,128)(2,1)}, u32[]{:S(2)}) copy-start(bf16[1,256,896]{2,1,0:T(8,128)(2,1)} %v.1) | copy-start | bytes 1376260
  7.2 4.1 %copy-start.3 = (f32[1,7,4,256]{3,2,1,0:T(4,128)S(1)}, f32[1,7,4,256]{3,2,1,0:T(4,128)}, u32[]{:S(2)}) copy-start(f32[1,7,4,256]{3,2,1,0:T(4,128)} %taps.1) | copy-start | bytes 86020
  11.3 2.7 %copy-start.2 = (bf16[1,256,896]{2,1,0:T(8,128)(2,1)S(1)}, bf16[1,256,896]{2,1,0:T(8,128)(2,1)}, u32[]{:S(2)}) copy-start(bf16[1,256,896]{2,1,0:T(8,128)(2,1)} %q.2) | copy-start | bytes 1376260
  12.9 1.1 %copy-start.4 = (f32[1,7,256]{2,0,1:T(1,128)S(1)}, f32[1,7,256]{2,0,1:T(1,128)}, u32[]{:S(2)}) copy-start(f32[1,7,256]{2,0,1:T(1,128)} %param.23) | copy-start | bytes 21508
  12.9 2.5 %collective-permute-start.2 = (bf16[14,128,128]{2,1,0:T(8,128)(2,1)S(1)}, bf16[14,128,128]{2,1,0:T(8,128)(2,1)S(1)}, u32[]{:S(2)}, u32[]{:S(2)}) collective-permute-start(bf16[14,128,128]{2,1,0:T(8,128)(2,1)S(1)} %get-tuple-element.28.own), channel_id=1, source_target_pairs={{0,32},{32,0},{64,96},{96,64},{128,160},{160,128},{192,224},{224,1... | collective-permute-start | bytes 1376264 | tf_op jit(solution)/shard_map/ppermute | solution.py:453
  13.8 6.4 %collective-permute-start.5 = (bf16[528,128]{1,0:T(8,128)(2,1)S(1)}, bf16[528,128]{1,0:T(8,128)(2,1)S(1)}, u32[]{:S(2)}, u32[]{:S(2)}) collective-permute-start(bf16[528,128]{1,0:T(8,128)(2,1)S(1)} %collective-permute-done.1.after.r2), channel_id=1, source_target_pairs={{0,64},{32,96},{64,128},{96,160},{128,192},{160,224},{192,0},{224,... | collective-permute-start | bytes 405512 | tf_op jit(solution)/shard_map/ppermute | solution.py:450
  15.4 2.3 %copy-start.7 = (bf16[528,128]{1,0:T(8,128)(2,1)S(1)}, bf16[528,128]{1,0:T(8,128)(2,1)}, u32[]{:S(2)}) copy-start(bf16[528,128]{1,0:T(8,128)(2,1)} %get-tuple-element.27.own) | copy-start | bytes 405508
  15.7 7.4 %copy-start.6 = (bf16[1,256,896]{2,1,0:T(8,128)(2,1)S(1)}, bf16[1,256,896]{2,1,0:T(8,128)(2,1)}, u32[]{:S(2)}) copy-start(bf16[1,256,896]{2,1,0:T(8,128)(2,1)} %q.3) | copy-start | bytes 1376260
  15.7 6.9 %collective-permute-start.3 = (bf16[7,64,128]{2,1,0:T(8,128)(2,1)S(1)}, bf16[7,64,128]{2,1,0:T(8,128)(2,1)S(1)}, u32[]{:S(2)}, u32[]{:S(2)}) collective-permute-start(bf16[7,64,128]{2,1,0:T(8,128)(2,1)S(1)} %get-tuple-element.34.i), channel_id=1, source_target_pairs={{0,64},{32,96},{64,128},{96,160},{128,192},{160,224},{192,0},{224,... | collective-permute-start | bytes 344072 | tf_op jit(solution)/shard_map/ppermute | solution.py:450
  17.7 5.3 %collective-permute-start.6 = (bf16[528,128]{1,0:T(8,128)(2,1)S(1)}, bf16[528,128]{1,0:T(8,128)(2,1)S(1)}, u32[]{:S(2)}, u32[]{:S(2)}) collective-permute-start(bf16[528,128]{1,0:T(8,128)(2,1)S(1)} %copy-done.7), channel_id=1, source_target_pairs={{0,32},{32,0},{64,96},{96,64},{128,160},{160,128},{192,224},{224,1... | collective-permute-start | bytes 405512 | tf_op jit(solution)/shard_map/ppermute | solution.py:453
  18.7 4.4 %collective-permute-start.7 = (bf16[528,128]{1,0:T(8,128)(2,1)S(1)}, bf16[528,128]{1,0:T(8,128)(2,1)S(1)}, u32[]{:S(2)}, u32[]{:S(2)}) collective-permute-start(bf16[528,128]{1,0:T(8,128)(2,1)S(1)} %collective-permute-done.1.after.r2), channel_id=1, source_target_pairs={{0,32},{32,0},{64,96},{96,64},{128,160},{160,128},{192,224},{224,1... | collective-permute-start | bytes 405512 | tf_op jit(solution)/shard_map/ppermute | solution.py:453
  20.1 3.0 %collective-permute-start.8 = (bf16[528,128]{1,0:T(8,128)(2,1)S(1)}, bf16[528,128]{1,0:T(8,128)(2,1)S(1)}, u32[]{:S(2)}, u32[]{:S(2)}) collective-permute-start(bf16[528,128]{1,0:T(8,128)(2,1)S(1)} %collective-permute-done.5.r4), channel_id=1, source_target_pairs={{0,32},{32,0},{64,96},{96,64},{128,160},{160,128},{192,224},{224,1... | collective-permute-start | bytes 405512 | tf_op jit(solution)/shard_map/ppermute | solution.py:453
  22.8 5.1 %collective-permute-start.4 = (bf16[7,64,128]{2,1,0:T(8,128)(2,1)S(1)}, bf16[7,64,128]{2,1,0:T(8,128)(2,1)S(1)}, u32[]{:S(2)}, u32[]{:S(2)}) collective-permute-start(bf16[7,64,128]{2,1,0:T(8,128)(2,1)S(1)} %shard_map.144), channel_id=1, source_target_pairs={{0,64},{32,96},{64,128},{96,160},{128,192},{160,224},{192,0},{224,... | collective-permute-start | bytes 344072 | tf_op jit(solution)/shard_map/ppermute | solution.py:450
  23.1 6.8 %copy-start.10 = (f32[896]{0:T(1024)S(1)}, f32[896]{0:T(1024)}, u32[]{:S(2)}) copy-start(f32[896]{0:T(1024)} %param.18) | copy-start | bytes 10756
  27.9 3.0 %collective-permute-start.9 = (bf16[7,64,128]{2,1,0:T(8,128)(2,1)S(1)}, bf16[7,64,128]{2,1,0:T(8,128)(2,1)S(1)}, u32[]{:S(2)}, u32[]{:S(2)}) collective-permute-start(bf16[7,64,128]{2,1,0:T(8,128)(2,1)S(1)} %collective-permute-done.4.mine), channel_id=1, source_target_pairs={{0,32},{32,0},{64,96},{96,64},{128,160},{160,128},{192,224},{224,1... | collective-permute-start | bytes 344072 | tf_op jit(solution)/shard_map/ppermute | solution.py:453

commit v6 on v5

--- a/solution.py
+++ b/solution.py
@@ -82,6 +82,10 @@
     ).astype(BF16)
     for move in moves[1:]:
         move.wait()
+
+
+def is_odd():
+    return lax.rem(lax.axis_index("ctx"), 2) == 1
 
 
 def eye(n):
@@ -269,7 +273,7 @@
         mi_out[heads + h] = ends[h].astype(BF16)
 
 
-def queries_body(q, k, rim, rows, cols_in, uk, uv, lw, local_out, reader_out, lw_out, lw_s):
+def queries_body(q, k, rim, rows, cols_in, uk, uv, other, lw, local_out, reader_out, lw_out, lw_s):
     tokens = q.shape[1]
     features = q.shape[2]
     heads = uk.shape[0]
@@ -295,10 +299,17 @@
         between = jnp.where(visible, jnp.exp(cols[:, h : h + 1] - rows[h : h + 1]), 0.0)
         readings.append((between * rows[8 + h : 9 + h] * (norms[h] * qks[h])).astype(BF16))
     both = [nt(readings[h], jnp.concatenate([uv[h], uk[h]], axis=0)) for h in every]
-    for h in every:
-        local_out[h] = both[h][:, 0:HEAD]
+    readers = []
+    for h in every:
         reader = (cols[:, 16 + h : 17 + h] * norms[h]) * qs[h].astype(F32) - both[h][:, HEAD:]
-        reader_out[h] = (joined * reader).astype(BF16)
+        readers.append((joined * reader).astype(BF16))
+    odd = is_odd()
+    steps = [
+        nt(readers[h], jnp.concatenate([other[h], other[heads + h]], axis=0)) for h in every
+    ]
+    for h in every:
+        local_out[h] = both[h][:, 0:HEAD] + jnp.where(odd, steps[h][:, HEAD:], 0.0)
+        reader_out[h] = jnp.where(odd, steps[h][:, 0:HEAD].astype(BF16), readers[h])
 
 
 def teacher_body(first_head, last_head, q, cols_in, own, r2, r4, x0, x2, x4, *refs):
@@ -363,11 +374,7 @@
         out[0, rows, head_lanes(h)] = o.astype(BF16)
 
 
-def is_odd():
-    return lax.rem(lax.axis_index("ctx"), 2) == 1
-
-
-def chip_body(own, other, after, m_out, i_out):
+def chip_body(own, other, m_out, i_out):
     heads, rows, _ = i_out.shape
     every = range(heads)
     odd = is_odd()
@@ -382,14 +389,14 @@
         i_out[h] = (ends[h] + later_i.astype(F32)).astype(BF16)
 
 
-def join_body(m, i, arriving, out):
+def join_body(m, i, arriving, after, out):
     every = range(m.shape[0])
     ends = [nn(arriving[h], m[h]) for h in every]
     for h in every:
         out[h] = (ends[h] + i[h].astype(F32)).astype(BF16)
 
 
-def finish_body(mine, theirs, other, local, reader, gain, teachers, lw, out, sums, out_s, student_s, sems):
+def finish_body(mine, theirs, local, reader, gain, teachers, lw, out, sums, out_s, student_s, sems):
     heads = mine.shape[0]
     every = range(heads)
     odd = is_odd()
@@ -397,10 +404,6 @@
     for h in every:
         a, b = mine[h], theirs[h]
         states.append(jnp.concatenate([jnp.where(odd, b, a), jnp.where(odd, a, b)], axis=0))
-    steps = [nn(states[h], other[h]) for h in every]
-    for h in every:
-        step = (steps[h] + other[heads + h].astype(F32)).astype(BF16)
-        states[h] = jnp.where(odd, step, states[h])
     half = lw.shape[0] // 2
     moves = []
     for r in range(2):
@@ -524,6 +527,7 @@
         cols,
         uk,
         uv,
+        mi_other,
         by_head(loss_weight),
         scratch=[((128, tokens), F32)],
         flops=2 * 10**8,
@@ -533,7 +537,6 @@
         [((heads, HEAD, HEAD), BF16), ((heads, HEAD // 2, HEAD), BF16)],
         mi,
         mi_other,
-        lw,
     )
     behind = rotated(i_chip, 2)
     x4 = swapped(r4)
@@ -562,7 +565,7 @@
         )
 
     (joined,) = call(
-        join_body, [((heads, HEAD // 2, HEAD), BF16)], m_chip, i_chip, behind
+        join_body, [((heads, HEAD // 2, HEAD), BF16)], m_chip, i_chip, behind, lw
     )
     mine = rotated(joined, 2)
     teacher_out, teacher = attend(0, heads)
@@ -573,7 +576,6 @@
         [((1, tokens, features), BF16), ((everyone, 128), F32)],
         mine,
         theirs,
-        mi_other,
         local,
         reader,
         out_gain.reshape(1, features),

time: 58.3 us -> 58.2 us (level)
  starting transfers between devices: 11.9 us -> 9.89 us
  waiting for transfers between devices: 4.15 us -> 5.8 us
    ppermute x5, starting transfers between devices: 6.68 us -> 5.46 us  [rotated(): lax.ppermute(block, 'ctx', [(i, (i + distance) % shards) for i in range(s...]
    ppermute x5, waiting for transfers between devices: 0.97 us -> 2.18 us  [swapped(): return lax.ppermute(block, 'ctx', [(i, i ^ 1) for i in range(shards)])]
    ppermute x5, starting transfers between devices: 5.17 us -> 4.42 us  [swapped(): return lax.ppermute(block, 'ctx', [(i, i ^ 1) for i in range(shards)])]
  transfers between devices with their start and end apart: 10 -> 10, of which waited for: 4 -> 4; matrix products, arithmetic and copies ran while one was open for 0% -> 0% of each run, Pallas kernels for 17% -> 18%
where the time goes in v6:
time: 58.2 us; the launch traced here: 58 us
  blocking collectives  24.8 us (43%)
  Pallas kernels  15.5 us (27%)
  starting transfers between devices  9.89 us (17%)
  waiting for transfers between devices  5.8 us (10%)
  local copies, waits for them, and re-layouts  1.2 us (2%)
  between operations  0.8 us (1%)
    all_to_all x1, blocking collectives, on_device(): gathered = lax.all_to_all(sums, ('ctx', 'head', 'dp'), 0, 0, tiled=True)  24.8 us
    pallas_call x9, Pallas kernels, call(): pl.pallas_call(body, out_shape=[jax.ShapeDtypeStruct(s, d) for s, d in ou...  15.5 us
    ppermute x5, starting transfers between devices, rotated(): lax.ppermute(block, 'ctx', [(i, (i + distance) % shards) for i in range(s...  5.46 us
    ppermute x5, starting transfers between devices, swapped(): return lax.ppermute(block, 'ctx', [(i, i ^ 1) for i in range(shards)])  4.42 us
    ppermute x5, waiting for transfers between devices, rotated(): lax.ppermute(block, 'ctx', [(i, (i + distance) % shards) for i in range(s...  3.62 us
    ppermute x5, waiting for transfers between devices, swapped(): return lax.ppermute(block, 'ctx', [(i, i ^ 1) for i in range(shards)])  2.18 us
    unnamed x22, local copies, waits for them, and re-layouts  1.2 us
  transfers between devices with their start and end apart: 10, of which 4 were waited for; matrix products, arithmetic and copies ran while one was open for 0% of the time, Pallas kernels for 18%

profile of v6, /device:TPU:1, one launch (start us, length us, event | category | flops | bytes accessed | tf_op | source)
XLA Modules:
  0.0 58.0 jit_solution(10180676368321587577)
XLA Ops:
  0.6 0.0 copy-start.1
  0.6 0.0 copy-start.8
  0.7 0.0 copy-start.9
  0.7 1.7 %shard_map.139 = (bf16[528,128]{1,0:T(8,128)(2,1)}, bf16[16,1024]{1,0:T(8,128)(2,1)}) custom-call(bf16[1,256,128]{2,1,0:T(8,128)(2,1)} %tk.1, bf16[1,256,128]{2,1,0:T(8,128)(2,1)} %tv.1, bf16[1,256,896]{2,1,0:T(8,128)(2,1)} %v.1, s32[1,256]{1,0:T(1,128)} %ids.3), custom_call_target="tpu_custom_call" | custom-call | tf_op jit(solution)/shard_map/pallas_call | solution.py:43
  2.3 2.1 %collective-permute-start.1 = (bf16[528,128]{1,0:T(8,128)(2,1)}, bf16[528,128]{1,0:T(8,128)(2,1)S(1)}, u32[]{:S(2)}, u32[]{:S(2)}) collective-permute-start(bf16[528,128]{1,0:T(8,128)(2,1)} %get-tuple-element.27.own), channel_id=1, source_target_pairs={{0,64},{32,96},{64,128},{96,160},{128,192},{160,224},{192,0},{224,... | collective-permute-start | bytes 405512 | tf_op jit(solution)/shard_map/ppermute | solution.py:453
  4.4 2.1 %collective-permute-start = (bf16[16,1024]{1,0:T(8,128)(2,1)}, bf16[16,1024]{1,0:T(8,128)(2,1)S(1)}, u32[]{:S(2)}, u32[]{:S(2)}) collective-permute-start(bf16[16,1024]{1,0:T(8,128)(2,1)} %get-tuple-element.23), channel_id=1, source_target_pairs={{0,32},{32,64},{64,96},{96,128},{128,160},{160,192},{192,224},{224... | collective-permute-start | bytes 98312 | tf_op jit(solution)/shard_map/ppermute | solution.py:453
  6.5 0.0 copy-start.5
  6.5 0.0 copy-done.1
  6.5 0.0 copy-done.8
  6.5 0.0 copy-done.9
  6.5 0.7 %copy-done.5 = s32[1,256]{1,0:T(1,128)S(1)} copy-done((s32[1,256]{1,0:T(1,128)S(1)}, s32[1,256]{1,0:T(1,128)}, u32[]{:S(2)}) %copy-start.5) | copy-done | bytes 1048
  7.2 0.0 copy-start
  7.2 0.0 copy-start.3
  7.2 4.1 %shard_map.140 = (bf16[7,256,256]{2,1,0:T(8,128)(2,1)S(1)}, bf16[7,128,256]{2,1,0:T(8,128)(2,1)S(1)}, f32[7,128,128]{2,1,0:T(8,128)S(1)}, f32[32,256]{1,0:T(8,128)S(1)}, f32[256,128]{1,0:T(8,128)S(1)}) custom-call(bf16[1,256,896]{2,1,0:T(8,128)(2,1)S(1)} %copy-done.1, f32[7,1,256]{2,1,0:T(1,128)S(1)} %bitcast.11, f32[7,1,256]{2,1,0:T(1,128)S(1)} %bitcast.12, ...), custom_call_target="tpu_custom_call" | custom-call | flops 500000000 | tf_op jit(solution)/shard_map/pallas_call | solution.py:43
  11.3 0.0 collective-permute-done.rim
  11.3 0.0 collective-permute-done.1.after.r2
  11.3 0.0 copy-done
  11.3 0.0 copy-done.3
  11.3 1.6 %shard_map.141 = (bf16[14,128,128]{2,1,0:T(8,128)(2,1)S(1)}, bf16[7,128,256]{2,1,0:T(8,128)(2,1)S(1)}) custom-call(bf16[1,256,896]{2,1,0:T(8,128)(2,1)S(1)} %copy-done, bf16[16,1024]{1,0:T(8,128)(2,1)S(1)} %collective-permute-done.rim, f32[1,7,4,256]{3,2,1,0:T(4,128)S(1)} %copy-done.3, f32[32,256]{1,0:T(8,128)S(1)} %get-tuple-element.24.rows, ...), custom_call_target="tpu_custom_call" | custom-call | flops 200000000 | tf_op jit(solution)/shard_map/pallas_call | solution.py:43
  12.9 0.0 copy-start.7
  12.9 0.0 copy-start.2
  12.9 0.9 %collective-permute-start.2 = (bf16[14,128,128]{2,1,0:T(8,128)(2,1)S(1)}, bf16[14,128,128]{2,1,0:T(8,128)(2,1)S(1)}, u32[]{:S(2)}, u32[]{:S(2)}) collective-permute-start(bf16[14,128,128]{2,1,0:T(8,128)(2,1)S(1)} %get-tuple-element.28.own), channel_id=1, source_target_pairs={{0,32},{32,0},{64,96},{96,64},{128,160},{160,128},{192,224},{224,1... | collective-permute-start | bytes 1376264 | tf_op jit(solution)/shard_map/ppermute | solution.py:456
  13.8 0.2 collective-permute-start.5
  14.0 1.2 %collective-permute-done.2.other = bf16[14,128,128]{2,1,0:T(8,128)(2,1)S(1)} collective-permute-done((bf16[14,128,128]{2,1,0:T(8,128)(2,1)S(1)}, bf16[14,128,128]{2,1,0:T(8,128)(2,1)S(1)}, u32[]{:S(2)}, u32[]{:S(2)}) %collective-permute-start.2) | collective-permute-done | bytes 458784 | tf_op jit(solution)/shard_map/ppermute | solution.py:456
  15.2 0.3 shard_map.142
  15.5 0.0 copy-start.4
  15.5 0.8 %collective-permute-start.3 = (bf16[7,64,128]{2,1,0:T(8,128)(2,1)S(1)}, bf16[7,64,128]{2,1,0:T(8,128)(2,1)S(1)}, u32[]{:S(2)}, u32[]{:S(2)}) collective-permute-start(bf16[7,64,128]{2,1,0:T(8,128)(2,1)S(1)} %get-tuple-element.30.i), channel_id=1, source_target_pairs={{0,64},{32,96},{64,128},{96,160},{128,192},{160,224},{192,0},{224,... | collective-permute-start | bytes 344072 | tf_op jit(solution)/shard_map/ppermute | solution.py:453
  16.3 0.0 copy-done.7
  16.3 1.0 %collective-permute-start.6 = (bf16[528,128]{1,0:T(8,128)(2,1)S(1)}, bf16[528,128]{1,0:T(8,128)(2,1)S(1)}, u32[]{:S(2)}, u32[]{:S(2)}) collective-permute-start(bf16[528,128]{1,0:T(8,128)(2,1)S(1)} %copy-done.7), channel_id=1, source_target_pairs={{0,32},{32,0},{64,96},{96,64},{128,160},{160,128},{192,224},{224,1... | collective-permute-start | bytes 405512 | tf_op jit(solution)/shard_map/ppermute | solution.py:456
  17.3 0.0 collective-permute-start.7
  17.3 2.8 %collective-permute-done.5.r4 = bf16[528,128]{1,0:T(8,128)(2,1)S(1)} collective-permute-done((bf16[528,128]{1,0:T(8,128)(2,1)S(1)}, bf16[528,128]{1,0:T(8,128)(2,1)S(1)}, u32[]{:S(2)}, u32[]{:S(2)}) %collective-permute-start.5) | collective-permute-done | bytes 135200 | tf_op jit(solution)/shard_map/ppermute | solution.py:453
  20.1 1.3 %collective-permute-start.8 = (bf16[528,128]{1,0:T(8,128)(2,1)S(1)}, bf16[528,128]{1,0:T(8,128)(2,1)S(1)}, u32[]{:S(2)}, u32[]{:S(2)}) collective-permute-start(bf16[528,128]{1,0:T(8,128)(2,1)S(1)} %collective-permute-done.5.r4), channel_id=1, source_target_pairs={{0,32},{32,0},{64,96},{96,64},{128,160},{160,128},{192,224},{224,1... | collective-permute-start | bytes 405512 | tf_op jit(solution)/shard_map/ppermute | solution.py:456
  21.5 0.0 copy-done.2
  21.5 0.0 copy-done.4
  21.5 1.5 %shard_map.143 = (f32[7,256,128]{2,1,0:T(8,128)S(1)}, bf16[7,256,128]{2,1,0:T(8,128)(2,1)S(1)}, f32[256,128]{1,0:T(8,128)S(1)}) custom-call(bf16[1,256,896]{2,1,0:T(8,128)(2,1)S(1)} %copy-done.2, bf16[1,256,896]{2,1,0:T(8,128)(2,1)S(1)} %copy-done.1, bf16[16,1024]{1,0:T(8,128)(2,1)S(1)} %collective-permute-done.rim, f32[32,256]{1,0:T(8,128)S(1)} %get-tuple-element.24.rows, ...), custom_call_target="tpu_custom_call" | custom-call | flops 200000000 | tf_op jit(solution)/shard_map/pallas_call | solution.py:43
  23.0 0.0 copy-start.6
  23.0 0.0 collective-permute-done.3.arriving
  23.1 0.2 shard_map.144
  23.3 0.3 collective-permute-start.4
  23.5 0.0 collective-permute-done.6.x0
  23.5 0.0 collective-permute-done.7.x2
  23.6 0.0 collective-permute-done.8.x4
  23.6 0.5 copy-done.6
  24.1 0.0 copy-start.10
  24.1 4.2 %shard_map.145 = (bf16[1,256,896]{2,1,0:T(8,128)(2,1)}, f32[256,896]{1,0:T(8,128)S(1)}) custom-call(bf16[1,256,896]{2,1,0:T(8,128)(2,1)S(1)} %copy-done.6, f32[256,128]{1,0:T(8,128)S(1)} %get-tuple-element.31.cols_in, bf16[528,128]{1,0:T(8,128)(2,1)S(1)} %copy-done.7, bf16[528,128]{1,0:T(8,128)(2,1)S(1)} %collective-permute-done.1.after.r2, ...), custom_call_target="tpu_custom_call" | custom-call | flops 700000000 | tf_op jit(solution)/shard_map/pallas_call | solution.py:43
  28.3 0.8 %collective-permute-done.4.mine = bf16[7,64,128]{2,1,0:T(8,128)(2,1)S(1)} collective-permute-done((bf16[7,64,128]{2,1,0:T(8,128)(2,1)S(1)}, bf16[7,64,128]{2,1,0:T(8,128)(2,1)S(1)}, u32[]{:S(2)}, u32[]{:S(2)}) %collective-permute-start.4) | collective-permute-done | bytes 114720 | tf_op jit(solution)/shard_map/ppermute | solution.py:453
  29.1 1.2 %collective-permute-start.9 = (bf16[7,64,128]{2,1,0:T(8,128)(2,1)S(1)}, bf16[7,64,128]{2,1,0:T(8,128)(2,1)S(1)}, u32[]{:S(2)}, u32[]{:S(2)}) collective-permute-start(bf16[7,64,128]{2,1,0:T(8,128)(2,1)S(1)} %collective-permute-done.4.mine), channel_id=1, source_target_pairs={{0,32},{32,0},{64,96},{96,64},{128,160},{160,128},{192,224},{224,1... | collective-permute-start | bytes 344072 | tf_op jit(solution)/shard_map/ppermute | solution.py:456
  30.3 0.0 copy-done.10
  30.3 1.0 %collective-permute-done.9.theirs = bf16[7,64,128]{2,1,0:T(8,128)(2,1)S(1)} collective-permute-done((bf16[7,64,128]{2,1,0:T(8,128)(2,1)S(1)}, bf16[7,64,128]{2,1,0:T(8,128)(2,1)S(1)}, u32[]{:S(2)}, u32[]{:S(2)}) %collective-permute-start.9) | collective-permute-done | bytes 114720 | tf_op jit(solution)/shard_map/ppermute | solution.py:456
  31.3 1.4 %shard_map.146 = (bf16[1,256,896]{2,1,0:T(8,128)(2,1)}, f32[256,128]{1,0:T(8,128)S(1)}) custom-call(bf16[7,64,128]{2,1,0:T(8,128)(2,1)S(1)} %collective-permute-done.4.mine, bf16[7,64,128]{2,1,0:T(8,128)(2,1)S(1)} %collective-permute-done.9.theirs, f32[7,256,128]{2,1,0:T(8,128)S(1)} %get-tuple-element.37.local, ...), custom_call_target="tpu_custom_call" | custom-call | tf_op jit(solution)/shard_map/pallas_call | solution.py:43
  32.7 24.8 %all_to_all.11 = f32[256,1,128]{2,1,0:T(1,128)S(1)} all-to-all(f32[256,1,128]{2,1,0:T(1,128)S(1)} %bitcast.9), channel_id=1, replica_groups=mesh['ctx'=8,'head'=4,'dp'=8] {'ctx','head','dp'}, dimensions={0} | all-to-all | bytes 262144 | tf_op jit(solution)/shard_map/all_to_all | solution.py:588
  57.5 0.6 shard_map.147
  (1 shorter events, 0.0 us)
Async XLA Ops:
  0.6 5.9 %copy-start.1 = (bf16[1,256,896]{2,1,0:T(8,128)(2,1)S(1)}, bf16[1,256,896]{2,1,0:T(8,128)(2,1)}, u32[]{:S(2)}) copy-start(bf16[1,256,896]{2,1,0:T(8,128)(2,1)} %k.5) | copy-start | bytes 1376260
  0.6 5.9 %copy-start.8 = (f32[1,7,256]{2,0,1:T(1,128)S(1)}, f32[1,7,256]{2,0,1:T(1,128)}, u32[]{:S(2)}) copy-start(f32[1,7,256]{2,0,1:T(1,128)} %param.15) | copy-start | bytes 21508
  0.7 5.8 %copy-start.9 = (f32[1,7,256]{2,0,1:T(1,128)S(1)}, f32[1,7,256]{2,0,1:T(1,128)}, u32[]{:S(2)}) copy-start(f32[1,7,256]{2,0,1:T(1,128)} %param.16) | copy-start | bytes 21508
  2.3 8.9 %collective-permute-start.1 = (bf16[528,128]{1,0:T(8,128)(2,1)}, bf16[528,128]{1,0:T(8,128)(2,1)S(1)}, u32[]{:S(2)}, u32[]{:S(2)}) collective-permute-start(bf16[528,128]{1,0:T(8,128)(2,1)} %get-tuple-element.27.own), channel_id=1, source_target_pairs={{0,64},{32,96},{64,128},{96,160},{128,192},{160,224},{192,0},{224,... | collective-permute-start | bytes 405512 | tf_op jit(solution)/shard_map/ppermute | solution.py:453
  4.4 6.8 %collective-permute-start = (bf16[16,1024]{1,0:T(8,128)(2,1)}, bf16[16,1024]{1,0:T(8,128)(2,1)S(1)}, u32[]{:S(2)}, u32[]{:S(2)}) collective-permute-start(bf16[16,1024]{1,0:T(8,128)(2,1)} %get-tuple-element.23), channel_id=1, source_target_pairs={{0,32},{32,64},{64,96},{96,128},{128,160},{160,192},{192,224},{224... | collective-permute-start | bytes 98312 | tf_op jit(solution)/shard_map/ppermute | solution.py:453
  6.5 0.7 %copy-start.5 = (s32[1,256]{1,0:T(1,128)S(1)}, s32[1,256]{1,0:T(1,128)}, u32[]{:S(2)}) copy-start(s32[1,256]{1,0:T(1,128)} %ids.3) | copy-start | bytes 3076
  7.2 4.1 %copy-start = (bf16[1,256,896]{2,1,0:T(8,128)(2,1)S(1)}, bf16[1,256,896]{2,1,0:T(8,128)(2,1)}, u32[]{:S(2)}) copy-start(bf16[1,256,896]{2,1,0:T(8,128)(2,1)} %v.1) | copy-start | bytes 1376260
  7.2 4.1 %copy-start.3 = (f32[1,7,4,256]{3,2,1,0:T(4,128)S(1)}, f32[1,7,4,256]{3,2,1,0:T(4,128)}, u32[]{:S(2)}) copy-start(f32[1,7,4,256]{3,2,1,0:T(4,128)} %taps.1) | copy-start | bytes 86020
  12.9 3.4 %copy-start.7 = (bf16[528,128]{1,0:T(8,128)(2,1)S(1)}, bf16[528,128]{1,0:T(8,128)(2,1)}, u32[]{:S(2)}) copy-start(bf16[528,128]{1,0:T(8,128)(2,1)} %get-tuple-element.27.own) | copy-start | bytes 405508
  12.9 8.6 %copy-start.2 = (bf16[1,256,896]{2,1,0:T(8,128)(2,1)S(1)}, bf16[1,256,896]{2,1,0:T(8,128)(2,1)}, u32[]{:S(2)}) copy-start(bf16[1,256,896]{2,1,0:T(8,128)(2,1)} %q.2) | copy-start | bytes 1376260
  12.9 2.3 %collective-permute-start.2 = (bf16[14,128,128]{2,1,0:T(8,128)(2,1)S(1)}, bf16[14,128,128]{2,1,0:T(8,128)(2,1)S(1)}, u32[]{:S(2)}, u32[]{:S(2)}) collective-permute-start(bf16[14,128,128]{2,1,0:T(8,128)(2,1)S(1)} %get-tuple-element.28.own), channel_id=1, source_target_pairs={{0,32},{32,0},{64,96},{96,64},{128,160},{160,128},{192,224},{224,1... | collective-permute-start | bytes 1376264 | tf_op jit(solution)/shard_map/ppermute | solution.py:456
  13.8 6.4 %collective-permute-start.5 = (bf16[528,128]{1,0:T(8,128)(2,1)S(1)}, bf16[528,128]{1,0:T(8,128)(2,1)S(1)}, u32[]{:S(2)}, u32[]{:S(2)}) collective-permute-start(bf16[528,128]{1,0:T(8,128)(2,1)S(1)} %collective-permute-done.1.after.r2), channel_id=1, source_target_pairs={{0,64},{32,96},{64,128},{96,160},{128,192},{160,224},{192,0},{224,... | collective-permute-start | bytes 405512 | tf_op jit(solution)/shard_map/ppermute | solution.py:453
  15.5 6.0 %copy-start.4 = (f32[1,7,256]{2,0,1:T(1,128)S(1)}, f32[1,7,256]{2,0,1:T(1,128)}, u32[]{:S(2)}) copy-start(f32[1,7,256]{2,0,1:T(1,128)} %param.23) | copy-start | bytes 21508
  15.5 7.5 %collective-permute-start.3 = (bf16[7,64,128]{2,1,0:T(8,128)(2,1)S(1)}, bf16[7,64,128]{2,1,0:T(8,128)(2,1)S(1)}, u32[]{:S(2)}, u32[]{:S(2)}) collective-permute-start(bf16[7,64,128]{2,1,0:T(8,128)(2,1)S(1)} %get-tuple-element.30.i), channel_id=1, source_target_pairs={{0,64},{32,96},{64,128},{96,160},{128,192},{160,224},{192,0},{224,... | collective-permute-start | bytes 344072 | tf_op jit(solution)/shard_map/ppermute | solution.py:453
  16.3 7.2 %collective-permute-start.6 = (bf16[528,128]{1,0:T(8,128)(2,1)S(1)}, bf16[528,128]{1,0:T(8,128)(2,1)S(1)}, u32[]{:S(2)}, u32[]{:S(2)}) collective-permute-start(bf16[528,128]{1,0:T(8,128)(2,1)S(1)} %copy-done.7), channel_id=1, source_target_pairs={{0,32},{32,0},{64,96},{96,64},{128,160},{160,128},{192,224},{224,1... | collective-permute-start | bytes 405512 | tf_op jit(solution)/shard_map/ppermute | solution.py:456
  17.3 6.2 %collective-permute-start.7 = (bf16[528,128]{1,0:T(8,128)(2,1)S(1)}, bf16[528,128]{1,0:T(8,128)(2,1)S(1)}, u32[]{:S(2)}, u32[]{:S(2)}) collective-permute-start(bf16[528,128]{1,0:T(8,128)(2,1)S(1)} %collective-permute-done.1.after.r2), channel_id=1, source_target_pairs={{0,32},{32,0},{64,96},{96,64},{128,160},{160,128},{192,224},{224,1... | collective-permute-start | bytes 405512 | tf_op jit(solution)/shard_map/ppermute | solution.py:456
  20.1 3.4 %collective-permute-start.8 = (bf16[528,128]{1,0:T(8,128)(2,1)S(1)}, bf16[528,128]{1,0:T(8,128)(2,1)S(1)}, u32[]{:S(2)}, u32[]{:S(2)}) collective-permute-start(bf16[528,128]{1,0:T(8,128)(2,1)S(1)} %collective-permute-done.5.r4), channel_id=1, source_target_pairs={{0,32},{32,0},{64,96},{96,64},{128,160},{160,128},{192,224},{224,1... | collective-permute-start | bytes 405512 | tf_op jit(solution)/shard_map/ppermute | solution.py:456
  23.0 1.0 %copy-start.6 = (bf16[1,256,896]{2,1,0:T(8,128)(2,1)S(1)}, bf16[1,256,896]{2,1,0:T(8,128)(2,1)}, u32[]{:S(2)}) copy-start(bf16[1,256,896]{2,1,0:T(8,128)(2,1)} %q.3) | copy-start | bytes 1376260
  23.3 5.8 %collective-permute-start.4 = (bf16[7,64,128]{2,1,0:T(8,128)(2,1)S(1)}, bf16[7,64,128]{2,1,0:T(8,128)(2,1)S(1)}, u32[]{:S(2)}, u32[]{:S(2)}) collective-permute-start(bf16[7,64,128]{2,1,0:T(8,128)(2,1)S(1)} %shard_map.144), channel_id=1, source_target_pairs={{0,64},{32,96},{64,128},{96,160},{128,192},{160,224},{192,0},{224,... | collective-permute-start | bytes 344072 | tf_op jit(solution)/shard_map/ppermute | solution.py:453
  24.1 6.2 %copy-start.10 = (f32[896]{0:T(1024)S(1)}, f32[896]{0:T(1024)}, u32[]{:S(2)}) copy-start(f32[896]{0:T(1024)} %param.18) | copy-start | bytes 10756
  29.1 2.2 %collective-permute-start.9 = (bf16[7,64,128]{2,1,0:T(8,128)(2,1)S(1)}, bf16[7,64,128]{2,1,0:T(8,128)(2,1)S(1)}, u32[]{:S(2)}, u32[]{:S(2)}) collective-permute-start(bf16[7,64,128]{2,1,0:T(8,128)(2,1)S(1)} %collective-permute-done.4.mine), channel_id=1, source_target_pairs={{0,32},{32,0},{64,96},{96,64},{128,160},{160,128},{192,224},{224,1... | collective-permute-start | bytes 344072 | tf_op jit(solution)/shard_map/ppermute | solution.py:456
